TPU v7x, 256 devices: a whole 4x4x8 slice. The times are simulated.
256 devices in a mesh: island: 32 (over z, y_hi, core), tensor: 8 (over x, y_lo).
Axes of the slice: x: 4, y: 4 (y_hi: 2, y_lo: 2; y = y_hi * 2 + y_lo), z: 8, core: 2. Of those that a mesh axis runs over, the one named last changes fastest.
Arguments:
- hidden_rows: bfloat16 [32, 1024, 4096], P('island', 'tensor'), may hold values from -6 to 6
- queries: bfloat16 [32, 1024, 4096], P('island', None, 'tensor')
- key_states: bfloat16 [32, 1024, 1024], P('island', None, 'tensor')
- out_grads: bfloat16 [32, 1024, 4096], P('island', None, 'tensor'), may hold values from -6 to 6
- doc_ids: int32 [32, 1024], P('island'), may hold values from 0 to 3, never falling along the last dimension, each value on 1 to 512 neighbouring positions
- value_weight: bfloat16 [4096, 1024], P(None, 'tensor'), may hold values from -0.09375 to 0.09375
- momentum: float32 [4096, 1024], P(None, 'tensor'), may hold values from -0.015625 to 0.015625
- keep_index: int32 [4096, 8, 8], P(None, 'tensor'), may hold values from 0 to 127, all different within a row
Outputs:
- new_weight: bfloat16 [4096, 1024], P(None, 'tensor')
- new_momentum: float32 [4096, 1024], P(None, 'tensor')
Inputs may be any that keep to these rules, and one draw needn't show every extreme that they name: `keep_index`: the 8 indices of one span are distinct. `doc_ids`: ids never fall along a sequence.
All inputs are finite; a program needn't handle non-finite values.
Results may differ from a plain program's by a relative error of at most 0.0041.
Values may be sent and summed in bfloat16 or wider, within the bound.
No kernel may reach another device: no remote copies, remote signals or barrier semaphores. Data moves between devices by JAX's collectives and lax.ppermute only.
A program may use at most 128 MiB of HBM per device.

v0:
```python
import math

import jax
import jax.numpy as jnp
from jax import lax
from jax.sharding import PartitionSpec as P

HEAD_DIM = 128


inner_rate = 0.01
outer_rate = 0.7
momentum_beta = 0.9
masked_score = -1e30


def dct_table(length):
    frequency = jnp.arange(length, dtype=jnp.float32)[:, None]
    sample = jnp.arange(length, dtype=jnp.float32)[None, :]
    basis = jnp.cos(math.pi * (sample + 0.5) * frequency / length)
    return basis * jnp.where(frequency == 0.0, math.sqrt(1.0 / length), math.sqrt(2.0 / length))


def value_grads(queries, key_states, out_grads, doc_ids):
    length = key_states.shape[0]
    heads_kv = key_states.shape[1] // HEAD_DIM
    group = queries.shape[1] // key_states.shape[1]
    block = min(length, 512)
    count = length // block
    keys_split = key_states.reshape(length, heads_kv, HEAD_DIM)
    query_blocks = queries.reshape(count, block, heads_kv, group, HEAD_DIM)
    grad_blocks = out_grads.reshape(count, block, heads_kv, group, HEAD_DIM)
    doc_blocks = doc_ids.reshape(count, block)
    offsets = jnp.arange(count, dtype=jnp.int32) * block
    columns = jnp.arange(length, dtype=jnp.int32)
    scale = HEAD_DIM ** (-0.5)

    def step(totals, inputs):
        query_block, grad_block, doc_block, offset = inputs
        scores = (
            jnp.einsum(
                "bhgd,shd->hgbs", query_block, keys_split, preferred_element_type=jnp.float32
            )
            * scale
        )
        rows_here = offset + jnp.arange(block, dtype=jnp.int32)
        allowed = (doc_block[:, None] == doc_ids[None, :]) & (
            columns[None, :] <= rows_here[:, None]
        )
        scores = jnp.where(allowed[None, None], scores, masked_score)
        peak = jnp.max(scores, axis=3, keepdims=True)
        weights = jnp.exp(scores - peak)
        probs = (weights / jnp.sum(weights, axis=3, keepdims=True)).astype(jnp.bfloat16)
        totals = totals + jnp.einsum(
            "hgbs,bhgd->shd", probs, grad_block, preferred_element_type=jnp.float32
        )
        return (totals, None)

    start = jnp.zeros((length, heads_kv, HEAD_DIM), jnp.float32)
    totals, unused = lax.scan(step, start, (query_blocks, grad_blocks, doc_blocks, offsets))
    return totals.reshape(length, heads_kv * HEAD_DIM).astype(jnp.bfloat16)


def encode(pseudo, keep_index, table):
    length = table.shape[0]
    spans = pseudo.reshape(pseudo.shape[0], keep_index.shape[1], length)
    coeffs = jnp.einsum("rhn,kn->rhk", spans, table, precision=lax.Precision.HIGHEST)
    picker = keep_index[:, :, :, None] == jnp.arange(length, dtype=jnp.int32)[None, None, None, :]
    return jnp.sum(jnp.where(picker, coeffs[:, :, None, :], 0.0), axis=3)


def decode(kept, keep_index, table):
    length = table.shape[0]
    picker = keep_index[:, :, :, None] == jnp.arange(length, dtype=jnp.int32)[None, None, None, :]
    dense = jnp.sum(jnp.where(picker, kept[:, :, :, None], 0.0), axis=2)
    spans = jnp.einsum("rhk,kn->rhn", dense, table, precision=lax.Precision.HIGHEST)
    return spans.reshape(kept.shape[0], keep_index.shape[1] * length)


def island_mean(kept):
    summed = lax.psum(kept, "island")
    return summed / float(lax.axis_size("island"))


def outer_delta(weight_grad, keep_index, table):
    kept = encode(inner_rate * weight_grad, keep_index, table)
    return decode(island_mean(kept), keep_index, table)


def local(hidden_rows, queries, key_states, out_grads, doc_ids, value_weight, momentum, keep_index):
    table = dct_table(HEAD_DIM)
    layer_rows = hidden_rows[0]
    values = value_grads(queries[0], key_states[0], out_grads[0], doc_ids[0])
    contract = (((0,), (0,)), ((), ()))
    weight_grad = lax.dot_general(
        lax.all_gather(layer_rows, "tensor", axis=0, tiled=True),
        values,
        contract,
        preferred_element_type=jnp.float32,
    )
    delta = outer_delta(weight_grad, keep_index, table)
    new_momentum = momentum_beta * momentum + delta
    new_weight = (
        value_weight.astype(jnp.float32) - outer_rate * (delta + momentum_beta * new_momentum)
    ).astype(jnp.bfloat16)
    return (new_weight, new_momentum)


def solution(mesh):
    in_specs = (
        P("island", "tensor", None),
        P("island", None, "tensor"),
        P("island", None, "tensor"),
        P("island", None, "tensor"),
        P("island", None),
        P(None, "tensor"),
        P(None, "tensor"),
        P(None, "tensor", None),
    )
    out_specs = (P(None, "tensor"), P(None, "tensor"))
    return jax.shard_map(local, mesh=mesh, in_specs=in_specs, out_specs=out_specs, check_vma=False)
```

profile of v0, /device:TPU:1, one launch (start us, length us, event | category | flops | bytes accessed | tf_op | source)
XLA Modules:
  0.0 519.0 jit_solution(16430361786796962226)
XLA Ops:
  7.2 0.0 copy-start.4
  7.2 0.0 all-gather.3.cloned.1.call-start
  7.2 0.7 all-gather.3.cloned.1.call-update
  7.9 0.0 all-reduce.2.cloned.1.call-start
  8.0 0.0 copy-start.5
  8.0 0.0 copy-start.6
  8.0 2.2 reshape_squeeze.12
  10.2 0.0 copy-done.4
  10.2 0.0 copy-start.1
  10.2 1.1 reshape_squeeze.14
  11.3 0.5 broadcast.168
  11.8 0.0 copy-done.5
  11.8 0.6 reduce.7
  12.4 0.0 copy-done.6
  12.4 0.6 copy.14
  13.0 0.0 copy-done.1
  13.0 33.6 %while.11 = (s32[]{:T(128)}, f32[1024,1,128]{0,2,1:T(8,128)}, bf16[2,512,1,4,128]{4,3,1,0,2:T(4,128)(2,1)}, s32[2,512]{1,0:T(2,128)S(1)}, s32[1,1024]{1,0:T(1,12...) while((s32[]{:T(128)}, f32[1024,1,128]{0,2,1:T(8,128)}, ...), condition=%wide.region_3.4_spmd.clone, body=%wide.region_0.3_spmd.clone.sunk | while | flops 1100739072 | bytes 66377888 | solution.py:60
  13.0 0.6 dynamic_slice.27
  13.6 0.6 iota_add_fusion.2
  14.2 0.6 fusion.45
  14.8 1.6 constant_dynamic-slice_fusion.6
  16.3 1.9 fusion.46
  18.2 2.5 fusion.47
  20.7 0.7 copy-done
  21.5 1.1 copy.26
  22.6 7.3 %fusion.48 = f32[1024,1,128]{0,2,1:T(8,128)} fusion(f32[4,512]{1,0:T(4,128)S(1)} %fusion.47, f32[4,512]{1,0:T(4,128)S(1)} %get-tuple-element.174, f32[512,4,1024]{2,0,1:T(8,128)} %copy-done, pred[512,1024]{1,0:T(8,128)(4,1)S(1)} %fusion.45, bf16[1,512,1,4,128]{1,4,3,2,0:T(8,128)(2,1)} %copy.26, f32[1024,1,128]{0,2,1:T(8,128)} %get-tuple-element.187, ...), kind=kOutput, calls=%fused_computation.11.clone.1 | convolution fusion | flops 547618816 | bytes 10502145 | tf_op jit(solution)/shard_map/while/body/eval_jaxpr/hgbs,bhgd->shd/dot_general | solution.py:54
  29.9 0.6 dynamic_slice.27
  30.5 0.6 iota_add_fusion.2
  31.1 0.6 fusion.45
  31.6 1.6 constant_dynamic-slice_fusion.6
  33.2 1.9 fusion.46
  35.1 2.5 fusion.47
  37.6 0.7 copy-done
  38.3 1.1 copy.26
  39.5 7.1 %fusion.48 = f32[1024,1,128]{0,2,1:T(8,128)} fusion(f32[4,512]{1,0:T(4,128)S(1)} %fusion.47, f32[4,512]{1,0:T(4,128)S(1)} %get-tuple-element.174, f32[512,4,1024]{2,0,1:T(8,128)} %copy-done, pred[512,1024]{1,0:T(8,128)(4,1)S(1)} %fusion.45, bf16[1,512,1,4,128]{1,4,3,2,0:T(8,128)(2,1)} %copy.26, f32[1024,1,128]{0,2,1:T(8,128)} %get-tuple-element.187, ...), kind=kOutput, calls=%fused_computation.11.clone.1 | convolution fusion | flops 547618816 | bytes 10502145 | tf_op jit(solution)/shard_map/while/body/eval_jaxpr/hgbs,bhgd->shd/dot_general | solution.py:54
  46.6 137.9 %all-gather.3.cloned.1.call-done = bf16[1,1024,4096]{2,1,0:T(8,128)(2,1)} async-done(((bf16[1,128,4096]{2,1,0:T(8,128)(2,1)}), bf16[1,1024,4096]{2,1,0:T(8,128)(2,1)}) %all-gather.3.cloned.1.call-update) | async-done | bytes 8388624 | tf_op jit(solution)/shard_map/all_gather | solution.py:96
  184.5 4.9 fusion.20
  189.4 3.6 fusion.26
  193.1 13.7 %select_reduce_fusion.1 = f32[4096,8]{1,0:T(8,128)} fusion(f32[4096,128]{1,0:T(8,128)S(1)} %fusion.26, s32[4096,8]{1,0:T(8,128)S(1)} %copy.14), kind=kLoop, calls=%fused_computation.23 | loop fusion | flops 12550144 | bytes 2359296 | tf_op jit(solution)/shard_map/reduce_sum | solution.py:69
  206.7 0.0 all-reduce.2.cloned.1.call-update
  206.7 279.8 %all-reduce.2.cloned.1.call-done = f32[4096,1,8]{2,0,1:T(8,128)} async-done(((f32[4096,1,8]{2,0,1:T(8,128)}), f32[4096,1,8]{2,0,1:T(8,128)}) %all-reduce.2.cloned.1.call-update) | async-done | bytes 131088 | tf_op jit(solution)/shard_map/psum | solution.py:81
  486.5 1.7 multiply_bitcast_fusion
  488.2 0.0 copy-start.2
  488.3 0.0 copy-start.3
  488.3 19.9 %select_reduce_fusion = f32[4096,128]{1,0:T(8,128)S(1)} fusion(f32[4096,8]{1,0:T(8,128)S(1)} %multiply_bitcast_fusion, s32[4096,8]{1,0:T(8,128)S(1)} %copy.14), kind=kLoop, calls=%fused_computation.22 | loop fusion | flops 12058624 | bytes 2359296 | tf_op jit(solution)/shard_map/reduce_sum | solution.py:75
  508.2 0.0 copy-done.2
  508.2 0.0 copy-done.3
  508.2 4.0 subtract_convert_fusion
  (8 shorter events, 0.0 us)
Async XLA Ops:
  7.2 3.0 copy-start.4
  7.2 177.4 %all-gather.3.cloned.1.call-start = ((), (), s32[]{:S(2)}) async-start(), calls=%async_computation.1 | async-start | bytes 9437184 | tf_op jit(solution)/shard_map/all_gather | solution.py:96
  7.9 478.6 %all-reduce.2.cloned.1.call-start = ((), (), s32[]{:S(2)}) async-start(), calls=%async_computation | async-start | bytes 4194304 | tf_op jit(solution)/shard_map/psum | solution.py:81
  8.0 3.8 copy-start.5
  8.0 4.4 copy-start.6
  10.2 2.8 copy-start.1
  18.2 3.2 copy-start
  35.1 3.2 copy-start
  488.2 19.9 %copy-start.2 = (f32[4096,128]{1,0:T(8,128)S(1)}, f32[4096,128]{1,0:T(8,128)}, u32[]{:S(2)}) copy-start(f32[4096,128]{1,0:T(8,128)} %param.16) | copy-start | bytes 6291460
  488.3 19.9 %copy-start.3 = (bf16[4096,128]{1,0:T(8,128)(2,1)S(1)}, bf16[4096,128]{1,0:T(8,128)(2,1)}, u32[]{:S(2)}) copy-start(bf16[4096,128]{1,0:T(8,128)(2,1)} %param.15) | copy-start | bytes 3145732
Sparse Core Ops, SparseCore 0:
  9.8 174.6 all-gather.2
  206.9 279.6 all-reduce.1
where the time goes:
time: 519 us
  waiting for transfers between devices  418 us (81%)
  other arithmetic  43.2 us (8%)
  matrix products  30.7 us (6%)
  between operations  14.2 us (3%)
  local copies, waits for them, and re-layouts  12.4 us (2%)
    psum x1, waiting for transfers between devices, island_mean(): summed = lax.psum(kept, 'island')  280 us
    all_gather x1, waiting for transfers between devices, local(): lax.all_gather(layer_rows, 'tensor', axis=0, tiled=True)  138 us
    reduce_sum x1, other arithmetic, decode(): dense = jnp.sum(jnp.where(picker, kept[:, :, :, None], 0.0), axis=2)  19.9 us
    dot_general x2, matrix products, step(): jnp.einsum('hgbs,bhgd->shd', probs, grad_block, preferred_element_type=jn...  14.4 us
    reduce_sum x1, other arithmetic, encode(): return jnp.sum(jnp.where(picker, coeffs[:, :, None, :], 0.0), axis=3)  13.7 us
  transfers between devices with their start and end apart: 2, of which 2 were waited for; matrix products, arithmetic and copies ran while one was open for 7% of the time, Pallas kernels for 0%

commit v1 on v0

v1 whole, which is shorter than its diff:
```python
import functools
import math

import jax
import jax.numpy as jnp
import numpy as np
from jax import lax
from jax.experimental import pallas as pl
from jax.experimental.pallas import tpu as pltpu
from jax.sharding import Mesh
from jax.sharding import PartitionSpec as P

HEAD_DIM = 128
KEEP = 8
SPAN = 512
ROWS = 256

inner_rate = 0.01
outer_rate = 0.7
momentum_beta = 0.9
masked_score = -1e30
exp2_scale = HEAD_DIM ** (-0.5) / math.log(2.0)

BF16 = jnp.bfloat16
F32 = jnp.float32
LAST = (((1,), (1,)), ((), ()))
PLAIN = (((1,), (0,)), ((), ()))
FIRST = (((0,), (0,)), ((), ()))
MIB = 1 << 20


def dot(a, b, dims):
    return lax.dot_general(a, b, dims, preferred_element_type=F32)


def dct_tables():
    frequency = np.arange(HEAD_DIM, dtype=np.float64)[:, None]
    sample = np.arange(HEAD_DIM, dtype=np.float64)[None, :]
    basis = np.cos(np.pi * (sample + 0.5) * frequency / HEAD_DIM)
    table = basis * np.where(frequency == 0.0, math.sqrt(1.0 / HEAD_DIM), math.sqrt(2.0 / HEAD_DIM))
    high = table.astype(jnp.bfloat16)
    low = (table - high.astype(np.float64)).astype(jnp.bfloat16)
    return high, low


def grads_kernel(doc_ref, q_ref, k_ref, g_ref, index_ref, out_ref, cap_ref, total_ref):
    length = k_ref.shape[0]
    group = q_ref.shape[1] // HEAD_DIM
    docs = doc_ref[...]
    first = jnp.zeros_like(docs)
    for ident in (1, 2, 3):
        before = jnp.sum((docs < ident).astype(jnp.int32), axis=1, keepdims=True)
        first = jnp.where(docs == ident, before, first)
    total_ref[...] = jnp.zeros_like(total_ref)
    for row in range(0, length, ROWS):
        low = max(0, row - SPAN)
        width = row + ROWS - low
        start = first[:, row : row + ROWS]
        key = lax.broadcasted_iota(jnp.int32, (width, ROWS), 0) + low
        query = lax.broadcasted_iota(jnp.int32, (width, ROWS), 1) + row
        allowed = (key >= start) & (key <= query)
        cap_ref[:width] = jnp.where(allowed, jnp.finfo(F32).max, masked_score)
        for head in range(group):
            lanes = slice(head * HEAD_DIM, (head + 1) * HEAD_DIM)
            scores = dot(k_ref[low : row + ROWS], q_ref[row : row + ROWS, lanes], LAST)
            scores = jnp.minimum(scores, cap_ref[:width])
            peak = jnp.max(scores, axis=0, keepdims=True)
            weights = jnp.exp2((scores - peak) * exp2_scale)
            inverse = 1.0 / jnp.sum(weights, axis=0, keepdims=True)
            probs = (weights * inverse).astype(BF16)
            total_ref[low : row + ROWS] += dot(probs, g_ref[row : row + ROWS, lanes], PLAIN)
    parts = out_ref.shape[0]
    part = length // parts
    for p in range(parts):
        out_ref[p, :part] = total_ref[p * part : (p + 1) * part].astype(BF16)
        out_ref[p, part:] = index_ref[...]


def value_grads(doc_ids, queries, key_states, out_grads, index_rows, parts):
    length = key_states.shape[0]
    part = length // parts
    return pl.pallas_call(
        grads_kernel,
        out_shape=jax.ShapeDtypeStruct((parts, part + index_rows.shape[0], HEAD_DIM), BF16),
        scratch_shapes=[pltpu.VMEM((SPAN + ROWS, ROWS), F32), pltpu.VMEM((length, HEAD_DIM), F32)],
        compiler_params=pltpu.CompilerParams(vmem_limit_bytes=40 * MIB),
    )(doc_ids, queries, key_states, out_grads, index_rows)


def encode_kernel(own_ref, other_ref, hid_own_ref, hid_other_ref, high_ref, low_ref, kept_ref, wave_ref, hid_ref):
    heads = own_ref.shape[0]
    part = other_ref.shape[1]
    half = hid_own_ref.shape[1] // 2
    hid_ref[:part] = hid_own_ref[...]
    hid_ref[part:] = hid_other_ref[...]
    both = 2 * part
    for h in range(heads):
        values = jnp.concatenate([own_ref[h, :part], other_ref[h]], axis=0)
        wave = dot(high_ref[...], values, LAST) + dot(low_ref[...], values, LAST)
        high = wave.astype(BF16)
        wave_ref[h, :, :both] = high
        wave_ref[h, :, both:] = (wave - high.astype(F32)).astype(BF16)

    def step(c, carry):
        at = pl.multiple_of(c * 128, 128)
        rows = jnp.concatenate([hid_ref[:, pl.ds(at, 128)], hid_ref[:, pl.ds(half + at, 128)]], axis=1)
        rows = jnp.concatenate([rows, rows], axis=0)
        for h in range(heads):
            coeffs = dot(wave_ref[h], rows, PLAIN)
            place = pl.multiple_of(part + c * 16, 16)
            index = own_ref[h, pl.ds(place, 16), :].astype(F32).astype(jnp.int32)
            kept = []
            for side in range(2):
                mine = index[side * 8 : side * 8 + 8]
                block, within = mine // 8, mine % 8
                found = jnp.zeros((8, 128), F32)
                for v in range(16):
                    vreg = coeffs[v * 8 : v * 8 + 8, side * 128 : side * 128 + 128]
                    picked = jnp.take_along_axis(vreg, within, axis=0)
                    found = jnp.where(block == v, picked, found)
                kept.append(found)
            kept_ref[h, :, pl.ds(at, 128)] = jnp.concatenate(kept, axis=0).astype(BF16)
        return carry

    lax.fori_loop(0, half // 128, step, 0)


def encode(own, other, hid_own, hid_other, high, low):
    heads, part = own.shape[0], other.shape[1]
    half = hid_own.shape[1] // 2
    return pl.pallas_call(
        encode_kernel,
        out_shape=jax.ShapeDtypeStruct((heads, 2 * KEEP, half), BF16),
        scratch_shapes=[pltpu.VMEM((heads, HEAD_DIM, 4 * part), BF16), pltpu.VMEM((2 * part, 2 * half), BF16)],
        compiler_params=pltpu.CompilerParams(vmem_limit_bytes=40 * MIB),
    )(own, other, hid_own, hid_other, high, low)


def update_kernel(scale, kept_ref, index_ref, high_ref, low_ref, momentum_ref, weight_ref, new_weight_ref, new_momentum_ref):
    frequency = lax.broadcasted_iota(jnp.int32, (HEAD_DIM, 128), 0)
    for c in range(index_ref.shape[1] // 128):
        lanes = slice(c * 128, (c + 1) * 128)
        dense = jnp.zeros((HEAD_DIM, 128), F32)
        for t in range(KEEP):
            dense = jnp.where(frequency == index_ref[t : t + 1, lanes], kept_ref[0, t : t + 1, lanes] * scale, dense)
        high = dense.astype(BF16)
        low = (dense - high.astype(F32)).astype(BF16)
        delta = dot(high, high_ref[...], FIRST) + dot(low, high_ref[...], FIRST) + dot(high, low_ref[...], FIRST)
        fresh = momentum_beta * momentum_ref[lanes] + delta
        new_momentum_ref[lanes] = fresh
        new_weight_ref[lanes] = (
            weight_ref[lanes].astype(F32) - outer_rate * (delta + momentum_beta * fresh)
        ).astype(BF16)


def update(scale, kept, index, high, low, momentum, weight):
    rows = momentum.shape[0]
    block = rows // 4
    table = pl.BlockSpec((HEAD_DIM, HEAD_DIM), lambda i: (0, 0))
    wide = pl.BlockSpec((block, HEAD_DIM), lambda i: (i, 0))
    return pl.pallas_call(
        functools.partial(update_kernel, scale),
        grid=(4,),
        out_shape=(jax.ShapeDtypeStruct(weight.shape, BF16), jax.ShapeDtypeStruct(momentum.shape, F32)),
        in_specs=[
            pl.BlockSpec((1, KEEP, block), lambda i: (i, 0, 0)),
            pl.BlockSpec((KEEP, block), lambda i: (0, i)),
            table,
            table,
            wide,
            wide,
        ],
        out_specs=(wide, wide),
        compiler_params=pltpu.CompilerParams(vmem_limit_bytes=40 * MIB),
    )(kept, index, high, low, momentum, weight)


def swap(x):
    return lax.ppermute(x, "core", [(0, 1), (1, 0)])


def local(hidden_rows, queries, key_states, out_grads, doc_ids, value_weight, momentum, keep_index):
    high, low = dct_tables()
    tensor, ring = ("x", "y_lo"), ("z", "y_hi")
    parts = lax.axis_size(tensor)
    islands = lax.axis_size(ring) * 2
    core = lax.axis_index("core")
    hidden = hidden_rows[0]
    half = hidden.shape[1] // 2
    hid_own = lax.dynamic_slice_in_dim(hidden, core * half, half, 1)
    hid_other = swap(lax.dynamic_slice_in_dim(hidden, (1 - core) * half, half, 1))
    index = keep_index[:, 0, :].T
    mine = lax.dynamic_slice_in_dim(index, core * half, half, 1)
    index_rows = mine.reshape(KEEP, 2, half // 256, 128).transpose(2, 1, 0, 3).reshape(-1, 128).astype(BF16)
    packed = value_grads(doc_ids, queries[0], key_states[0], out_grads[0], index_rows, parts)
    packed = lax.all_to_all(packed, tensor, 0, 0, tiled=True)
    part = hidden.shape[0]
    other = swap(packed[:, :part])
    kept = encode(packed, other, hid_own, hid_other, high, low)
    kept = lax.all_to_all(kept, tensor, 0, 0, tiled=True)
    kept = jnp.sum(kept.astype(F32), axis=0).astype(BF16)
    spread = jnp.broadcast_to(kept[None], (lax.axis_size(ring),) + kept.shape)
    kept = jnp.sum(lax.all_to_all(spread, ring, 0, 0, tiled=True).astype(F32), axis=0)
    there = swap(kept)
    first = jnp.where(core == 0, kept, there)
    second = jnp.where(core == 0, there, kept)
    kept = jnp.concatenate([first, second], axis=0).reshape(4, KEEP, half // 2)
    return update(inner_rate / islands, kept, index, high, low, momentum, value_weight)


def solution(mesh):
    fine = Mesh(mesh.devices.reshape(-1, 2, 2, 4, 2), ("z", "y_hi", "core", "x", "y_lo"))
    island, tensor = ("z", "y_hi", "core"), ("x", "y_lo")
    in_specs = (
        P(island, tensor, None),
        P(island, None, tensor),
        P(island, None, tensor),
        P(island, None, tensor),
        P(island, None),
        P(None, tensor),
        P(None, tensor),
        P(None, tensor, None),
    )
    out_specs = (P(None, tensor), P(None, tensor))
    return jax.shard_map(local, mesh=fine, in_specs=in_specs, out_specs=out_specs, check_vma=False)
```

time: 519 us -> 79.3 us (0.15)
  waiting for transfers between devices: 418 us -> 9.6 us
  other arithmetic: 43.2 us -> 1.94 us
  blocking collectives: 0 us -> 35.5 us
  matrix products: 30.7 us -> 0 us
  between operations: 14.2 us -> 0.75 us
  Pallas kernels: 0 us -> 13.4 us
  starting transfers between devices: 0.08 us -> 13.3 us
  local copies, waits for them, and re-layouts: 12.4 us -> 4.29 us
    psum x1 -> x0, waiting for transfers between devices: 280 us -> none  [island_mean(): summed = lax.psum(kept, 'island')]
    all_gather x1 -> x0, waiting for transfers between devices: 138 us -> none  [local(): lax.all_gather(layer_rows, 'tensor', axis=0, tiled=True)]
    reduce_sum x4 -> x2, other arithmetic: 38.5 us -> 1.07 us  [the longest x1 0.99 us: local(): kept = jnp.sum(kept.astype(F32), axis=0).astype(BF16)]
    all_to_all x0 -> x2, blocking collectives: none -> 35.5 us  [the longest x1 26.2 us: local(): lax.all_to_all(spread, ring, 0, 0, tiled=True).astype(F32)]
    dot_general x7 -> x0, matrix products: 30.7 us -> none  [the longest x2 14.4 us: step(): jnp.einsum('hgbs,bhgd->shd', probs, grad_block, preferred_element_type=jn...]
    pallas_call x0 -> x3, Pallas kernels: none -> 13.4 us  [the longest x1 5.07 us: value_grads(): pl.pallas_call(grads_kernel, out_shape=jax.ShapeDtypeStruct((parts, part...]
    all_to_all x0 -> x1, waiting for transfers between devices: none -> 7.53 us  [local(): packed = lax.all_to_all(packed, tensor, 0, 0, tiled=True)]
    ppermute x0 -> x3, starting transfers between devices: none -> 7.27 us  [swap(): return lax.ppermute(x, 'core', [(0, 1), (1, 0)])]
  transfers between devices with their start and end apart: 2 -> 4, of which waited for: 2 -> 3; matrix products, arithmetic and copies ran while one was open for 7% -> 0% of each run, Pallas kernels for 0% -> 0%
where the time goes in v1:
time: 79.3 us; the launch traced here: 78.8 us
  blocking collectives  35.5 us (45%)
  Pallas kernels  13.4 us (17%)
  starting transfers between devices  13.3 us (17%)
  waiting for transfers between devices  9.6 us (12%)
  local copies, waits for them, and re-layouts  4.29 us (5%)
  other arithmetic  1.94 us (2%)
    all_to_all x1, blocking collectives, local(): lax.all_to_all(spread, ring, 0, 0, tiled=True).astype(F32)  26.2 us
    all_to_all x1, blocking collectives, local(): kept = lax.all_to_all(kept, tensor, 0, 0, tiled=True)  9.32 us
    all_to_all x1, waiting for transfers between devices, local(): packed = lax.all_to_all(packed, tensor, 0, 0, tiled=True)  7.53 us
    ppermute x3, starting transfers between devices, swap(): return lax.ppermute(x, 'core', [(0, 1), (1, 0)])  7.27 us
    all_to_all x1, starting transfers between devices, local(): packed = lax.all_to_all(packed, tensor, 0, 0, tiled=True)  5.99 us
    pallas_call x1, Pallas kernels, value_grads(): pl.pallas_call(grads_kernel, out_shape=jax.ShapeDtypeStruct((parts, part...  5.07 us
    pallas_call x1, Pallas kernels, update(): pl.pallas_call(functools.partial(update_kernel, scale), grid=(4,), out_sh...  4.17 us
    pallas_call x1, Pallas kernels, encode(): pl.pallas_call(encode_kernel, out_shape=jax.ShapeDtypeStruct((heads, 2 *...  4.16 us
  transfers between devices with their start and end apart: 4, of which 3 were waited for; matrix products, arithmetic and copies ran while one was open for 0% of the time, Pallas kernels for 0%

profile of v1, /device:TPU:1, one launch (start us, length us, event | category | flops | bytes accessed | tf_op | source)
XLA Modules:
  0.0 78.8 jit_solution(6797980687102665845)
XLA Ops:
  0.6 0.8 %dynamic-slice_convert_fusion = bf16[2048,1,8]{0,2,1:T(8,128)(2,1)S(1)} fusion(s32[4096,1,8]{0,2,1:T(8,128)} %param.17, s32[]{:T(128)S(6)} %select_n.20), kind=kLoop, calls=%fused_computation.4 | loop fusion | flops 16384 | bytes 98308 | tf_op jit(solution)/shard_map/convert.1
  1.5 0.0 copy-start.1
  1.5 1.2 %copy-done.1 = bf16[1,1024,512]{2,1,0:T(8,128)(2,1)S(1)} copy-done((bf16[1,1024,512]{2,1,0:T(8,128)(2,1)S(1)}, bf16[1,1024,512]{2,1,0:T(8,128)(2,1)}, u32[]{:S(2)}) %copy-start.1) | copy-done | bytes 1048600
  2.7 0.0 copy-start.2
  2.7 1.2 %copy-done.2 = bf16[1,1024,512]{2,1,0:T(8,128)(2,1)S(1)} copy-done((bf16[1,1024,512]{2,1,0:T(8,128)(2,1)S(1)}, bf16[1,1024,512]{2,1,0:T(8,128)(2,1)}, u32[]{:S(2)}) %copy-start.2) | copy-done | bytes 1048600
  3.9 0.0 copy-start.5
  3.9 0.9 %copy-done.5 = bf16[1,1024,128]{2,1,0:T(8,128)(2,1)S(1)} copy-done((bf16[1,1024,128]{2,1,0:T(8,128)(2,1)S(1)}, bf16[1,1024,128]{2,1,0:T(8,128)(2,1)}, u32[]{:S(2)}) %copy-start.5) | copy-done | bytes 262168
  4.9 0.0 copy-start.8
  4.9 0.7 copy-done.8
  5.6 0.0 copy-start.9
  5.6 5.1 %shard_map.113 = bf16[8,256,128]{2,1,0:T(8,128)(2,1)} custom-call(s32[1,1024]{1,0:T(1,128)S(1)} %copy-done.8, bf16[1024,512]{1,0:T(8,128)(2,1)S(1)} %bitcast.20, bf16[1024,128]{1,0:T(8,128)(2,1)S(1)} %bitcast.23, bf16[1024,512]{1,0:T(8,128)(2,1)S(1)} %bitcast.21, bf16[128,128]{1,0:T(8,128)(2,1)S(1)} %bitcast.24), custom_call_target="tpu_custom_call" | custom-call | tf_op jit(solution)/shard_map/pallas_call | solution.py:82
  10.7 0.0 copy-start.6
  10.7 0.0 copy-start.7
  10.7 6.0 %all-to-all-start = ((bf16[8,256,128]{2,1,0:T(8,128)(2,1)}), bf16[8,256,128]{2,1,0:T(8,128)(2,1)S(1)}, u32[]{:S(2)}, u32[]{:S(2)}) async-start(bf16[8,256,128]{2,1,0:T(8,128)(2,1)} %shard_map.113), calls=%async_computation | async-start | bytes 1048576 | tf_op jit(solution)/shard_map/all_to_all | solution.py:196
  16.7 0.0 copy-done.9
  16.7 0.1 dynamic-slice_bitcast_fusion
  16.8 1.0 %collective-permute-start.1 = (bf16[128,2048]{1,0:T(8,128)(2,1)S(1)}, bf16[128,2048]{1,0:T(8,128)(2,1)S(1)}, u32[]{:S(2)}, u32[]{:S(2)}) collective-permute-start(bf16[128,2048]{1,0:T(8,128)(2,1)S(1)} %get-tuple-element.2), channel_id=1, source_target_pairs={{0,8},{8,0},{1,9},{9,1},{2,10},{10,2},{3,11},{11,3},{4,12},{12,4},... | collective-permute-start | bytes 1572872 | tf_op jit(solution)/shard_map/ppermute | solution.py:179
  17.8 7.5 %all-to-all-done.own_ref = bf16[8,256,128]{2,1,0:T(8,128)(2,1)S(1)} async-done(((bf16[8,256,128]{2,1,0:T(8,128)(2,1)}), bf16[8,256,128]{2,1,0:T(8,128)(2,1)S(1)}, u32[]{:S(2)}, u32[]{:S(2)}) %all-to-all-start) | async-done | bytes 524320 | tf_op jit(solution)/shard_map/all_to_all | solution.py:196
  25.4 1.8 %collective-permute-start = (bf16[8,128,128]{2,1,0:T(8,128)(2,1)S(1)}, bf16[8,128,128]{2,1,0:T(8,128)(2,1)S(1)}, u32[]{:S(2)}, u32[]{:S(2)}) collective-permute-start(bf16[8,128,128]{2,1,0:T(8,128)(2,1)S(1)} %slice.4), channel_id=1, source_target_pairs={{0,8},{8,0},{1,9},{9,1},{2,10},{10,2},{3,11},{11,3},{4,12},{12,4},... | collective-permute-start | bytes 786440 | tf_op jit(solution)/shard_map/ppermute | solution.py:179
  27.2 0.0 collective-permute-done.1.hid_other_ref
  27.2 1.2 %collective-permute-done.other_ref = bf16[8,128,128]{2,1,0:T(8,128)(2,1)S(1)} collective-permute-done((bf16[8,128,128]{2,1,0:T(8,128)(2,1)S(1)}, bf16[8,128,128]{2,1,0:T(8,128)(2,1)S(1)}, u32[]{:S(2)}, u32[]{:S(2)}) %collective-permute-start) | collective-permute-done | bytes 262176 | tf_op jit(solution)/shard_map/ppermute | solution.py:179
  28.4 0.0 copy-done.6
  28.4 0.0 copy-done.7
  28.4 4.2 %shard_map.114 = bf16[8,16,1024]{2,1,0:T(8,128)(2,1)S(1)} custom-call(bf16[8,256,128]{2,1,0:T(8,128)(2,1)S(1)} %all-to-all-done.own_ref, bf16[8,128,128]{2,1,0:T(8,128)(2,1)S(1)} %collective-permute-done.other_ref, bf16[128,2048]{1,0:T(8,128)(2,1)S(1)} %get-tuple-element.3.hid_own_ref, bf16[128,2048]{1,0:T(8,128)(2,1)S(1)} %collective-permute-done.1.hid_other_ref, ...), custom_call_target="tpu_custom_call" | custom-call | tf_op jit(solution)/shard_map/pallas_call | solution.py:131
  32.5 0.0 copy-start
  32.5 0.0 copy-start.3
  32.6 0.0 copy-start.4
  32.6 9.3 %all_to_all.15 = bf16[8,16,1024]{2,1,0:T(8,128)(2,1)} all-to-all(bf16[8,16,1024]{2,1,0:T(8,128)(2,1)S(1)} %shard_map.114), channel_id=1, replica_groups=mesh['z'=8,'y_hi'=2,'core'=2,'x'=4,'y_lo'=2] {'x','y_lo'}, dimensions={0} | all-to-all | bytes 524288 | tf_op jit(solution)/shard_map/all_to_all | solution.py:200
  41.9 1.0 %reduce_sum.21 = bf16[16,1024]{1,0:T(8,128)(2,1)S(1)} reduce(bf16[8,16,1024]{2,1,0:T(8,128)(2,1)} %all_to_all.15, bf16[]{:T(256)} %constant.23.clone.1), dimensions={0}, to_apply=%region_0.0 | reduce | flops 114688 | bytes 294914 | tf_op jit(solution)/shard_map/reduce_sum | solution.py:201
  42.9 0.1 broadcast_in_dim.2
  42.9 26.2 %all_to_all.16 = bf16[16,16,1024]{2,1,0:T(8,128)(2,1)S(1)} all-to-all(bf16[16,16,1024]{2,1,0:T(8,128)(2,1)S(1)} %broadcast_in_dim.2), channel_id=1, replica_groups=mesh['z'=8,'y_hi'=2,'core'=2,'x'=4,'y_lo'=2] {'z','y_hi'}, dimensions={0} | all-to-all | bytes 1048576 | tf_op jit(solution)/shard_map/all_to_all | solution.py:203
  69.2 0.1 convert_reduce_fusion
  69.2 4.4 %collective-permute-start.2 = (f32[16,1024]{1,0:T(8,128)S(1)}, f32[16,1024]{1,0:T(8,128)S(1)}, u32[]{:S(2)}, u32[]{:S(2)}) collective-permute-start(f32[16,1024]{1,0:T(8,128)S(1)} %convert_reduce_fusion), channel_id=1, source_target_pairs={{0,8},{8,0},{1,9},{9,1},{2,10},{10,2},{3,11},{11,3},{4,12},{12,4},... | collective-permute-start | bytes 196616 | tf_op jit(solution)/shard_map/ppermute | solution.py:179
  73.7 0.9 %collective-permute-done.2 = f32[16,1024]{1,0:T(8,128)S(1)} collective-permute-done((f32[16,1024]{1,0:T(8,128)S(1)}, f32[16,1024]{1,0:T(8,128)S(1)}, u32[]{:S(2)}, u32[]{:S(2)}) %collective-permute-start.2) | collective-permute-done | bytes 65568 | tf_op jit(solution)/shard_map/ppermute | solution.py:179
  74.6 0.0 copy-done
  74.6 0.0 copy-done.3
  74.6 0.0 copy-done.4
  74.6 4.2 %shard_map.115 = (bf16[4096,128]{1,0:T(8,128)(2,1)}, f32[4096,128]{1,0:T(8,128)}) custom-call(f32[4,8,1024]{2,1,0:T(8,128)S(1)} %maximum_bitcast_fusion.kept_ref, s32[8,4096]{1,0:T(8,128)S(1)} %bitcast.22, bf16[128,128]{1,0:T(8,128)(2,1)S(1)} %copy-done.7, bf16[128,128]{1,0:T(8,128)(2,1)S(1)} %copy-done.6, f32[4096,128]{1,0:T(8,128)S(1)} %copy-done, ...), custom_call_target="tpu_custom_call" | custom-call | tf_op jit(solution)/shard_map/pallas_call | solution.py:161
  (4 shorter events, 0.0 us)
Async XLA Ops:
  1.5 1.2 %copy-start.1 = (bf16[1,1024,512]{2,1,0:T(8,128)(2,1)S(1)}, bf16[1,1024,512]{2,1,0:T(8,128)(2,1)}, u32[]{:S(2)}) copy-start(bf16[1,1024,512]{2,1,0:T(8,128)(2,1)} %param.11) | copy-start | bytes 3145732
  2.7 1.2 %copy-start.2 = (bf16[1,1024,512]{2,1,0:T(8,128)(2,1)S(1)}, bf16[1,1024,512]{2,1,0:T(8,128)(2,1)}, u32[]{:S(2)}) copy-start(bf16[1,1024,512]{2,1,0:T(8,128)(2,1)} %param.13) | copy-start | bytes 3145732
  3.9 0.9 %copy-start.5 = (bf16[1,1024,128]{2,1,0:T(8,128)(2,1)S(1)}, bf16[1,1024,128]{2,1,0:T(8,128)(2,1)}, u32[]{:S(2)}) copy-start(bf16[1,1024,128]{2,1,0:T(8,128)(2,1)} %param.12) | copy-start | bytes 786436
  4.9 0.7 copy-start.8
  5.6 11.1 %copy-start.9 = (bf16[1,128,4096]{2,1,0:T(8,128)(2,1)S(1)}, bf16[1,128,4096]{2,1,0:T(8,128)(2,1)}, u32[]{:S(2)}) copy-start(bf16[1,128,4096]{2,1,0:T(8,128)(2,1)} %param.10) | copy-start | bytes 3145732
  10.7 17.7 %copy-start.6 = (bf16[128,128]{1,0:T(8,128)(2,1)S(1)}, bf16[128,128]{1,0:T(8,128)(2,1)}, u32[]{:S(2)}) copy-start(bf16[128,128]{1,0:T(8,128)(2,1)} %constant.26.clone.low_ref) | copy-start | bytes 98308
  10.7 17.7 %copy-start.7 = (bf16[128,128]{1,0:T(8,128)(2,1)S(1)}, bf16[128,128]{1,0:T(8,128)(2,1)}, u32[]{:S(2)}) copy-start(bf16[128,128]{1,0:T(8,128)(2,1)} %constant.25.clone.high_ref) | copy-start | bytes 98308
  10.7 14.7 %all-to-all-start = ((bf16[8,256,128]{2,1,0:T(8,128)(2,1)}), bf16[8,256,128]{2,1,0:T(8,128)(2,1)S(1)}, u32[]{:S(2)}, u32[]{:S(2)}) async-start(bf16[8,256,128]{2,1,0:T(8,128)(2,1)} %shard_map.113), calls=%async_computation | async-start | bytes 1048576 | tf_op jit(solution)/shard_map/all_to_all | solution.py:196
  16.8 10.4 %collective-permute-start.1 = (bf16[128,2048]{1,0:T(8,128)(2,1)S(1)}, bf16[128,2048]{1,0:T(8,128)(2,1)S(1)}, u32[]{:S(2)}, u32[]{:S(2)}) collective-permute-start(bf16[128,2048]{1,0:T(8,128)(2,1)S(1)} %get-tuple-element.2), channel_id=1, source_target_pairs={{0,8},{8,0},{1,9},{9,1},{2,10},{10,2},{3,11},{11,3},{4,12},{12,4},... | collective-permute-start | bytes 1572872 | tf_op jit(solution)/shard_map/ppermute | solution.py:179
  25.4 3.0 %collective-permute-start = (bf16[8,128,128]{2,1,0:T(8,128)(2,1)S(1)}, bf16[8,128,128]{2,1,0:T(8,128)(2,1)S(1)}, u32[]{:S(2)}, u32[]{:S(2)}) collective-permute-start(bf16[8,128,128]{2,1,0:T(8,128)(2,1)S(1)} %slice.4), channel_id=1, source_target_pairs={{0,8},{8,0},{1,9},{9,1},{2,10},{10,2},{3,11},{11,3},{4,12},{12,4},... | collective-permute-start | bytes 786440 | tf_op jit(solution)/shard_map/ppermute | solution.py:179
  32.5 42.1 %copy-start = (f32[4096,128]{1,0:T(8,128)S(1)}, f32[4096,128]{1,0:T(8,128)}, u32[]{:S(2)}) copy-start(f32[4096,128]{1,0:T(8,128)} %momentum_ref.1) | copy-start | bytes 6291460
  32.5 42.1 %copy-start.3 = (bf16[4096,128]{1,0:T(8,128)(2,1)S(1)}, bf16[4096,128]{1,0:T(8,128)(2,1)}, u32[]{:S(2)}) copy-start(bf16[4096,128]{1,0:T(8,128)(2,1)} %weight_ref.1) | copy-start | bytes 3145732
  32.6 42.1 %copy-start.4 = (s32[4096,1,8]{0,2,1:T(8,128)S(1)}, s32[4096,1,8]{0,2,1:T(8,128)}, u32[]{:S(2)}) copy-start(s32[4096,1,8]{0,2,1:T(8,128)} %param.17) | copy-start | bytes 393220
  69.2 5.3 %collective-permute-start.2 = (f32[16,1024]{1,0:T(8,128)S(1)}, f32[16,1024]{1,0:T(8,128)S(1)}, u32[]{:S(2)}, u32[]{:S(2)}) collective-permute-start(f32[16,1024]{1,0:T(8,128)S(1)} %convert_reduce_fusion), channel_id=1, source_target_pairs={{0,8},{8,0},{1,9},{9,1},{2,10},{10,2},{3,11},{11,3},{4,12},{12,4},... | collective-permute-start | bytes 196616 | tf_op jit(solution)/shard_map/ppermute | solution.py:179

commit v2 on v1

v2 whole, which is shorter than its diff:
```python
import functools
import math

import jax
import jax.numpy as jnp
import numpy as np
from jax import lax
from jax.experimental import pallas as pl
from jax.experimental.pallas import tpu as pltpu
from jax.sharding import Mesh
from jax.sharding import PartitionSpec as P

HEAD_DIM = 128
KEEP = 8
SPAN = 512
ROWS = 128
FETCH = 256
STORE = 512

inner_rate = 0.01
outer_rate = 0.7
momentum_beta = 0.9
masked_score = -1e30
exp2_scale = HEAD_DIM ** (-0.5) / math.log(2.0)

BF16 = jnp.bfloat16
F32 = jnp.float32
LAST = (((1,), (1,)), ((), ()))
PLAIN = (((1,), (0,)), ((), ()))
FIRST = (((0,), (0,)), ((), ()))
MIB = 1 << 20


def dot(a, b, dims):
    return lax.dot_general(a, b, dims, preferred_element_type=F32)


def dct_tables():
    frequency = np.arange(HEAD_DIM, dtype=np.float64)[:, None]
    sample = np.arange(HEAD_DIM, dtype=np.float64)[None, :]
    basis = np.cos(np.pi * (sample + 0.5) * frequency / HEAD_DIM)
    table = basis * np.where(frequency == 0.0, math.sqrt(1.0 / HEAD_DIM), math.sqrt(2.0 / HEAD_DIM))
    high = table.astype(jnp.bfloat16)
    low = (table - high.astype(np.float64)).astype(jnp.bfloat16)
    return high, low


def grads_kernel(
    core_ref, doc_hbm, q_hbm, k_hbm, g_hbm, index_hbm, out_ref, doc_ref, q_ref, k_ref, g_ref, index_ref, cap_ref, total_ref, sems
):
    length = k_ref.shape[0]
    group = q_ref.shape[1] // HEAD_DIM
    half = index_ref.shape[1]
    count = length // FETCH

    def fetch(source, target, sem):
        copy = pltpu.make_async_copy(source, target, sems.at[sem])
        copy.start()
        return copy

    doc_copy = fetch(doc_hbm, doc_ref, 0)
    copies = []
    for b in range(count):
        rows = pl.ds(b * FETCH, FETCH)
        copies.append(
            [
                fetch(source.at[rows], target.at[rows], 2 + 3 * b + n)
                for n, (source, target) in enumerate(((k_hbm, k_ref), (q_hbm, q_ref), (g_hbm, g_ref)))
            ]
        )
    at = pl.multiple_of(core_ref[0] * half, 128)
    index_copy = fetch(index_hbm.at[:, pl.ds(at, half)], index_ref, 1)

    total_ref[...] = jnp.zeros_like(total_ref)
    doc_copy.wait()
    docs = doc_ref[...]
    first = jnp.zeros_like(docs)
    for ident in (1, 2, 3):
        before = jnp.sum((docs < ident).astype(jnp.int32), axis=1, keepdims=True)
        first = jnp.where(docs == ident, before, first)
    for row in range(0, length, ROWS):
        if row % FETCH == 0:
            for copy in copies[row // FETCH]:
                copy.wait()
        low = max(0, row - SPAN)
        width = row + ROWS - low
        start = first[:, row : row + ROWS]
        key = lax.broadcasted_iota(jnp.int32, (width, ROWS), 0) + low
        query = lax.broadcasted_iota(jnp.int32, (width, ROWS), 1) + row
        allowed = (key >= start) & (key <= query)
        cap_ref[:width] = jnp.where(allowed, jnp.finfo(F32).max, masked_score)
        for head in range(group):
            lanes = slice(head * HEAD_DIM, (head + 1) * HEAD_DIM)
            scores = dot(k_ref[low : row + ROWS], q_ref[row : row + ROWS, lanes], LAST)
            scores = jnp.minimum(scores, cap_ref[:width])
            peak = jnp.max(scores, axis=0, keepdims=True)
            weights = jnp.exp2((scores - peak) * exp2_scale)
            inverse = 1.0 / jnp.sum(weights, axis=0, keepdims=True)
            probs = (weights * inverse).astype(BF16)
            total_ref[low : row + ROWS] += dot(probs, g_ref[row : row + ROWS, lanes], PLAIN)
    index_copy.wait()
    pieces = []
    for c in range(half // 256):
        for side in range(2):
            lane = side * (half // 2) + c * 128
            pieces.append(index_ref[:, lane : lane + 128])
    index = jnp.concatenate(pieces, axis=0).astype(F32).astype(BF16)
    parts = out_ref.shape[0]
    part = length // parts
    for p in range(parts):
        out_ref[p, :part] = total_ref[p * part : (p + 1) * part].astype(BF16)
        out_ref[p, part:] = index


def in_hbm(*arrays):
    return [pltpu.with_memory_space_constraint(x, pltpu.HBM) for x in arrays]


def in_vmem(*arrays):
    return [pltpu.with_memory_space_constraint(x, pltpu.VMEM) for x in arrays]


HBM = pl.BlockSpec(memory_space=pltpu.HBM)
VMEM = pl.BlockSpec(memory_space=pltpu.VMEM)
SMEM = pl.BlockSpec(memory_space=pltpu.SMEM)


def value_grads(core, doc_ids, queries, key_states, out_grads, index, parts):
    length = key_states.shape[0]
    part = length // parts
    half = index.shape[1] // 2
    index_rows = half * KEEP // 128
    return pl.pallas_call(
        grads_kernel,
        out_shape=jax.ShapeDtypeStruct((parts, part + index_rows, HEAD_DIM), BF16),
        in_specs=[SMEM] + [HBM] * 5,
        out_specs=VMEM,
        scratch_shapes=[
            pltpu.VMEM(doc_ids.shape, jnp.int32),
            pltpu.VMEM(queries.shape, BF16),
            pltpu.VMEM(key_states.shape, BF16),
            pltpu.VMEM(out_grads.shape, BF16),
            pltpu.VMEM((KEEP, half), jnp.int32),
            pltpu.VMEM((SPAN + ROWS, ROWS), F32),
            pltpu.VMEM((length, HEAD_DIM), F32),
            pltpu.SemaphoreType.DMA((2 + 3 * (length // FETCH),)),
        ],
        compiler_params=pltpu.CompilerParams(vmem_limit_bytes=40 * MIB),
    )(core, *in_hbm(doc_ids, queries, key_states, out_grads, index))


def encode_kernel(core_ref, own_ref, other_ref, hid_own_ref, hid_other_ref, high_ref, low_ref, kept_ref, wave_ref):
    heads = own_ref.shape[0]
    part = other_ref.shape[1]
    both = 2 * part
    quarter = hid_own_ref.shape[1] // 4
    for h in range(heads):
        values = jnp.concatenate([own_ref[h, :part], other_ref[h]], axis=0)
        wave = dot(high_ref[...], values, LAST) + dot(low_ref[...], values, LAST)
        high = wave.astype(BF16)
        wave_ref[h, :, :both] = high
        wave_ref[h, :, both:] = (wave - high.astype(F32)).astype(BF16)
    for c in range(quarter // 128):
        first, second = (
            pl.ds(pl.multiple_of(core_ref[0] * (2 * quarter) + side * quarter + c * 128, 128), 128) for side in range(2)
        )
        rows = [jnp.concatenate([ref[:, first], ref[:, second]], axis=1) for ref in (hid_own_ref, hid_other_ref)]
        rows = jnp.concatenate(rows + rows, axis=0)
        for h in range(heads):
            coeffs = dot(wave_ref[h], rows, PLAIN)
            index = own_ref[h, part + c * 16 : part + (c + 1) * 16].astype(F32).astype(jnp.int32)
            kept = []
            for side in range(2):
                mine = index[side * 8 : side * 8 + 8]
                block, within = mine >> 3, mine & 7
                found = jnp.zeros((8, 128), F32)
                for v in range(HEAD_DIM // 8):
                    piece = coeffs[v * 8 : v * 8 + 8, side * 128 : side * 128 + 128]
                    found = jnp.where(block == v, jnp.take_along_axis(piece, within, axis=0), found)
                kept.append(found)
            kept_ref[h, :, c * 128 : (c + 1) * 128] = jnp.concatenate(kept, axis=0).astype(BF16)


def encode(core, own, other, hid_own, hid_other, high, low):
    heads, part = own.shape[0], other.shape[1]
    return pl.pallas_call(
        encode_kernel,
        out_shape=jax.ShapeDtypeStruct((heads, 2 * KEEP, hid_own.shape[1] // 4), BF16),
        in_specs=[SMEM] + [VMEM] * 6,
        out_specs=VMEM,
        scratch_shapes=[pltpu.VMEM((heads, HEAD_DIM, 4 * part), BF16)],
        compiler_params=pltpu.CompilerParams(vmem_limit_bytes=40 * MIB),
    )(core, *in_vmem(own, other, hid_own, hid_other, high, low))


def spread_kernel(kept_ref, out_ref):
    total = kept_ref[0].astype(F32)
    for n in range(1, kept_ref.shape[0]):
        total += kept_ref[n].astype(F32)
    total = total.astype(BF16)
    for n in range(out_ref.shape[0]):
        out_ref[n] = total


def spread(kept, copies):
    return pl.pallas_call(
        spread_kernel,
        out_shape=jax.ShapeDtypeStruct((copies,) + kept.shape[1:], BF16),
        in_specs=[VMEM],
        out_specs=VMEM,
    )(*in_vmem(kept))


def update_kernel(
    scale,
    core_ref,
    own_ref,
    other_ref,
    index_ref,
    high_ref,
    low_ref,
    momentum_ref,
    weight_ref,
    new_weight_hbm,
    new_momentum_hbm,
    new_weight_ref,
    new_momentum_ref,
    sems,
):
    core = core_ref[0]
    frequency = lax.broadcasted_iota(jnp.int32, (HEAD_DIM, 128), 0).astype(F32).astype(BF16)
    total, quarter = momentum_ref.shape[0], own_ref.shape[1]
    copies = []
    for row in range(0, total, 128):
        rows = slice(row, row + 128)
        lane = row % quarter
        place = (row // quarter) % 2 * KEEP
        half = row // (2 * quarter)
        ours = own_ref[place : place + KEEP, lane : lane + 128]
        theirs = other_ref[place : place + KEEP, lane : lane + 128]
        kept = jnp.where(core == half, ours, theirs) * scale
        kept_high = kept.astype(BF16)
        kept_low = (kept - kept_high.astype(F32)).astype(BF16)
        index = index_ref[:, rows].astype(F32).astype(BF16)
        high = jnp.zeros((HEAD_DIM, 128), BF16)
        low = jnp.zeros((HEAD_DIM, 128), BF16)
        for t in range(KEEP):
            here = frequency == index[t : t + 1]
            high = jnp.where(here, kept_high[t : t + 1], high)
            low = jnp.where(here, kept_low[t : t + 1], low)
        delta = dot(high, high_ref[...], FIRST) + dot(low, high_ref[...], FIRST) + dot(high, low_ref[...], FIRST)
        fresh = momentum_beta * momentum_ref[rows] + delta
        new_momentum_ref[rows] = fresh
        new_weight_ref[rows] = (
            weight_ref[rows].astype(F32) - outer_rate * (delta + momentum_beta * fresh)
        ).astype(BF16)
        if (row + 128) % STORE == 0:
            done = pl.ds(row + 128 - STORE, STORE)
            n = 2 * (row // STORE)
            copies.append(pltpu.make_async_copy(new_momentum_ref.at[done], new_momentum_hbm.at[done], sems.at[n]))
            copies.append(pltpu.make_async_copy(new_weight_ref.at[done], new_weight_hbm.at[done], sems.at[n + 1]))
            copies[-2].start()
            copies[-1].start()
    for copy in copies:
        copy.wait()


def update(scale, core, own, other, index, high, low, momentum, weight):
    return pl.pallas_call(
        functools.partial(update_kernel, scale),
        out_shape=(jax.ShapeDtypeStruct(weight.shape, BF16), jax.ShapeDtypeStruct(momentum.shape, F32)),
        in_specs=[SMEM] + [VMEM] * 7,
        out_specs=(HBM, HBM),
        scratch_shapes=[
            pltpu.VMEM(weight.shape, BF16),
            pltpu.VMEM(momentum.shape, F32),
            pltpu.SemaphoreType.DMA((2 * momentum.shape[0] // STORE,)),
        ],
        compiler_params=pltpu.CompilerParams(vmem_limit_bytes=40 * MIB),
    )(core, *in_vmem(own, other, index, high, low, momentum, weight))


def swap(x):
    return lax.ppermute(x, "core", [(0, 1), (1, 0)])


def local(hidden_rows, queries, key_states, out_grads, doc_ids, value_weight, momentum, keep_index):
    high, low = dct_tables()
    tensor, ring = ("x", "y_lo"), ("z", "y_hi")
    islands = lax.axis_size(ring) * 2
    core = lax.axis_index("core").astype(jnp.int32).reshape(1)
    hid_own = hidden_rows[0]
    hid_other = swap(hid_own)
    part = hid_own.shape[0]
    index = keep_index[:, 0, :].T
    packed = value_grads(core, doc_ids, queries[0], key_states[0], out_grads[0], index, lax.axis_size(tensor))
    packed = lax.all_to_all(packed, tensor, 0, 0, tiled=True)
    other = swap(packed[:, :part])
    kept = encode(core, packed, other, hid_own, hid_other, high, low)
    kept = lax.all_to_all(kept, tensor, 0, 0, tiled=True)
    kept = lax.all_to_all(spread(kept, lax.axis_size(ring)), ring, 0, 0, tiled=True)
    kept = jnp.sum(kept.astype(F32), axis=0)
    return update(inner_rate / islands, core, kept, swap(kept), index, high, low, momentum, value_weight)


def solution(mesh):
    fine = Mesh(mesh.devices.reshape(-1, 2, 2, 4, 2), ("z", "y_hi", "core", "x", "y_lo"))
    island, tensor = ("z", "y_hi", "core"), ("x", "y_lo")
    in_specs = (
        P(island, tensor, None),
        P(island, None, tensor),
        P(island, None, tensor),
        P(island, None, tensor),
        P(island, None),
        P(None, tensor),
        P(None, tensor),
        P(None, tensor, None),
    )
    out_specs = (P(None, tensor), P(None, tensor))
    return jax.shard_map(local, mesh=fine, in_specs=in_specs, out_specs=out_specs, check_vma=False)
```

time: 79.3 us -> 73.5 us (0.927)
  blocking collectives: 35.5 us -> 47.5 us
  waiting for transfers between devices: 9.6 us -> 2.07 us
  starting transfers between devices: 13.3 us -> 8.98 us
  local copies, waits for them, and re-layouts: 4.29 us -> 1.56 us
  other arithmetic: 1.94 us -> 0.08 us
  Pallas kernels: 13.4 us -> 12.2 us
    all_to_all x1 -> x2, blocking collectives: 26.2 us -> 38.8 us  [the longest x1 26.2 us: local(): lax.all_to_all(spread(kept, lax.axis_size(ring)), ring, 0, 0, tiled=True)]
    all_to_all x1 -> x0, waiting for transfers between devices: 7.53 us -> none  [local(): packed = lax.all_to_all(packed, tensor, 0, 0, tiled=True)]
    all_to_all x1 -> x0, starting transfers between devices: 5.99 us -> none  [local(): packed = lax.all_to_all(packed, tensor, 0, 0, tiled=True)]
    unnamed x20 -> x16, local copies, waits for them, and re-layouts: 4.11 us -> 1.54 us
    ppermute x3, starting transfers between devices: 7.27 us -> 8.98 us  [swap(): return lax.ppermute(x, 'core', [(0, 1), (1, 0)])]
    pallas_call x1, Pallas kernels: 4.16 us -> 2.7 us  [encode(): pl.pallas_call(encode_kernel, out_shape=jax.ShapeDtypeStruct((heads, 2 *...]
    reduce_sum x2 -> x1, other arithmetic: 1.07 us -> 0.08 us  [local(): kept = jnp.sum(kept.astype(F32), axis=0)]
    another operation x1 -> x0, other arithmetic: 0.85 us -> none
  transfers between devices with their start and end apart: 4 -> 3, of which waited for: 3 -> 2; matrix products, arithmetic and copies ran while one was open for 0% -> 0% of each run, Pallas kernels for 0% -> 8%
where the time goes in v2:
time: 73.5 us; the launch traced here: 73.1 us
  blocking collectives  47.5 us (65%)
  Pallas kernels  12.2 us (17%)
  starting transfers between devices  8.98 us (12%)
  waiting for transfers between devices  2.07 us (3%)
  local copies, waits for them, and re-layouts  1.56 us (2%)
    all_to_all x1, blocking collectives, local(): lax.all_to_all(spread(kept, lax.axis_size(ring)), ring, 0, 0, tiled=True)  26.2 us
    all_to_all x1, blocking collectives, local(): packed = lax.all_to_all(packed, tensor, 0, 0, tiled=True)  12.7 us
    ppermute x3, starting transfers between devices, swap(): return lax.ppermute(x, 'core', [(0, 1), (1, 0)])  8.98 us
    all_to_all x1, blocking collectives, local(): kept = lax.all_to_all(kept, tensor, 0, 0, tiled=True)  8.68 us
    pallas_call x1, Pallas kernels, value_grads(): pl.pallas_call(grads_kernel, out_shape=jax.ShapeDtypeStruct((parts, part...  5.62 us
    pallas_call x1, Pallas kernels, update(): pl.pallas_call(functools.partial(update_kernel, scale), out_shape=(jax.Sh...  3.04 us
    pallas_call x1, Pallas kernels, encode(): pl.pallas_call(encode_kernel, out_shape=jax.ShapeDtypeStruct((heads, 2 *...  2.7 us
    ppermute x3, waiting for transfers between devices, swap(): return lax.ppermute(x, 'core', [(0, 1), (1, 0)])  2.07 us
  transfers between devices with their start and end apart: 3, of which 2 were waited for; matrix products, arithmetic and copies ran while one was open for 0% of the time, Pallas kernels for 8%

profile of v2, /device:TPU:1, one launch (start us, length us, event | category | flops | bytes accessed | tf_op | source)
XLA Modules:
  0.0 73.1 jit_solution(14626504957879780627)
XLA Ops:
  0.6 3.3 %collective-permute-start.1 = (bf16[128,4096]{1,0:T(8,128)(2,1)}, bf16[128,4096]{1,0:T(8,128)(2,1)S(1)}, u32[]{:S(2)}, u32[]{:S(2)}) collective-permute-start(bf16[128,4096]{1,0:T(8,128)(2,1)} %bitcast.8), channel_id=1, source_target_pairs={{0,8},{8,0},{1,9},{9,1},{2,10},{10,2},{3,11},{11,3},{4,12},{12,4},... | collective-permute-start | bytes 3145736 | tf_op jit(solution)/shard_map/ppermute | solution.py:284
  4.0 0.0 copy-start.1
  4.0 0.0 copy-start.4
  4.0 0.0 copy-start.6
  4.0 5.6 %shard_map.113 = bf16[8,256,128]{2,1,0:T(8,128)(2,1)S(1)} custom-call(s32[1]{0:T(128)} %bitcast.core_ref, s32[1,1024]{1,0:T(1,128)} %doc_hbm.1, bf16[1024,512]{1,0:T(8,128)(2,1)} %bitcast.12, bf16[1024,128]{1,0:T(8,128)(2,1)} %bitcast.14, bf16[1024,512]{1,0:T(8,128)(2,1)} %bitcast.13, s32[8,4096]{1,0:T(8,128)} %bitcast.10), custom_call_target="tpu_custom_call" | custom-call | tf_op jit(solution)/shard_map/pallas_call | solution.py:133
  9.6 12.7 %all_to_all.15.own_ref = bf16[8,256,128]{2,1,0:T(8,128)(2,1)S(1)} all-to-all(bf16[8,256,128]{2,1,0:T(8,128)(2,1)S(1)} %shard_map.113), channel_id=1, replica_groups=mesh['z'=8,'y_hi'=2,'core'=2,'x'=4,'y_lo'=2] {'x','y_lo'}, dimensions={0} | all-to-all | bytes 1048576 | tf_op jit(solution)/shard_map/all_to_all | solution.py:297
  22.3 1.2 %collective-permute-start = (bf16[8,128,128]{2,1,0:T(8,128)(2,1)S(1)}, bf16[8,128,128]{2,1,0:T(8,128)(2,1)S(1)}, u32[]{:S(2)}, u32[]{:S(2)}) collective-permute-start(bf16[8,128,128]{2,1,0:T(8,128)(2,1)S(1)} %slice.4), channel_id=1, source_target_pairs={{0,8},{8,0},{1,9},{9,1},{2,10},{10,2},{3,11},{11,3},{4,12},{12,4},... | collective-permute-start | bytes 786440 | tf_op jit(solution)/shard_map/ppermute | solution.py:284
  23.5 1.2 %collective-permute-done.other_ref = bf16[8,128,128]{2,1,0:T(8,128)(2,1)S(1)} collective-permute-done((bf16[8,128,128]{2,1,0:T(8,128)(2,1)S(1)}, bf16[8,128,128]{2,1,0:T(8,128)(2,1)S(1)}, u32[]{:S(2)}, u32[]{:S(2)}) %collective-permute-start) | collective-permute-done | bytes 262176 | tf_op jit(solution)/shard_map/ppermute | solution.py:284
  24.6 0.0 collective-permute-done.1.hid_other_ref
  24.6 0.0 copy-done.1
  24.6 0.0 copy-done.4
  24.6 0.0 copy-done.6
  24.7 0.0 copy-start.2
  24.7 2.7 %shard_map.114 = bf16[8,16,1024]{2,1,0:T(8,128)(2,1)S(1)} custom-call(s32[1]{0:T(128)} %bitcast.core_ref, bf16[8,256,128]{2,1,0:T(8,128)(2,1)S(1)} %all_to_all.15.own_ref, bf16[8,128,128]{2,1,0:T(8,128)(2,1)S(1)} %collective-permute-done.other_ref, bf16[128,4096]{1,0:T(8,128)(2,1)S(1)} %bitcast.9, ...), custom_call_target="tpu_custom_call" | custom-call | tf_op jit(solution)/shard_map/pallas_call | solution.py:186
  27.4 0.0 copy-start
  27.4 0.0 copy-start.3
  27.4 8.7 %all_to_all.16.kept_ref = bf16[8,16,1024]{2,1,0:T(8,128)(2,1)S(1)} all-to-all(bf16[8,16,1024]{2,1,0:T(8,128)(2,1)S(1)} %shard_map.114), channel_id=1, replica_groups=mesh['z'=8,'y_hi'=2,'core'=2,'x'=4,'y_lo'=2] {'x','y_lo'}, dimensions={0} | all-to-all | bytes 524288 | tf_op jit(solution)/shard_map/all_to_all | solution.py:300
  36.1 0.9 %shard_map.115 = bf16[16,16,1024]{2,1,0:T(8,128)(2,1)} custom-call(bf16[8,16,1024]{2,1,0:T(8,128)(2,1)S(1)} %all_to_all.16.kept_ref), custom_call_target="tpu_custom_call" | custom-call | tf_op jit(solution)/shard_map/pallas_call | solution.py:206
  36.9 26.2 %all_to_all.17 = bf16[16,16,1024]{2,1,0:T(8,128)(2,1)S(1)} all-to-all(bf16[16,16,1024]{2,1,0:T(8,128)(2,1)} %shard_map.115), channel_id=1, replica_groups=mesh['z'=8,'y_hi'=2,'core'=2,'x'=4,'y_lo'=2] {'z','y_hi'}, dimensions={0} | all-to-all | bytes 1048576 | tf_op jit(solution)/shard_map/all_to_all | solution.py:301
  63.1 0.1 convert_reduce_fusion.own_ref
  63.2 4.5 %collective-permute-start.2 = (f32[16,1024]{1,0:T(8,128)S(1)}, f32[16,1024]{1,0:T(8,128)S(1)}, u32[]{:S(2)}, u32[]{:S(2)}) collective-permute-start(f32[16,1024]{1,0:T(8,128)S(1)} %convert_reduce_fusion.own_ref), channel_id=1, source_target_pairs={{0,8},{8,0},{1,9},{9,1},{2,10},{10,2},{3,11},{11,3},{4,12},{12,4},... | collective-permute-start | bytes 196616 | tf_op jit(solution)/shard_map/ppermute | solution.py:284
  67.7 0.9 %collective-permute-done.2.other_ref = f32[16,1024]{1,0:T(8,128)S(1)} collective-permute-done((f32[16,1024]{1,0:T(8,128)S(1)}, f32[16,1024]{1,0:T(8,128)S(1)}, u32[]{:S(2)}, u32[]{:S(2)}) %collective-permute-start.2) | collective-permute-done | bytes 65568 | tf_op jit(solution)/shard_map/ppermute | solution.py:284
  68.6 0.0 copy-done.2
  68.6 0.0 copy-done
  68.6 0.0 copy-done.3
  68.6 0.0 copy-start.5
  68.6 0.8 %copy-done.5 = bf16[128,128]{1,0:T(8,128)(2,1)S(1)} copy-done((bf16[128,128]{1,0:T(8,128)(2,1)S(1)}, bf16[128,128]{1,0:T(8,128)(2,1)}, u32[]{:S(2)}) %copy-start.5) | copy-done | bytes 32792
  69.3 0.0 copy-start.7
  69.3 0.8 %copy-done.7 = bf16[128,128]{1,0:T(8,128)(2,1)S(1)} copy-done((bf16[128,128]{1,0:T(8,128)(2,1)S(1)}, bf16[128,128]{1,0:T(8,128)(2,1)}, u32[]{:S(2)}) %copy-start.7) | copy-done | bytes 32792
  70.1 3.0 %shard_map.116 = (bf16[4096,128]{1,0:T(8,128)(2,1)}, f32[4096,128]{1,0:T(8,128)}) custom-call(s32[1]{0:T(128)} %bitcast.core_ref, f32[16,1024]{1,0:T(8,128)S(1)} %convert_reduce_fusion.own_ref, f32[16,1024]{1,0:T(8,128)S(1)} %collective-permute-done.2.other_ref, s32[8,4096]{1,0:T(8,128)S(1)} %bitcast.11, bf16[128,128]{1,0:T(8,128)(2,1)S(1)} %copy-done.7, ...), custom_call_target="tpu_custom_call" | custom-call | tf_op jit(solution)/shard_map/pallas_call | solution.py:269
  (1 shorter events, 0.0 us)
Async XLA Ops:
  0.6 24.0 %collective-permute-start.1 = (bf16[128,4096]{1,0:T(8,128)(2,1)}, bf16[128,4096]{1,0:T(8,128)(2,1)S(1)}, u32[]{:S(2)}, u32[]{:S(2)}) collective-permute-start(bf16[128,4096]{1,0:T(8,128)(2,1)} %bitcast.8), channel_id=1, source_target_pairs={{0,8},{8,0},{1,9},{9,1},{2,10},{10,2},{3,11},{11,3},{4,12},{12,4},... | collective-permute-start | bytes 3145736 | tf_op jit(solution)/shard_map/ppermute | solution.py:284
  4.0 20.7 %copy-start.1 = (bf16[1,128,4096]{2,1,0:T(8,128)(2,1)S(1)}, bf16[1,128,4096]{2,1,0:T(8,128)(2,1)}, u32[]{:S(2)}) copy-start(bf16[1,128,4096]{2,1,0:T(8,128)(2,1)} %param.10) | copy-start | bytes 3145732
  4.0 20.7 %copy-start.4 = (bf16[128,128]{1,0:T(8,128)(2,1)S(1)}, bf16[128,128]{1,0:T(8,128)(2,1)}, u32[]{:S(2)}) copy-start(bf16[128,128]{1,0:T(8,128)(2,1)} %constant.13.clone.low_ref) | copy-start | bytes 98308
  4.0 20.7 %copy-start.6 = (bf16[128,128]{1,0:T(8,128)(2,1)S(1)}, bf16[128,128]{1,0:T(8,128)(2,1)}, u32[]{:S(2)}) copy-start(bf16[128,128]{1,0:T(8,128)(2,1)} %constant.12.clone.high_ref) | copy-start | bytes 98308
  22.3 2.4 %collective-permute-start = (bf16[8,128,128]{2,1,0:T(8,128)(2,1)S(1)}, bf16[8,128,128]{2,1,0:T(8,128)(2,1)S(1)}, u32[]{:S(2)}, u32[]{:S(2)}) collective-permute-start(bf16[8,128,128]{2,1,0:T(8,128)(2,1)S(1)} %slice.4), channel_id=1, source_target_pairs={{0,8},{8,0},{1,9},{9,1},{2,10},{10,2},{3,11},{11,3},{4,12},{12,4},... | collective-permute-start | bytes 786440 | tf_op jit(solution)/shard_map/ppermute | solution.py:284
  24.7 43.9 %copy-start.2 = (bf16[4096,128]{1,0:T(8,128)(2,1)S(1)}, bf16[4096,128]{1,0:T(8,128)(2,1)}, u32[]{:S(2)}) copy-start(bf16[4096,128]{1,0:T(8,128)(2,1)} %weight_ref.1) | copy-start | bytes 3145732
  27.4 41.2 %copy-start = (f32[4096,128]{1,0:T(8,128)S(1)}, f32[4096,128]{1,0:T(8,128)}, u32[]{:S(2)}) copy-start(f32[4096,128]{1,0:T(8,128)} %momentum_ref.1) | copy-start | bytes 6291460
  27.4 41.2 %copy-start.3 = (s32[4096,1,8]{0,2,1:T(8,128)S(1)}, s32[4096,1,8]{0,2,1:T(8,128)}, u32[]{:S(2)}) copy-start(s32[4096,1,8]{0,2,1:T(8,128)} %param.17) | copy-start | bytes 393220
  63.2 5.4 %collective-permute-start.2 = (f32[16,1024]{1,0:T(8,128)S(1)}, f32[16,1024]{1,0:T(8,128)S(1)}, u32[]{:S(2)}, u32[]{:S(2)}) collective-permute-start(f32[16,1024]{1,0:T(8,128)S(1)} %convert_reduce_fusion.own_ref), channel_id=1, source_target_pairs={{0,8},{8,0},{1,9},{9,1},{2,10},{10,2},{3,11},{11,3},{4,12},{12,4},... | collective-permute-start | bytes 196616 | tf_op jit(solution)/shard_map/ppermute | solution.py:284
  68.6 0.8 %copy-start.5 = (bf16[128,128]{1,0:T(8,128)(2,1)S(1)}, bf16[128,128]{1,0:T(8,128)(2,1)}, u32[]{:S(2)}) copy-start(bf16[128,128]{1,0:T(8,128)(2,1)} %constant.13.clone.low_ref) | copy-start | bytes 98308
  69.3 0.8 %copy-start.7 = (bf16[128,128]{1,0:T(8,128)(2,1)S(1)}, bf16[128,128]{1,0:T(8,128)(2,1)}, u32[]{:S(2)}) copy-start(bf16[128,128]{1,0:T(8,128)(2,1)} %constant.12.clone.high_ref) | copy-start | bytes 98308

commit v3 on v2

--- a/solution.py
+++ b/solution.py
@@ -14,7 +14,6 @@
 KEEP = 8
 SPAN = 512
 ROWS = 128
-FETCH = 256
 STORE = 512
 
 inner_rate = 0.01
@@ -42,7 +41,7 @@
     table = basis * np.where(frequency == 0.0, math.sqrt(1.0 / HEAD_DIM), math.sqrt(2.0 / HEAD_DIM))
     high = table.astype(jnp.bfloat16)
     low = (table - high.astype(np.float64)).astype(jnp.bfloat16)
-    return high, low
+    return np.concatenate([high, low])
 
 
 def grads_kernel(
@@ -51,37 +50,31 @@
     length = k_ref.shape[0]
     group = q_ref.shape[1] // HEAD_DIM
     half = index_ref.shape[1]
-    count = length // FETCH
-
-    def fetch(source, target, sem):
-        copy = pltpu.make_async_copy(source, target, sems.at[sem])
+    at = pl.multiple_of(core_ref[0] * half, 128)
+    copies = [
+        pltpu.make_async_copy(source, target, sems.at[n])
+        for n, (source, target) in enumerate(
+            (
+                (doc_hbm, doc_ref),
+                (k_hbm, k_ref),
+                (q_hbm, q_ref),
+                (g_hbm, g_ref),
+                (index_hbm.at[:, pl.ds(at, half)], index_ref),
+            )
+        )
+    ]
+    for copy in copies:
         copy.start()
-        return copy
-
-    doc_copy = fetch(doc_hbm, doc_ref, 0)
-    copies = []
-    for b in range(count):
-        rows = pl.ds(b * FETCH, FETCH)
-        copies.append(
-            [
-                fetch(source.at[rows], target.at[rows], 2 + 3 * b + n)
-                for n, (source, target) in enumerate(((k_hbm, k_ref), (q_hbm, q_ref), (g_hbm, g_ref)))
-            ]
-        )
-    at = pl.multiple_of(core_ref[0] * half, 128)
-    index_copy = fetch(index_hbm.at[:, pl.ds(at, half)], index_ref, 1)
-
     total_ref[...] = jnp.zeros_like(total_ref)
-    doc_copy.wait()
+    copies[0].wait()
     docs = doc_ref[...]
     first = jnp.zeros_like(docs)
     for ident in (1, 2, 3):
         before = jnp.sum((docs < ident).astype(jnp.int32), axis=1, keepdims=True)
         first = jnp.where(docs == ident, before, first)
+    for copy in copies[1:]:
+        copy.wait()
     for row in range(0, length, ROWS):
-        if row % FETCH == 0:
-            for copy in copies[row // FETCH]:
-                copy.wait()
         low = max(0, row - SPAN)
         width = row + ROWS - low
         start = first[:, row : row + ROWS]
@@ -98,12 +91,13 @@
             inverse = 1.0 / jnp.sum(weights, axis=0, keepdims=True)
             probs = (weights * inverse).astype(BF16)
             total_ref[low : row + ROWS] += dot(probs, g_ref[row : row + ROWS, lanes], PLAIN)
-    index_copy.wait()
+    section = half // 4
     pieces = []
-    for c in range(half // 256):
-        for side in range(2):
-            lane = side * (half // 2) + c * 128
-            pieces.append(index_ref[:, lane : lane + 128])
+    for quarter in range(2):
+        for c in range(section // 128):
+            for side in range(2):
+                lane = (2 * quarter + side) * section + c * 128
+                pieces.append(index_ref[:, lane : lane + 128])
     index = jnp.concatenate(pieces, axis=0).astype(F32).astype(BF16)
     parts = out_ref.shape[0]
     part = length // parts
@@ -143,32 +137,37 @@
             pltpu.VMEM((KEEP, half), jnp.int32),
             pltpu.VMEM((SPAN + ROWS, ROWS), F32),
             pltpu.VMEM((length, HEAD_DIM), F32),
-            pltpu.SemaphoreType.DMA((2 + 3 * (length // FETCH),)),
+            pltpu.SemaphoreType.DMA((5,)),
         ],
         compiler_params=pltpu.CompilerParams(vmem_limit_bytes=40 * MIB),
     )(core, *in_hbm(doc_ids, queries, key_states, out_grads, index))
 
 
-def encode_kernel(core_ref, own_ref, other_ref, hid_own_ref, hid_other_ref, high_ref, low_ref, kept_ref, wave_ref):
+def encode_kernel(
+    core_ref, own_ref, other_ref, hid_own_ref, hid_other_ref, table_ref, kept_ref, table_out_ref, wave_ref
+):
+    table_out_ref[...] = table_ref[...]
     heads = own_ref.shape[0]
     part = other_ref.shape[1]
     both = 2 * part
-    quarter = hid_own_ref.shape[1] // 4
+    half = hid_own_ref.shape[1] // 2
+    section = half // 4
+    chunks = section // 128
     for h in range(heads):
         values = jnp.concatenate([own_ref[h, :part], other_ref[h]], axis=0)
-        wave = dot(high_ref[...], values, LAST) + dot(low_ref[...], values, LAST)
+        wave = dot(table_ref[:HEAD_DIM], values, LAST) + dot(table_ref[HEAD_DIM:], values, LAST)
         high = wave.astype(BF16)
         wave_ref[h, :, :both] = high
         wave_ref[h, :, both:] = (wave - high.astype(F32)).astype(BF16)
-    for c in range(quarter // 128):
-        first, second = (
-            pl.ds(pl.multiple_of(core_ref[0] * (2 * quarter) + side * quarter + c * 128, 128), 128) for side in range(2)
-        )
+    for n in range(2 * chunks):
+        quarter, c = divmod(n, chunks)
+        at = core_ref[0] * half + quarter * (2 * section) + c * 128
+        first, second = (pl.ds(pl.multiple_of(at + side * section, 128), 128) for side in range(2))
         rows = [jnp.concatenate([ref[:, first], ref[:, second]], axis=1) for ref in (hid_own_ref, hid_other_ref)]
         rows = jnp.concatenate(rows + rows, axis=0)
         for h in range(heads):
             coeffs = dot(wave_ref[h], rows, PLAIN)
-            index = own_ref[h, part + c * 16 : part + (c + 1) * 16].astype(F32).astype(jnp.int32)
+            index = own_ref[h, part + n * 16 : part + (n + 1) * 16].astype(F32).astype(jnp.int32)
             kept = []
             for side in range(2):
                 mine = index[side * 8 : side * 8 + 8]
@@ -178,37 +177,27 @@
                     piece = coeffs[v * 8 : v * 8 + 8, side * 128 : side * 128 + 128]
                     found = jnp.where(block == v, jnp.take_along_axis(piece, within, axis=0), found)
                 kept.append(found)
-            kept_ref[h, :, c * 128 : (c + 1) * 128] = jnp.concatenate(kept, axis=0).astype(BF16)
-
-
-def encode(core, own, other, hid_own, hid_other, high, low):
+            kept_ref[quarter, h, :, c * 128 : (c + 1) * 128] = jnp.concatenate(kept, axis=0).astype(BF16)
+
+
+def encode(core, own, other, hid_own, hid_other, table):
     heads, part = own.shape[0], other.shape[1]
     return pl.pallas_call(
         encode_kernel,
-        out_shape=jax.ShapeDtypeStruct((heads, 2 * KEEP, hid_own.shape[1] // 4), BF16),
-        in_specs=[SMEM] + [VMEM] * 6,
-        out_specs=VMEM,
+        out_shape=(
+            jax.ShapeDtypeStruct((2, heads, 2 * KEEP, hid_own.shape[1] // 8), BF16),
+            jax.ShapeDtypeStruct(table.shape, BF16),
+        ),
+        in_specs=[SMEM] + [VMEM] * 5,
+        out_specs=(VMEM, VMEM),
         scratch_shapes=[pltpu.VMEM((heads, HEAD_DIM, 4 * part), BF16)],
         compiler_params=pltpu.CompilerParams(vmem_limit_bytes=40 * MIB),
-    )(core, *in_vmem(own, other, hid_own, hid_other, high, low))
-
-
-def spread_kernel(kept_ref, out_ref):
-    total = kept_ref[0].astype(F32)
-    for n in range(1, kept_ref.shape[0]):
-        total += kept_ref[n].astype(F32)
-    total = total.astype(BF16)
-    for n in range(out_ref.shape[0]):
-        out_ref[n] = total
+    )(core, *in_vmem(own, other, hid_own, hid_other, table))
 
 
 def spread(kept, copies):
-    return pl.pallas_call(
-        spread_kernel,
-        out_shape=jax.ShapeDtypeStruct((copies,) + kept.shape[1:], BF16),
-        in_specs=[VMEM],
-        out_specs=VMEM,
-    )(*in_vmem(kept))
+    total = jnp.sum(kept.astype(F32), axis=0).astype(BF16)
+    return jnp.broadcast_to(total[None], (copies,) + total.shape)
 
 
 def update_kernel(
@@ -217,8 +206,7 @@
     own_ref,
     other_ref,
     index_ref,
-    high_ref,
-    low_ref,
+    table_ref,
     momentum_ref,
     weight_ref,
     new_weight_hbm,
@@ -229,15 +217,17 @@
 ):
     core = core_ref[0]
     frequency = lax.broadcasted_iota(jnp.int32, (HEAD_DIM, 128), 0).astype(F32).astype(BF16)
-    total, quarter = momentum_ref.shape[0], own_ref.shape[1]
+    high_table, low_table = table_ref[:HEAD_DIM], table_ref[HEAD_DIM:]
+    total, section = momentum_ref.shape[0], own_ref.shape[2]
     copies = []
     for row in range(0, total, 128):
         rows = slice(row, row + 128)
-        lane = row % quarter
-        place = (row // quarter) % 2 * KEEP
-        half = row // (2 * quarter)
-        ours = own_ref[place : place + KEEP, lane : lane + 128]
-        theirs = other_ref[place : place + KEEP, lane : lane + 128]
+        lane = row % section
+        place = row // section % 2 * KEEP
+        quarter = row // (2 * section) % 2
+        half = row // (4 * section)
+        ours = own_ref[quarter, place : place + KEEP, lane : lane + 128]
+        theirs = other_ref[quarter, place : place + KEEP, lane : lane + 128]
         kept = jnp.where(core == half, ours, theirs) * scale
         kept_high = kept.astype(BF16)
         kept_low = (kept - kept_high.astype(F32)).astype(BF16)
@@ -248,7 +238,7 @@
             here = frequency == index[t : t + 1]
             high = jnp.where(here, kept_high[t : t + 1], high)
             low = jnp.where(here, kept_low[t : t + 1], low)
-        delta = dot(high, high_ref[...], FIRST) + dot(low, high_ref[...], FIRST) + dot(high, low_ref[...], FIRST)
+        delta = dot(high, high_table, FIRST) + dot(low, high_table, FIRST) + dot(high, low_table, FIRST)
         fresh = momentum_beta * momentum_ref[rows] + delta
         new_momentum_ref[rows] = fresh
         new_weight_ref[rows] = (
@@ -265,11 +255,11 @@
         copy.wait()
 
 
-def update(scale, core, own, other, index, high, low, momentum, weight):
+def update(scale, core, own, other, index, table, momentum, weight):
     return pl.pallas_call(
         functools.partial(update_kernel, scale),
         out_shape=(jax.ShapeDtypeStruct(weight.shape, BF16), jax.ShapeDtypeStruct(momentum.shape, F32)),
-        in_specs=[SMEM] + [VMEM] * 7,
+        in_specs=[SMEM] + [VMEM] * 6,
         out_specs=(HBM, HBM),
         scratch_shapes=[
             pltpu.VMEM(weight.shape, BF16),
@@ -277,7 +267,7 @@
             pltpu.SemaphoreType.DMA((2 * momentum.shape[0] // STORE,)),
         ],
         compiler_params=pltpu.CompilerParams(vmem_limit_bytes=40 * MIB),
-    )(core, *in_vmem(own, other, index, high, low, momentum, weight))
+    )(core, *in_vmem(own, other, index, table, momentum, weight))
 
 
 def swap(x):
@@ -285,8 +275,7 @@
 
 
 def local(hidden_rows, queries, key_states, out_grads, doc_ids, value_weight, momentum, keep_index):
-    high, low = dct_tables()
-    tensor, ring = ("x", "y_lo"), ("z", "y_hi")
+    tensor, plane, ring = ("x", "y_lo"), ("y_hi", "x", "y_lo"), ("z", "y_hi")
     islands = lax.axis_size(ring) * 2
     core = lax.axis_index("core").astype(jnp.int32).reshape(1)
     hid_own = hidden_rows[0]
@@ -296,11 +285,12 @@
     packed = value_grads(core, doc_ids, queries[0], key_states[0], out_grads[0], index, lax.axis_size(tensor))
     packed = lax.all_to_all(packed, tensor, 0, 0, tiled=True)
     other = swap(packed[:, :part])
-    kept = encode(core, packed, other, hid_own, hid_other, high, low)
-    kept = lax.all_to_all(kept, tensor, 0, 0, tiled=True)
+    kept, table = encode(core, packed, other, hid_own, hid_other, dct_tables())
+    kept = kept.reshape((-1,) + kept.shape[2:])
+    kept = lax.all_to_all(kept, plane, 0, 0, tiled=True)
     kept = lax.all_to_all(spread(kept, lax.axis_size(ring)), ring, 0, 0, tiled=True)
-    kept = jnp.sum(kept.astype(F32), axis=0)
-    return update(inner_rate / islands, core, kept, swap(kept), index, high, low, momentum, value_weight)
+    kept = jnp.sum(kept.reshape((lax.axis_size("z"), -1) + kept.shape[1:]).astype(F32), axis=0)
+    return update(inner_rate / islands, core, kept, swap(kept), index, table, momentum, value_weight)
 
 
 def solution(mesh):

time: 73.5 us -> 68.4 us (0.931)
  blocking collectives: 47.5 us -> 45.1 us
  Pallas kernels: 12.2 us -> 10.8 us
  starting transfers between devices: 8.98 us -> 8.1 us
    all_to_all x1, blocking collectives: 26.2 us -> 20.3 us  [local(): lax.all_to_all(spread(kept, lax.axis_size(ring)), ring, 0, 0, tiled=True)]
    all_to_all x1, blocking collectives: 8.68 us -> 12.1 us  [local(): kept = lax.all_to_all(kept, plane, 0, 0, tiled=True)]
    ppermute x3, starting transfers between devices: 8.98 us -> 8.1 us  [swap(): return lax.ppermute(x, 'core', [(0, 1), (1, 0)])]
    pallas_call x2 -> x1, Pallas kernels: 3.56 us -> 2.69 us  [encode(): pl.pallas_call(encode_kernel, out_shape=(jax.ShapeDtypeStruct((2, heads,...]
    unnamed x16 -> x10, local copies, waits for them, and re-layouts: 1.54 us -> 1.25 us
  transfers between devices with their start and end apart: 3 -> 3, of which waited for: 2 -> 2; matrix products, arithmetic and copies ran while one was open for 0% -> 0% of each run, Pallas kernels for 8% -> 7%
where the time goes in v3:
time: 68.4 us; the launch traced here: 68.1 us
  blocking collectives  45.1 us (66%)
  Pallas kernels  10.8 us (16%)
  starting transfers between devices  8.1 us (12%)
  waiting for transfers between devices  2.07 us (3%)
  local copies, waits for them, and re-layouts  1.28 us (2%)
    all_to_all x1, blocking collectives, local(): lax.all_to_all(spread(kept, lax.axis_size(ring)), ring, 0, 0, tiled=True)  20.3 us
    all_to_all x1, blocking collectives, local(): packed = lax.all_to_all(packed, tensor, 0, 0, tiled=True)  12.7 us
    all_to_all x1, blocking collectives, local(): kept = lax.all_to_all(kept, plane, 0, 0, tiled=True)  12.1 us
    ppermute x3, starting transfers between devices, swap(): return lax.ppermute(x, 'core', [(0, 1), (1, 0)])  8.1 us
    pallas_call x1, Pallas kernels, value_grads(): pl.pallas_call(grads_kernel, out_shape=jax.ShapeDtypeStruct((parts, part...  5.01 us
    pallas_call x1, Pallas kernels, update(): pl.pallas_call(functools.partial(update_kernel, scale), out_shape=(jax.Sh...  3.06 us
    pallas_call x1, Pallas kernels, encode(): pl.pallas_call(encode_kernel, out_shape=(jax.ShapeDtypeStruct((2, heads,...  2.69 us
    ppermute x3, waiting for transfers between devices, swap(): return lax.ppermute(x, 'core', [(0, 1), (1, 0)])  2.07 us
  transfers between devices with their start and end apart: 3, of which 2 were waited for; matrix products, arithmetic and copies ran while one was open for 0% of the time, Pallas kernels for 7%

profile of v3, /device:TPU:1, one launch (start us, length us, event | category | flops | bytes accessed | tf_op | source)
XLA Modules:
  0.0 68.1 jit_solution(547140588932816157)
XLA Ops:
  0.6 3.3 %collective-permute-start.1 = (bf16[128,4096]{1,0:T(8,128)(2,1)}, bf16[128,4096]{1,0:T(8,128)(2,1)S(1)}, u32[]{:S(2)}, u32[]{:S(2)}) collective-permute-start(bf16[128,4096]{1,0:T(8,128)(2,1)} %bitcast.11), channel_id=1, source_target_pairs={{0,8},{8,0},{1,9},{9,1},{2,10},{10,2},{3,11},{11,3},{4,12},{12,4},... | collective-permute-start | bytes 3145736 | tf_op jit(solution)/shard_map/ppermute | solution.py:274
  4.0 0.0 copy-start.1
  4.0 0.0 copy-start.4
  4.0 5.0 %shard_map.104 = bf16[8,256,128]{2,1,0:T(8,128)(2,1)S(1)} custom-call(s32[1]{0:T(128)} %bitcast.core_ref, s32[1,1024]{1,0:T(1,128)} %doc_hbm.1, bf16[1024,512]{1,0:T(8,128)(2,1)} %bitcast.17, bf16[1024,128]{1,0:T(8,128)(2,1)} %bitcast.19, bf16[1024,512]{1,0:T(8,128)(2,1)} %bitcast.18, s32[8,4096]{1,0:T(8,128)} %bitcast.13), custom_call_target="tpu_custom_call" | custom-call | tf_op jit(solution)/shard_map/pallas_call | solution.py:127
  9.0 12.7 %all_to_all.15.own_ref = bf16[8,256,128]{2,1,0:T(8,128)(2,1)S(1)} all-to-all(bf16[8,256,128]{2,1,0:T(8,128)(2,1)S(1)} %shard_map.104), channel_id=1, replica_groups=mesh['z'=8,'y_hi'=2,'core'=2,'x'=4,'y_lo'=2] {'x','y_lo'}, dimensions={0} | all-to-all | bytes 1048576 | tf_op jit(solution)/shard_map/all_to_all | solution.py:286
  21.7 0.0 copy-start
  21.7 0.0 copy-start.3
  21.7 1.2 %collective-permute-start = (bf16[8,128,128]{2,1,0:T(8,128)(2,1)S(1)}, bf16[8,128,128]{2,1,0:T(8,128)(2,1)S(1)}, u32[]{:S(2)}, u32[]{:S(2)}) collective-permute-start(bf16[8,128,128]{2,1,0:T(8,128)(2,1)S(1)} %slice.4), channel_id=1, source_target_pairs={{0,8},{8,0},{1,9},{9,1},{2,10},{10,2},{3,11},{11,3},{4,12},{12,4},... | collective-permute-start | bytes 786440 | tf_op jit(solution)/shard_map/ppermute | solution.py:274
  22.9 1.2 %collective-permute-done.other_ref = bf16[8,128,128]{2,1,0:T(8,128)(2,1)S(1)} collective-permute-done((bf16[8,128,128]{2,1,0:T(8,128)(2,1)S(1)}, bf16[8,128,128]{2,1,0:T(8,128)(2,1)S(1)}, u32[]{:S(2)}, u32[]{:S(2)}) %collective-permute-start) | collective-permute-done | bytes 262176 | tf_op jit(solution)/shard_map/ppermute | solution.py:274
  24.1 0.0 collective-permute-done.1.hid_other_ref
  24.1 0.0 copy-done.1
  24.1 0.0 copy-done.4
  24.1 2.7 %shard_map.105 = (bf16[2,8,16,512]{3,2,1,0:T(8,128)(2,1)S(1)}, bf16[256,128]{1,0:T(8,128)(2,1)S(1)}) custom-call(s32[1]{0:T(128)} %bitcast.core_ref, bf16[8,256,128]{2,1,0:T(8,128)(2,1)S(1)} %all_to_all.15.own_ref, bf16[8,128,128]{2,1,0:T(8,128)(2,1)S(1)} %collective-permute-done.other_ref, bf16[128,4096]{1,0:T(8,128)(2,1)S(1)} %bitcast.12, ...), custom_call_target="tpu_custom_call" | custom-call | tf_op jit(solution)/shard_map/pallas_call | solution.py:185
  26.8 12.1 %all_to_all.16 = bf16[16,16,512]{2,1,0:T(8,128)(2,1)S(1)} all-to-all(bf16[16,16,512]{2,1,0:T(8,128)(2,1)S(1)} %bitcast.15), channel_id=1, replica_groups=mesh['z'=8,'y_hi'=2,'core'=2,'x'=4,'y_lo'=2] {'y_hi','x','y_lo'}, dimensions={0} | all-to-all | bytes 524288 | tf_op jit(solution)/shard_map/all_to_all | solution.py:290
  39.0 20.3 %all_to_all.17 = bf16[16,16,512]{2,1,0:T(8,128)(2,1)S(1)} all-to-all(bf16[16,16,512]{2,1,0:T(8,128)(2,1)S(1)} %broadcast_in_dim.2), channel_id=1, replica_groups=mesh['z'=8,'y_hi'=2,'core'=2,'x'=4,'y_lo'=2] {'z','y_hi'}, dimensions={0} | all-to-all | bytes 524288 | tf_op jit(solution)/shard_map/all_to_all | solution.py:291
  59.4 3.6 %collective-permute-start.2 = (f32[2,16,512]{2,1,0:T(8,128)S(1)}, f32[2,16,512]{2,1,0:T(8,128)S(1)}, u32[]{:S(2)}, u32[]{:S(2)}) collective-permute-start(f32[2,16,512]{2,1,0:T(8,128)S(1)} %convert_reduce_fusion.own_ref), channel_id=1, source_target_pairs={{0,8},{8,0},{1,9},{9,1},{2,10},{10,2},{3,11},{11,3},{4,12},{12,4},... | collective-permute-start | bytes 196616 | tf_op jit(solution)/shard_map/ppermute | solution.py:274
  62.9 0.9 %collective-permute-done.2.other_ref = f32[2,16,512]{2,1,0:T(8,128)S(1)} collective-permute-done((f32[2,16,512]{2,1,0:T(8,128)S(1)}, f32[2,16,512]{2,1,0:T(8,128)S(1)}, u32[]{:S(2)}, u32[]{:S(2)}) %collective-permute-start.2) | collective-permute-done | bytes 65568 | tf_op jit(solution)/shard_map/ppermute | solution.py:274
  63.8 0.0 copy-done
  63.8 0.0 copy-done.3
  63.8 0.0 copy-start.2
  63.8 1.2 %copy-done.2 = bf16[4096,128]{1,0:T(8,128)(2,1)S(1)} copy-done((bf16[4096,128]{1,0:T(8,128)(2,1)S(1)}, bf16[4096,128]{1,0:T(8,128)(2,1)}, u32[]{:S(2)}) %copy-start.2) | copy-done | bytes 1048600
  65.1 3.1 %shard_map.106 = (bf16[4096,128]{1,0:T(8,128)(2,1)}, f32[4096,128]{1,0:T(8,128)}) custom-call(s32[1]{0:T(128)} %bitcast.core_ref, f32[2,16,512]{2,1,0:T(8,128)S(1)} %convert_reduce_fusion.own_ref, f32[2,16,512]{2,1,0:T(8,128)S(1)} %collective-permute-done.2.other_ref, s32[8,4096]{1,0:T(8,128)S(1)} %bitcast.14, ...), custom_call_target="tpu_custom_call" | custom-call | tf_op jit(solution)/shard_map/pallas_call | solution.py:259
  (4 shorter events, 0.1 us)
Async XLA Ops:
  0.6 23.4 %collective-permute-start.1 = (bf16[128,4096]{1,0:T(8,128)(2,1)}, bf16[128,4096]{1,0:T(8,128)(2,1)S(1)}, u32[]{:S(2)}, u32[]{:S(2)}) collective-permute-start(bf16[128,4096]{1,0:T(8,128)(2,1)} %bitcast.11), channel_id=1, source_target_pairs={{0,8},{8,0},{1,9},{9,1},{2,10},{10,2},{3,11},{11,3},{4,12},{12,4},... | collective-permute-start | bytes 3145736 | tf_op jit(solution)/shard_map/ppermute | solution.py:274
  4.0 20.1 %copy-start.1 = (bf16[1,128,4096]{2,1,0:T(8,128)(2,1)S(1)}, bf16[1,128,4096]{2,1,0:T(8,128)(2,1)}, u32[]{:S(2)}) copy-start(bf16[1,128,4096]{2,1,0:T(8,128)(2,1)} %param.9) | copy-start | bytes 3145732
  4.0 20.1 %copy-start.4 = (bf16[256,128]{1,0:T(8,128)(2,1)S(1)}, bf16[256,128]{1,0:T(8,128)(2,1)}, u32[]{:S(2)}) copy-start(bf16[256,128]{1,0:T(8,128)(2,1)} %constant.12.clone.table_ref) | copy-start | bytes 196612
  21.7 42.2 %copy-start = (f32[4096,128]{1,0:T(8,128)S(1)}, f32[4096,128]{1,0:T(8,128)}, u32[]{:S(2)}) copy-start(f32[4096,128]{1,0:T(8,128)} %momentum_ref.1) | copy-start | bytes 6291460
  21.7 42.2 %copy-start.3 = (s32[4096,1,8]{0,2,1:T(8,128)S(1)}, s32[4096,1,8]{0,2,1:T(8,128)}, u32[]{:S(2)}) copy-start(s32[4096,1,8]{0,2,1:T(8,128)} %param.16) | copy-start | bytes 393220
  21.7 2.4 %collective-permute-start = (bf16[8,128,128]{2,1,0:T(8,128)(2,1)S(1)}, bf16[8,128,128]{2,1,0:T(8,128)(2,1)S(1)}, u32[]{:S(2)}, u32[]{:S(2)}) collective-permute-start(bf16[8,128,128]{2,1,0:T(8,128)(2,1)S(1)} %slice.4), channel_id=1, source_target_pairs={{0,8},{8,0},{1,9},{9,1},{2,10},{10,2},{3,11},{11,3},{4,12},{12,4},... | collective-permute-start | bytes 786440 | tf_op jit(solution)/shard_map/ppermute | solution.py:274
  59.4 4.5 %collective-permute-start.2 = (f32[2,16,512]{2,1,0:T(8,128)S(1)}, f32[2,16,512]{2,1,0:T(8,128)S(1)}, u32[]{:S(2)}, u32[]{:S(2)}) collective-permute-start(f32[2,16,512]{2,1,0:T(8,128)S(1)} %convert_reduce_fusion.own_ref), channel_id=1, source_target_pairs={{0,8},{8,0},{1,9},{9,1},{2,10},{10,2},{3,11},{11,3},{4,12},{12,4},... | collective-permute-start | bytes 196616 | tf_op jit(solution)/shard_map/ppermute | solution.py:274
  63.8 1.2 %copy-start.2 = (bf16[4096,128]{1,0:T(8,128)(2,1)S(1)}, bf16[4096,128]{1,0:T(8,128)(2,1)}, u32[]{:S(2)}) copy-start(bf16[4096,128]{1,0:T(8,128)(2,1)} %weight_ref.1) | copy-start | bytes 3145732

commit v4 on v3

--- a/solution.py
+++ b/solution.py
@@ -72,8 +72,8 @@
     for ident in (1, 2, 3):
         before = jnp.sum((docs < ident).astype(jnp.int32), axis=1, keepdims=True)
         first = jnp.where(docs == ident, before, first)
-    for copy in copies[1:]:
-        copy.wait()
+    copies[1].wait()
+    copies[2].wait()
     for row in range(0, length, ROWS):
         low = max(0, row - SPAN)
         width = row + ROWS - low
@@ -90,7 +90,10 @@
             weights = jnp.exp2((scores - peak) * exp2_scale)
             inverse = 1.0 / jnp.sum(weights, axis=0, keepdims=True)
             probs = (weights * inverse).astype(BF16)
+            if row == 0 and head == 0:
+                copies[3].wait()
             total_ref[low : row + ROWS] += dot(probs, g_ref[row : row + ROWS, lanes], PLAIN)
+    copies[4].wait()
     section = half // 4
     pieces = []
     for quarter in range(2):
@@ -144,27 +147,37 @@
 
 
 def encode_kernel(
-    core_ref, own_ref, other_ref, hid_own_ref, hid_other_ref, table_ref, kept_ref, table_out_ref, wave_ref
+    core_ref,
+    own_ref,
+    other_ref,
+    hid_own_ref,
+    hid_other_ref,
+    table_ref,
+    weight_hbm,
+    kept_ref,
+    table_out_ref,
+    weight_ref,
+    wave_ref,
+    sems,
 ):
+    copy = pltpu.make_async_copy(weight_hbm, weight_ref, sems.at[0])
+    copy.start()
     table_out_ref[...] = table_ref[...]
     heads = own_ref.shape[0]
     part = other_ref.shape[1]
-    both = 2 * part
     half = hid_own_ref.shape[1] // 2
     section = half // 4
     chunks = section // 128
     for h in range(heads):
         values = jnp.concatenate([own_ref[h, :part], other_ref[h]], axis=0)
         wave = dot(table_ref[:HEAD_DIM], values, LAST) + dot(table_ref[HEAD_DIM:], values, LAST)
-        high = wave.astype(BF16)
-        wave_ref[h, :, :both] = high
-        wave_ref[h, :, both:] = (wave - high.astype(F32)).astype(BF16)
+        wave_ref[h] = wave.astype(BF16)
     for n in range(2 * chunks):
         quarter, c = divmod(n, chunks)
         at = core_ref[0] * half + quarter * (2 * section) + c * 128
         first, second = (pl.ds(pl.multiple_of(at + side * section, 128), 128) for side in range(2))
         rows = [jnp.concatenate([ref[:, first], ref[:, second]], axis=1) for ref in (hid_own_ref, hid_other_ref)]
-        rows = jnp.concatenate(rows + rows, axis=0)
+        rows = jnp.concatenate(rows, axis=0)
         for h in range(heads):
             coeffs = dot(wave_ref[h], rows, PLAIN)
             index = own_ref[h, part + n * 16 : part + (n + 1) * 16].astype(F32).astype(jnp.int32)
@@ -178,21 +191,23 @@
                     found = jnp.where(block == v, jnp.take_along_axis(piece, within, axis=0), found)
                 kept.append(found)
             kept_ref[quarter, h, :, c * 128 : (c + 1) * 128] = jnp.concatenate(kept, axis=0).astype(BF16)
-
-
-def encode(core, own, other, hid_own, hid_other, table):
+    copy.wait()
+
+
+def encode(core, own, other, hid_own, hid_other, table, weight):
     heads, part = own.shape[0], other.shape[1]
     return pl.pallas_call(
         encode_kernel,
         out_shape=(
             jax.ShapeDtypeStruct((2, heads, 2 * KEEP, hid_own.shape[1] // 8), BF16),
             jax.ShapeDtypeStruct(table.shape, BF16),
+            jax.ShapeDtypeStruct(weight.shape, BF16),
         ),
-        in_specs=[SMEM] + [VMEM] * 5,
-        out_specs=(VMEM, VMEM),
-        scratch_shapes=[pltpu.VMEM((heads, HEAD_DIM, 4 * part), BF16)],
+        in_specs=[SMEM] + [VMEM] * 5 + [HBM],
+        out_specs=(VMEM, VMEM, VMEM),
+        scratch_shapes=[pltpu.VMEM((heads, HEAD_DIM, 2 * part), BF16), pltpu.SemaphoreType.DMA((1,))],
         compiler_params=pltpu.CompilerParams(vmem_limit_bytes=40 * MIB),
-    )(core, *in_vmem(own, other, hid_own, hid_other, table))
+    )(core, *in_vmem(own, other, hid_own, hid_other, table), *in_hbm(weight))
 
 
 def spread(kept, copies):
@@ -200,38 +215,22 @@
     return jnp.broadcast_to(total[None], (copies,) + total.shape)
 
 
-def update_kernel(
-    scale,
-    core_ref,
-    own_ref,
-    other_ref,
-    index_ref,
-    table_ref,
-    momentum_ref,
-    weight_ref,
-    new_weight_hbm,
-    new_momentum_hbm,
-    new_weight_ref,
-    new_momentum_ref,
-    sems,
-):
-    core = core_ref[0]
+def update_kernel(scale, half_ref, kept_ref, index_ref, table_ref, momentum_ref, weight_ref, *rest):
+    new_weight_hbm, new_momentum_hbm, new_weight_ref, new_momentum_ref, sems = rest[-5:]
     frequency = lax.broadcasted_iota(jnp.int32, (HEAD_DIM, 128), 0).astype(F32).astype(BF16)
     high_table, low_table = table_ref[:HEAD_DIM], table_ref[HEAD_DIM:]
-    total, section = momentum_ref.shape[0], own_ref.shape[2]
+    total, section = new_weight_ref.shape[0], kept_ref.shape[2]
+    base = half_ref[0] * total
     copies = []
     for row in range(0, total, 128):
         rows = slice(row, row + 128)
+        there = pl.ds(pl.multiple_of(base + row, 128), 128)
         lane = row % section
         place = row // section % 2 * KEEP
-        quarter = row // (2 * section) % 2
-        half = row // (4 * section)
-        ours = own_ref[quarter, place : place + KEEP, lane : lane + 128]
-        theirs = other_ref[quarter, place : place + KEEP, lane : lane + 128]
-        kept = jnp.where(core == half, ours, theirs) * scale
+        kept = kept_ref[row // (2 * section), place : place + KEEP, lane : lane + 128] * scale
         kept_high = kept.astype(BF16)
         kept_low = (kept - kept_high.astype(F32)).astype(BF16)
-        index = index_ref[:, rows].astype(F32).astype(BF16)
+        index = index_ref[:, there].astype(F32).astype(BF16)
         high = jnp.zeros((HEAD_DIM, 128), BF16)
         low = jnp.zeros((HEAD_DIM, 128), BF16)
         for t in range(KEEP):
@@ -239,35 +238,38 @@
             high = jnp.where(here, kept_high[t : t + 1], high)
             low = jnp.where(here, kept_low[t : t + 1], low)
         delta = dot(high, high_table, FIRST) + dot(low, high_table, FIRST) + dot(high, low_table, FIRST)
-        fresh = momentum_beta * momentum_ref[rows] + delta
+        fresh = momentum_beta * momentum_ref[there] + delta
         new_momentum_ref[rows] = fresh
         new_weight_ref[rows] = (
-            weight_ref[rows].astype(F32) - outer_rate * (delta + momentum_beta * fresh)
+            weight_ref[there].astype(F32) - outer_rate * (delta + momentum_beta * fresh)
         ).astype(BF16)
         if (row + 128) % STORE == 0:
             done = pl.ds(row + 128 - STORE, STORE)
+            target = pl.ds(pl.multiple_of(base + row + 128 - STORE, STORE), STORE)
             n = 2 * (row // STORE)
-            copies.append(pltpu.make_async_copy(new_momentum_ref.at[done], new_momentum_hbm.at[done], sems.at[n]))
-            copies.append(pltpu.make_async_copy(new_weight_ref.at[done], new_weight_hbm.at[done], sems.at[n + 1]))
+            copies.append(pltpu.make_async_copy(new_momentum_ref.at[done], new_momentum_hbm.at[target], sems.at[n]))
+            copies.append(pltpu.make_async_copy(new_weight_ref.at[done], new_weight_hbm.at[target], sems.at[n + 1]))
             copies[-2].start()
             copies[-1].start()
     for copy in copies:
         copy.wait()
 
 
-def update(scale, core, own, other, index, table, momentum, weight):
+def update(scale, half, kept, index, table, momentum, weight, before=()):
+    rows = momentum.shape[0] // 2
     return pl.pallas_call(
         functools.partial(update_kernel, scale),
         out_shape=(jax.ShapeDtypeStruct(weight.shape, BF16), jax.ShapeDtypeStruct(momentum.shape, F32)),
-        in_specs=[SMEM] + [VMEM] * 6,
+        in_specs=[SMEM] + [VMEM] * 5 + [HBM] * len(before),
         out_specs=(HBM, HBM),
         scratch_shapes=[
-            pltpu.VMEM(weight.shape, BF16),
-            pltpu.VMEM(momentum.shape, F32),
-            pltpu.SemaphoreType.DMA((2 * momentum.shape[0] // STORE,)),
+            pltpu.VMEM((rows, HEAD_DIM), BF16),
+            pltpu.VMEM((rows, HEAD_DIM), F32),
+            pltpu.SemaphoreType.DMA((2 * rows // STORE,)),
         ],
+        input_output_aliases={6 + n: n for n in range(len(before))},
         compiler_params=pltpu.CompilerParams(vmem_limit_bytes=40 * MIB),
-    )(core, *in_vmem(own, other, index, table, momentum, weight))
+    )(half, *in_vmem(kept, index, table, momentum, weight), *in_hbm(*before))
 
 
 def swap(x):
@@ -285,12 +287,14 @@
     packed = value_grads(core, doc_ids, queries[0], key_states[0], out_grads[0], index, lax.axis_size(tensor))
     packed = lax.all_to_all(packed, tensor, 0, 0, tiled=True)
     other = swap(packed[:, :part])
-    kept, table = encode(core, packed, other, hid_own, hid_other, dct_tables())
+    kept, table, weight = encode(core, packed, other, hid_own, hid_other, dct_tables(), value_weight)
     kept = kept.reshape((-1,) + kept.shape[2:])
     kept = lax.all_to_all(kept, plane, 0, 0, tiled=True)
     kept = lax.all_to_all(spread(kept, lax.axis_size(ring)), ring, 0, 0, tiled=True)
     kept = jnp.sum(kept.reshape((lax.axis_size("z"), -1) + kept.shape[1:]).astype(F32), axis=0)
-    return update(inner_rate / islands, core, kept, swap(kept), index, table, momentum, value_weight)
+    operands = (index, table, momentum, weight)
+    before = update(inner_rate / islands, core, kept, *operands)
+    return update(inner_rate / islands, 1 - core, swap(kept), *operands, before)
 
 
 def solution(mesh):

time: 68.4 us -> 70 us (1.023)
  local copies, waits for them, and re-layouts: 1.28 us -> 2.25 us
  other arithmetic: 0.08 us -> 1.03 us
  waiting for transfers between devices: 2.07 us -> 1.17 us
    unnamed x10 -> x12, local copies, waits for them, and re-layouts: 1.25 us -> 2.22 us
    reduce_sum x1, other arithmetic: 0.04 us -> 0.99 us  [spread(): total = jnp.sum(kept.astype(F32), axis=0).astype(BF16)]
    ppermute x3, waiting for transfers between devices: 2.07 us -> 1.17 us  [swap(): return lax.ppermute(x, 'core', [(0, 1), (1, 0)])]
    pallas_call x1 -> x2, Pallas kernels: 3.06 us -> 3.78 us  [update(): pl.pallas_call(functools.partial(update_kernel, scale), out_shape=(jax.Sh...]
  transfers between devices with their start and end apart: 3 -> 3, of which waited for: 2 -> 1; matrix products, arithmetic and copies ran while one was open for 0% -> 0% of each run, Pallas kernels for 7% -> 10%
where the time goes in v4:
time: 70 us; the launch traced here: 69.7 us
  blocking collectives  45.2 us (65%)
  Pallas kernels  11.2 us (16%)
  starting transfers between devices  8.1 us (12%)
  local copies, waits for them, and re-layouts  2.25 us (3%)
  waiting for transfers between devices  1.17 us (2%)
  other arithmetic  1.03 us (1%)
    all_to_all x1, blocking collectives, local(): lax.all_to_all(spread(kept, lax.axis_size(ring)), ring, 0, 0, tiled=True)  20.3 us
    all_to_all x1, blocking collectives, local(): packed = lax.all_to_all(packed, tensor, 0, 0, tiled=True)  12.7 us
    all_to_all x1, blocking collectives, local(): kept = lax.all_to_all(kept, plane, 0, 0, tiled=True)  12.2 us
    ppermute x3, starting transfers between devices, swap(): return lax.ppermute(x, 'core', [(0, 1), (1, 0)])  8.1 us
    pallas_call x1, Pallas kernels, value_grads(): pl.pallas_call(grads_kernel, out_shape=jax.ShapeDtypeStruct((parts, part...  4.9 us
    pallas_call x2, Pallas kernels, update(): pl.pallas_call(functools.partial(update_kernel, scale), out_shape=(jax.Sh...  3.78 us
    pallas_call x1, Pallas kernels, encode(): pl.pallas_call(encode_kernel, out_shape=(jax.ShapeDtypeStruct((2, heads,...  2.55 us
    unnamed x12, local copies, waits for them, and re-layouts  2.22 us
  transfers between devices with their start and end apart: 3, of which 1 were waited for; matrix products, arithmetic and copies ran while one was open for 0% of the time, Pallas kernels for 10%

profile of v4, /device:TPU:1, one launch (start us, length us, event | category | flops | bytes accessed | tf_op | source)
XLA Modules:
  0.0 69.7 jit_solution(8888944527983595657)
XLA Ops:
  0.6 3.3 %collective-permute-start.1 = (bf16[128,4096]{1,0:T(8,128)(2,1)}, bf16[128,4096]{1,0:T(8,128)(2,1)S(1)}, u32[]{:S(2)}, u32[]{:S(2)}) collective-permute-start(bf16[128,4096]{1,0:T(8,128)(2,1)} %bitcast.14), channel_id=1, source_target_pairs={{0,8},{8,0},{1,9},{9,1},{2,10},{10,2},{3,11},{11,3},{4,12},{12,4},... | collective-permute-start | bytes 3145736 | tf_op jit(solution)/shard_map/ppermute | solution.py:276
  4.0 0.0 copy-start.2
  4.0 0.0 copy-start.5
  4.0 4.9 %shard_map.104 = bf16[8,256,128]{2,1,0:T(8,128)(2,1)S(1)} custom-call(s32[1]{0:T(128)} %bitcast.core_ref.half_ref, s32[1,1024]{1,0:T(1,128)} %doc_hbm.1, bf16[1024,512]{1,0:T(8,128)(2,1)} %bitcast.18, bf16[1024,128]{1,0:T(8,128)(2,1)} %bitcast.20, bf16[1024,512]{1,0:T(8,128)(2,1)} %bitcast.19, s32[8,4096]{1,0:T(8,128)} %bitcast.11), custom_call_target="tpu_custom_call" | custom-call | tf_op jit(solution)/shard_map/pallas_call | solution.py:130
  8.9 12.7 %all_to_all.15.own_ref = bf16[8,256,128]{2,1,0:T(8,128)(2,1)S(1)} all-to-all(bf16[8,256,128]{2,1,0:T(8,128)(2,1)S(1)} %shard_map.104), channel_id=1, replica_groups=mesh['z'=8,'y_hi'=2,'core'=2,'x'=4,'y_lo'=2] {'x','y_lo'}, dimensions={0} | all-to-all | bytes 1048576 | tf_op jit(solution)/shard_map/all_to_all | solution.py:288
  21.6 0.0 copy-start
  21.6 0.0 copy-start.1
  21.6 1.2 %collective-permute-start = (bf16[8,128,128]{2,1,0:T(8,128)(2,1)S(1)}, bf16[8,128,128]{2,1,0:T(8,128)(2,1)S(1)}, u32[]{:S(2)}, u32[]{:S(2)}) collective-permute-start(bf16[8,128,128]{2,1,0:T(8,128)(2,1)S(1)} %slice.4), channel_id=1, source_target_pairs={{0,8},{8,0},{1,9},{9,1},{2,10},{10,2},{3,11},{11,3},{4,12},{12,4},... | collective-permute-start | bytes 786440 | tf_op jit(solution)/shard_map/ppermute | solution.py:276
  22.8 1.2 %collective-permute-done.other_ref = bf16[8,128,128]{2,1,0:T(8,128)(2,1)S(1)} collective-permute-done((bf16[8,128,128]{2,1,0:T(8,128)(2,1)S(1)}, bf16[8,128,128]{2,1,0:T(8,128)(2,1)S(1)}, u32[]{:S(2)}, u32[]{:S(2)}) %collective-permute-start) | collective-permute-done | bytes 262176 | tf_op jit(solution)/shard_map/ppermute | solution.py:276
  23.9 0.0 collective-permute-done.1.hid_other_ref
  23.9 0.0 copy-start.3
  24.0 1.0 %copy-done.3 = bf16[128,4096]{1,0:T(8,128)(2,1)} copy-done((bf16[128,4096]{1,0:T(8,128)(2,1)}, bf16[128,4096]{1,0:T(8,128)(2,1)S(1)}, u32[]{:S(2)}) %copy-start.3) | copy-done | bytes 1048600
  24.9 0.0 copy-done.2
  24.9 0.0 copy-done.5
  24.9 0.0 copy-start.4
  24.9 1.2 %copy-done.4 = bf16[128,4096]{1,0:T(8,128)(2,1)S(1)} copy-done((bf16[128,4096]{1,0:T(8,128)(2,1)S(1)}, bf16[128,4096]{1,0:T(8,128)(2,1)}, u32[]{:S(2)}) %copy-start.4) | copy-done | bytes 1048600
  26.2 2.5 %shard_map.105 = (bf16[2,8,16,512]{3,2,1,0:T(8,128)(2,1)S(1)}, bf16[256,128]{1,0:T(8,128)(2,1)S(1)}, bf16[4096,128]{1,0:T(8,128)(2,1)S(1)}) custom-call(s32[1]{0:T(128)} %bitcast.core_ref.half_ref, bf16[8,256,128]{2,1,0:T(8,128)(2,1)S(1)} %all_to_all.15.own_ref, bf16[8,128,128]{2,1,0:T(8,128)(2,1)S(1)} %collective-permute-done.other_ref, ...), custom_call_target="tpu_custom_call" | custom-call | tf_op jit(solution)/shard_map/pallas_call | solution.py:199
  28.7 12.2 %all_to_all.16 = bf16[16,16,512]{2,1,0:T(8,128)(2,1)} all-to-all(bf16[16,16,512]{2,1,0:T(8,128)(2,1)S(1)} %bitcast.16), channel_id=1, replica_groups=mesh['z'=8,'y_hi'=2,'core'=2,'x'=4,'y_lo'=2] {'y_hi','x','y_lo'}, dimensions={0} | all-to-all | bytes 524288 | tf_op jit(solution)/shard_map/all_to_all | solution.py:292
  40.9 1.0 %reduce_sum.21 = bf16[16,512]{1,0:T(8,128)(2,1)S(1)} reduce(bf16[16,16,512]{2,1,0:T(8,128)(2,1)} %all_to_all.16, bf16[]{:T(256)} %constant.12.clone.1), dimensions={0}, to_apply=%region_0.0 | reduce | flops 122880 | bytes 278530 | tf_op jit(solution)/shard_map/reduce_sum | solution.py:214
  42.0 20.3 %all_to_all.17 = bf16[16,16,512]{2,1,0:T(8,128)(2,1)S(1)} all-to-all(bf16[16,16,512]{2,1,0:T(8,128)(2,1)S(1)} %broadcast_in_dim.2), channel_id=1, replica_groups=mesh['z'=8,'y_hi'=2,'core'=2,'x'=4,'y_lo'=2] {'z','y_hi'}, dimensions={0} | all-to-all | bytes 524288 | tf_op jit(solution)/shard_map/all_to_all | solution.py:293
  62.3 3.6 %collective-permute-start.2 = (f32[2,16,512]{2,1,0:T(8,128)S(1)}, f32[2,16,512]{2,1,0:T(8,128)S(1)}, u32[]{:S(2)}, u32[]{:S(2)}) collective-permute-start(f32[2,16,512]{2,1,0:T(8,128)S(1)} %convert_reduce_fusion.kept_ref), channel_id=1, source_target_pairs={{0,8},{8,0},{1,9},{9,1},{2,10},{10,2},{3,11},{11,3},{4,12},{12,4},... | collective-permute-start | bytes 196616 | tf_op jit(solution)/shard_map/ppermute | solution.py:276
  65.9 0.0 copy-done
  65.9 0.0 copy-done.1
  65.9 1.9 %shard_map.106 = (bf16[4096,128]{1,0:T(8,128)(2,1)}, f32[4096,128]{1,0:T(8,128)}) custom-call(s32[1]{0:T(128)} %bitcast.core_ref.half_ref, f32[2,16,512]{2,1,0:T(8,128)S(1)} %convert_reduce_fusion.kept_ref, s32[8,4096]{1,0:T(8,128)S(1)} %bitcast.12, bf16[256,128]{1,0:T(8,128)(2,1)S(1)} %get-tuple-element.8.table_ref, f32[4096,128]{1,0:T(8,128)S(1)} %copy-done, ...), custom_call_target="tpu_custom_call" | custom-call | tf_op jit(solution)/shard_map/pallas_call | solution.py:260
  67.8 0.0 collective-permute-done.2.kept_ref
  67.8 1.9 %shard_map.107 = (bf16[4096,128]{1,0:T(8,128)(2,1)}, f32[4096,128]{1,0:T(8,128)}) custom-call(s32[1]{0:T(128)S(6)} %sub.3.half_ref, f32[2,16,512]{2,1,0:T(8,128)S(1)} %collective-permute-done.2.kept_ref, s32[8,4096]{1,0:T(8,128)S(1)} %bitcast.13, bf16[256,128]{1,0:T(8,128)(2,1)S(1)} %get-tuple-element.8.table_ref, ...), custom_call_target="tpu_custom_call", output_to_operand_aliasing={{0}: (6, {}), {1}: (7, {})} | custom-call | tf_op jit(solution)/shard_map/pallas_call | solution.py:260
  (3 shorter events, 0.1 us)
Async XLA Ops:
  0.6 23.3 %collective-permute-start.1 = (bf16[128,4096]{1,0:T(8,128)(2,1)}, bf16[128,4096]{1,0:T(8,128)(2,1)S(1)}, u32[]{:S(2)}, u32[]{:S(2)}) collective-permute-start(bf16[128,4096]{1,0:T(8,128)(2,1)} %bitcast.14), channel_id=1, source_target_pairs={{0,8},{8,0},{1,9},{9,1},{2,10},{10,2},{3,11},{11,3},{4,12},{12,4},... | collective-permute-start | bytes 3145736 | tf_op jit(solution)/shard_map/ppermute | solution.py:276
  4.0 21.0 %copy-start.2 = (bf16[1,128,4096]{2,1,0:T(8,128)(2,1)S(1)}, bf16[1,128,4096]{2,1,0:T(8,128)(2,1)}, u32[]{:S(2)}) copy-start(bf16[1,128,4096]{2,1,0:T(8,128)(2,1)} %param.9) | copy-start | bytes 3145732
  4.0 21.0 %copy-start.5 = (bf16[256,128]{1,0:T(8,128)(2,1)S(1)}, bf16[256,128]{1,0:T(8,128)(2,1)}, u32[]{:S(2)}) copy-start(bf16[256,128]{1,0:T(8,128)(2,1)} %constant.14.clone.table_ref) | copy-start | bytes 196612
  21.6 44.4 %copy-start = (f32[4096,128]{1,0:T(8,128)S(1)}, f32[4096,128]{1,0:T(8,128)}, u32[]{:S(2)}) copy-start(f32[4096,128]{1,0:T(8,128)} %momentum_ref.3) | copy-start | bytes 6291460
  21.6 44.3 %copy-start.1 = (s32[4096,1,8]{0,2,1:T(8,128)S(1)}, s32[4096,1,8]{0,2,1:T(8,128)}, u32[]{:S(2)}) copy-start(s32[4096,1,8]{0,2,1:T(8,128)} %param.16) | copy-start | bytes 393220
  21.6 2.4 %collective-permute-start = (bf16[8,128,128]{2,1,0:T(8,128)(2,1)S(1)}, bf16[8,128,128]{2,1,0:T(8,128)(2,1)S(1)}, u32[]{:S(2)}, u32[]{:S(2)}) collective-permute-start(bf16[8,128,128]{2,1,0:T(8,128)(2,1)S(1)} %slice.4), channel_id=1, source_target_pairs={{0,8},{8,0},{1,9},{9,1},{2,10},{10,2},{3,11},{11,3},{4,12},{12,4},... | collective-permute-start | bytes 786440 | tf_op jit(solution)/shard_map/ppermute | solution.py:276
  23.9 1.0 %copy-start.3 = (bf16[128,4096]{1,0:T(8,128)(2,1)}, bf16[128,4096]{1,0:T(8,128)(2,1)S(1)}, u32[]{:S(2)}) copy-start(bf16[128,4096]{1,0:T(8,128)(2,1)S(1)} %collective-permute-done.1.hid_other_ref) | copy-start | bytes 3145732
  24.9 1.2 %copy-start.4 = (bf16[128,4096]{1,0:T(8,128)(2,1)S(1)}, bf16[128,4096]{1,0:T(8,128)(2,1)}, u32[]{:S(2)}) copy-start(bf16[128,4096]{1,0:T(8,128)(2,1)} %copy-done.3) | copy-start | bytes 3145732
  62.3 5.5 %collective-permute-start.2 = (f32[2,16,512]{2,1,0:T(8,128)S(1)}, f32[2,16,512]{2,1,0:T(8,128)S(1)}, u32[]{:S(2)}, u32[]{:S(2)}) collective-permute-start(f32[2,16,512]{2,1,0:T(8,128)S(1)} %convert_reduce_fusion.kept_ref), channel_id=1, source_target_pairs={{0,8},{8,0},{1,9},{9,1},{2,10},{10,2},{3,11},{11,3},{4,12},{12,4},... | collective-permute-start | bytes 196616 | tf_op jit(solution)/shard_map/ppermute | solution.py:276

commit v5 on v4

--- a/solution.py
+++ b/solution.py
@@ -142,7 +142,7 @@
             pltpu.VMEM((length, HEAD_DIM), F32),
             pltpu.SemaphoreType.DMA((5,)),
         ],
-        compiler_params=pltpu.CompilerParams(vmem_limit_bytes=40 * MIB),
+        compiler_params=pltpu.CompilerParams(vmem_limit_bytes=16 * MIB),
     )(core, *in_hbm(doc_ids, queries, key_states, out_grads, index))
 
 
@@ -153,15 +153,10 @@
     hid_own_ref,
     hid_other_ref,
     table_ref,
-    weight_hbm,
     kept_ref,
     table_out_ref,
-    weight_ref,
     wave_ref,
-    sems,
 ):
-    copy = pltpu.make_async_copy(weight_hbm, weight_ref, sems.at[0])
-    copy.start()
     table_out_ref[...] = table_ref[...]
     heads = own_ref.shape[0]
     part = other_ref.shape[1]
@@ -191,27 +186,25 @@
                     found = jnp.where(block == v, jnp.take_along_axis(piece, within, axis=0), found)
                 kept.append(found)
             kept_ref[quarter, h, :, c * 128 : (c + 1) * 128] = jnp.concatenate(kept, axis=0).astype(BF16)
-    copy.wait()
-
-
-def encode(core, own, other, hid_own, hid_other, table, weight):
+
+
+def encode(core, own, other, hid_own, hid_other, table):
     heads, part = own.shape[0], other.shape[1]
     return pl.pallas_call(
         encode_kernel,
         out_shape=(
             jax.ShapeDtypeStruct((2, heads, 2 * KEEP, hid_own.shape[1] // 8), BF16),
             jax.ShapeDtypeStruct(table.shape, BF16),
-            jax.ShapeDtypeStruct(weight.shape, BF16),
         ),
-        in_specs=[SMEM] + [VMEM] * 5 + [HBM],
-        out_specs=(VMEM, VMEM, VMEM),
-        scratch_shapes=[pltpu.VMEM((heads, HEAD_DIM, 2 * part), BF16), pltpu.SemaphoreType.DMA((1,))],
-        compiler_params=pltpu.CompilerParams(vmem_limit_bytes=40 * MIB),
-    )(core, *in_vmem(own, other, hid_own, hid_other, table), *in_hbm(weight))
+        in_specs=[SMEM] + [VMEM] * 5,
+        out_specs=(VMEM, VMEM),
+        scratch_shapes=[pltpu.VMEM((heads, HEAD_DIM, 2 * part), BF16)],
+        compiler_params=pltpu.CompilerParams(vmem_limit_bytes=16 * MIB),
+    )(core, *in_vmem(own, other, hid_own, hid_other, table))
 
 
 def spread(kept, copies):
-    total = jnp.sum(kept.astype(F32), axis=0).astype(BF16)
+    total = lax.optimization_barrier(jnp.sum(kept.astype(F32), axis=0)).astype(BF16)
     return jnp.broadcast_to(total[None], (copies,) + total.shape)
 
 
@@ -268,7 +261,7 @@
             pltpu.SemaphoreType.DMA((2 * rows // STORE,)),
         ],
         input_output_aliases={6 + n: n for n in range(len(before))},
-        compiler_params=pltpu.CompilerParams(vmem_limit_bytes=40 * MIB),
+        compiler_params=pltpu.CompilerParams(vmem_limit_bytes=16 * MIB),
     )(half, *in_vmem(kept, index, table, momentum, weight), *in_hbm(*before))
 
 
@@ -287,12 +280,12 @@
     packed = value_grads(core, doc_ids, queries[0], key_states[0], out_grads[0], index, lax.axis_size(tensor))
     packed = lax.all_to_all(packed, tensor, 0, 0, tiled=True)
     other = swap(packed[:, :part])
-    kept, table, weight = encode(core, packed, other, hid_own, hid_other, dct_tables(), value_weight)
+    kept, table = encode(core, packed, other, hid_own, hid_other, dct_tables())
     kept = kept.reshape((-1,) + kept.shape[2:])
     kept = lax.all_to_all(kept, plane, 0, 0, tiled=True)
     kept = lax.all_to_all(spread(kept, lax.axis_size(ring)), ring, 0, 0, tiled=True)
     kept = jnp.sum(kept.reshape((lax.axis_size("z"), -1) + kept.shape[1:]).astype(F32), axis=0)
-    operands = (index, table, momentum, weight)
+    operands = (index, table, momentum, value_weight)
     before = update(inner_rate / islands, core, kept, *operands)
     return update(inner_rate / islands, 1 - core, swap(kept), *operands, before)
 

time: 70 us -> 65.7 us (0.939)
  local copies, waits for them, and re-layouts: 2.25 us -> 0.06 us
  other arithmetic: 1.03 us -> 0.08 us
  Pallas kernels: 11.2 us -> 10.3 us
    unnamed x12 -> x10, local copies, waits for them, and re-layouts: 2.22 us -> 0.03 us
    pallas_call x1, Pallas kernels: 2.55 us -> 1.58 us  [encode(): pl.pallas_call(encode_kernel, out_shape=(jax.ShapeDtypeStruct((2, heads,...]
    reduce_sum x1, other arithmetic: 0.99 us -> 0.04 us  [spread(): jnp.sum(kept.astype(F32), axis=0)]
where the time goes in v5:
time: 65.7 us; the launch traced here: 65.5 us
  blocking collectives  45.1 us (69%)
  Pallas kernels  10.3 us (16%)
  starting transfers between devices  8.1 us (12%)
  waiting for transfers between devices  1.17 us (2%)
  between operations  0.71 us (1%)
    all_to_all x1, blocking collectives, local(): lax.all_to_all(spread(kept, lax.axis_size(ring)), ring, 0, 0, tiled=True)  20.3 us
    all_to_all x1, blocking collectives, local(): packed = lax.all_to_all(packed, tensor, 0, 0, tiled=True)  12.7 us
    all_to_all x1, blocking collectives, local(): kept = lax.all_to_all(kept, plane, 0, 0, tiled=True)  12.1 us
    ppermute x3, starting transfers between devices, swap(): return lax.ppermute(x, 'core', [(0, 1), (1, 0)])  8.1 us
    pallas_call x1, Pallas kernels, value_grads(): pl.pallas_call(grads_kernel, out_shape=jax.ShapeDtypeStruct((parts, part...  4.9 us
    pallas_call x2, Pallas kernels, update(): pl.pallas_call(functools.partial(update_kernel, scale), out_shape=(jax.Sh...  3.79 us
    pallas_call x1, Pallas kernels, encode(): pl.pallas_call(encode_kernel, out_shape=(jax.ShapeDtypeStruct((2, heads,...  1.58 us
  transfers between devices with their start and end apart: 3, of which 1 were waited for; matrix products, arithmetic and copies ran while one was open for 0% of the time, Pallas kernels for 10%

profile of v5, /device:TPU:1, one launch (start us, length us, event | category | flops | bytes accessed | tf_op | source)
XLA Modules:
  0.0 65.5 jit_solution(9293200774448657813)
XLA Ops:
  0.6 3.3 %collective-permute-start.1 = (bf16[128,4096]{1,0:T(8,128)(2,1)}, bf16[128,4096]{1,0:T(8,128)(2,1)S(1)}, u32[]{:S(2)}, u32[]{:S(2)}) collective-permute-start(bf16[128,4096]{1,0:T(8,128)(2,1)} %bitcast.14), channel_id=1, source_target_pairs={{0,8},{8,0},{1,9},{9,1},{2,10},{10,2},{3,11},{11,3},{4,12},{12,4},... | collective-permute-start | bytes 3145736 | tf_op jit(solution)/shard_map/ppermute | solution.py:269
  4.0 0.0 copy-start.3
  4.0 0.0 copy-start.4
  4.0 4.9 %shard_map.104 = bf16[8,256,128]{2,1,0:T(8,128)(2,1)S(1)} custom-call(s32[1]{0:T(128)} %bitcast.core_ref.half_ref, s32[1,1024]{1,0:T(1,128)} %doc_hbm.1, bf16[1024,512]{1,0:T(8,128)(2,1)} %bitcast.18, bf16[1024,128]{1,0:T(8,128)(2,1)} %bitcast.20, bf16[1024,512]{1,0:T(8,128)(2,1)} %bitcast.19, s32[8,4096]{1,0:T(8,128)} %bitcast.11), custom_call_target="tpu_custom_call" | custom-call | tf_op jit(solution)/shard_map/pallas_call | solution.py:130
  8.9 12.7 %all_to_all.15.own_ref = bf16[8,256,128]{2,1,0:T(8,128)(2,1)S(1)} all-to-all(bf16[8,256,128]{2,1,0:T(8,128)(2,1)S(1)} %shard_map.104), channel_id=1, replica_groups=mesh['z'=8,'y_hi'=2,'core'=2,'x'=4,'y_lo'=2] {'x','y_lo'}, dimensions={0} | all-to-all | bytes 1048576 | tf_op jit(solution)/shard_map/all_to_all | solution.py:281
  21.6 0.0 copy-start
  21.6 0.0 copy-start.1
  21.6 0.0 copy-start.2
  21.6 1.2 %collective-permute-start = (bf16[8,128,128]{2,1,0:T(8,128)(2,1)S(1)}, bf16[8,128,128]{2,1,0:T(8,128)(2,1)S(1)}, u32[]{:S(2)}, u32[]{:S(2)}) collective-permute-start(bf16[8,128,128]{2,1,0:T(8,128)(2,1)S(1)} %slice.4), channel_id=1, source_target_pairs={{0,8},{8,0},{1,9},{9,1},{2,10},{10,2},{3,11},{11,3},{4,12},{12,4},... | collective-permute-start | bytes 786440 | tf_op jit(solution)/shard_map/ppermute | solution.py:269
  22.8 1.2 %collective-permute-done.other_ref = bf16[8,128,128]{2,1,0:T(8,128)(2,1)S(1)} collective-permute-done((bf16[8,128,128]{2,1,0:T(8,128)(2,1)S(1)}, bf16[8,128,128]{2,1,0:T(8,128)(2,1)S(1)}, u32[]{:S(2)}, u32[]{:S(2)}) %collective-permute-start) | collective-permute-done | bytes 262176 | tf_op jit(solution)/shard_map/ppermute | solution.py:269
  24.0 0.0 collective-permute-done.1.hid_other_ref
  24.0 0.0 copy-done.3
  24.0 0.0 copy-done.4
  24.0 1.6 %shard_map.105 = (bf16[2,8,16,512]{3,2,1,0:T(8,128)(2,1)S(1)}, bf16[256,128]{1,0:T(8,128)(2,1)S(1)}) custom-call(s32[1]{0:T(128)} %bitcast.core_ref.half_ref, bf16[8,256,128]{2,1,0:T(8,128)(2,1)S(1)} %all_to_all.15.own_ref, bf16[8,128,128]{2,1,0:T(8,128)(2,1)S(1)} %collective-permute-done.other_ref, bf16[128,4096]{1,0:T(8,128)(2,1)S(1)} %bitcast.15, ...), custom_call_target="tpu_custom_call" | custom-call | tf_op jit(solution)/shard_map/pallas_call | solution.py:193
  25.6 12.1 %all_to_all.16 = bf16[16,16,512]{2,1,0:T(8,128)(2,1)S(1)} all-to-all(bf16[16,16,512]{2,1,0:T(8,128)(2,1)S(1)} %bitcast.16), channel_id=1, replica_groups=mesh['z'=8,'y_hi'=2,'core'=2,'x'=4,'y_lo'=2] {'y_hi','x','y_lo'}, dimensions={0} | all-to-all | bytes 524288 | tf_op jit(solution)/shard_map/all_to_all | solution.py:285
  37.8 20.3 %all_to_all.17 = bf16[16,16,512]{2,1,0:T(8,128)(2,1)S(1)} all-to-all(bf16[16,16,512]{2,1,0:T(8,128)(2,1)S(1)} %broadcast_in_dim.2), channel_id=1, replica_groups=mesh['z'=8,'y_hi'=2,'core'=2,'x'=4,'y_lo'=2] {'z','y_hi'}, dimensions={0} | all-to-all | bytes 524288 | tf_op jit(solution)/shard_map/all_to_all | solution.py:286
  58.1 3.6 %collective-permute-start.2 = (f32[2,16,512]{2,1,0:T(8,128)S(1)}, f32[2,16,512]{2,1,0:T(8,128)S(1)}, u32[]{:S(2)}, u32[]{:S(2)}) collective-permute-start(f32[2,16,512]{2,1,0:T(8,128)S(1)} %convert_reduce_fusion.kept_ref), channel_id=1, source_target_pairs={{0,8},{8,0},{1,9},{9,1},{2,10},{10,2},{3,11},{11,3},{4,12},{12,4},... | collective-permute-start | bytes 196616 | tf_op jit(solution)/shard_map/ppermute | solution.py:269
  61.7 0.0 copy-done
  61.7 0.0 copy-done.1
  61.7 0.0 copy-done.2
  61.7 1.9 %shard_map.106 = (bf16[4096,128]{1,0:T(8,128)(2,1)}, f32[4096,128]{1,0:T(8,128)}) custom-call(s32[1]{0:T(128)} %bitcast.core_ref.half_ref, f32[2,16,512]{2,1,0:T(8,128)S(1)} %convert_reduce_fusion.kept_ref, s32[8,4096]{1,0:T(8,128)S(1)} %bitcast.12, bf16[256,128]{1,0:T(8,128)(2,1)S(1)} %get-tuple-element.7.table_ref, f32[4096,128]{1,0:T(8,128)S(1)} %copy-done, ...), custom_call_target="tpu_custom_call" | custom-call | tf_op jit(solution)/shard_map/pallas_call | solution.py:253
  63.6 0.0 collective-permute-done.2.kept_ref
  63.6 1.9 %shard_map.107 = (bf16[4096,128]{1,0:T(8,128)(2,1)}, f32[4096,128]{1,0:T(8,128)}) custom-call(s32[1]{0:T(128)S(6)} %sub.3.half_ref, f32[2,16,512]{2,1,0:T(8,128)S(1)} %collective-permute-done.2.kept_ref, s32[8,4096]{1,0:T(8,128)S(1)} %bitcast.13, bf16[256,128]{1,0:T(8,128)(2,1)S(1)} %get-tuple-element.7.table_ref, ...), custom_call_target="tpu_custom_call", output_to_operand_aliasing={{0}: (6, {}), {1}: (7, {})} | custom-call | tf_op jit(solution)/shard_map/pallas_call | solution.py:253
  (4 shorter events, 0.1 us)
Async XLA Ops:
  0.6 23.3 %collective-permute-start.1 = (bf16[128,4096]{1,0:T(8,128)(2,1)}, bf16[128,4096]{1,0:T(8,128)(2,1)S(1)}, u32[]{:S(2)}, u32[]{:S(2)}) collective-permute-start(bf16[128,4096]{1,0:T(8,128)(2,1)} %bitcast.14), channel_id=1, source_target_pairs={{0,8},{8,0},{1,9},{9,1},{2,10},{10,2},{3,11},{11,3},{4,12},{12,4},... | collective-permute-start | bytes 3145736 | tf_op jit(solution)/shard_map/ppermute | solution.py:269
  4.0 20.0 %copy-start.3 = (bf16[1,128,4096]{2,1,0:T(8,128)(2,1)S(1)}, bf16[1,128,4096]{2,1,0:T(8,128)(2,1)}, u32[]{:S(2)}) copy-start(bf16[1,128,4096]{2,1,0:T(8,128)(2,1)} %param.9) | copy-start | bytes 3145732
  4.0 20.0 %copy-start.4 = (bf16[256,128]{1,0:T(8,128)(2,1)S(1)}, bf16[256,128]{1,0:T(8,128)(2,1)}, u32[]{:S(2)}) copy-start(bf16[256,128]{1,0:T(8,128)(2,1)} %constant.12.clone.table_ref) | copy-start | bytes 196612
  21.6 40.1 %copy-start = (f32[4096,128]{1,0:T(8,128)S(1)}, f32[4096,128]{1,0:T(8,128)}, u32[]{:S(2)}) copy-start(f32[4096,128]{1,0:T(8,128)} %momentum_ref.3) | copy-start | bytes 6291460
  21.6 40.1 %copy-start.1 = (bf16[4096,128]{1,0:T(8,128)(2,1)S(1)}, bf16[4096,128]{1,0:T(8,128)(2,1)}, u32[]{:S(2)}) copy-start(bf16[4096,128]{1,0:T(8,128)(2,1)} %weight_ref.3) | copy-start | bytes 3145732
  21.6 40.1 %copy-start.2 = (s32[4096,1,8]{0,2,1:T(8,128)S(1)}, s32[4096,1,8]{0,2,1:T(8,128)}, u32[]{:S(2)}) copy-start(s32[4096,1,8]{0,2,1:T(8,128)} %param.16) | copy-start | bytes 393220
  21.6 2.4 %collective-permute-start = (bf16[8,128,128]{2,1,0:T(8,128)(2,1)S(1)}, bf16[8,128,128]{2,1,0:T(8,128)(2,1)S(1)}, u32[]{:S(2)}, u32[]{:S(2)}) collective-permute-start(bf16[8,128,128]{2,1,0:T(8,128)(2,1)S(1)} %slice.4), channel_id=1, source_target_pairs={{0,8},{8,0},{1,9},{9,1},{2,10},{10,2},{3,11},{11,3},{4,12},{12,4},... | collective-permute-start | bytes 786440 | tf_op jit(solution)/shard_map/ppermute | solution.py:269
  58.1 5.5 %collective-permute-start.2 = (f32[2,16,512]{2,1,0:T(8,128)S(1)}, f32[2,16,512]{2,1,0:T(8,128)S(1)}, u32[]{:S(2)}, u32[]{:S(2)}) collective-permute-start(f32[2,16,512]{2,1,0:T(8,128)S(1)} %convert_reduce_fusion.kept_ref), channel_id=1, source_target_pairs={{0,8},{8,0},{1,9},{9,1},{2,10},{10,2},{3,11},{11,3},{4,12},{12,4},... | collective-permute-start | bytes 196616 | tf_op jit(solution)/shard_map/ppermute | solution.py:269

commit v6 on v5

--- a/solution.py
+++ b/solution.py
@@ -208,61 +208,89 @@
     return jnp.broadcast_to(total[None], (copies,) + total.shape)
 
 
-def update_kernel(scale, half_ref, kept_ref, index_ref, table_ref, momentum_ref, weight_ref, *rest):
-    new_weight_hbm, new_momentum_hbm, new_weight_ref, new_momentum_ref, sems = rest[-5:]
+def update_rows(scale, base, row, kept_ref, index_ref, table_ref, momentum_ref, weight_ref, new_weight_ref, new_momentum_ref):
     frequency = lax.broadcasted_iota(jnp.int32, (HEAD_DIM, 128), 0).astype(F32).astype(BF16)
     high_table, low_table = table_ref[:HEAD_DIM], table_ref[HEAD_DIM:]
-    total, section = new_weight_ref.shape[0], kept_ref.shape[2]
-    base = half_ref[0] * total
+    section = kept_ref.shape[2]
+    rows = slice(row, row + 128)
+    there = pl.ds(pl.multiple_of(base + row, 128), 128)
+    lane = row % section
+    place = row // section % 2 * KEEP
+    kept = kept_ref[row // (2 * section), place : place + KEEP, lane : lane + 128] * scale
+    kept_high = kept.astype(BF16)
+    kept_low = (kept - kept_high.astype(F32)).astype(BF16)
+    index = index_ref[:, there].astype(F32).astype(BF16)
+    high = jnp.zeros((HEAD_DIM, 128), BF16)
+    low = jnp.zeros((HEAD_DIM, 128), BF16)
+    for t in range(KEEP):
+        here = frequency == index[t : t + 1]
+        high = jnp.where(here, kept_high[t : t + 1], high)
+        low = jnp.where(here, kept_low[t : t + 1], low)
+    delta = dot(high, high_table, FIRST) + dot(low, high_table, FIRST) + dot(high, low_table, FIRST)
+    fresh = momentum_beta * momentum_ref[there] + delta
+    new_momentum_ref[rows] = fresh
+    new_weight_ref[rows] = (
+        weight_ref[there].astype(F32) - outer_rate * (delta + momentum_beta * fresh)
+    ).astype(BF16)
+
+
+def update_first_kernel(scale, half_ref, *refs):
+    total = refs[-1].shape[0]
+    for row in range(0, total, 128):
+        update_rows(scale, half_ref[0] * total, row, *refs)
+
+
+def update_second_kernel(scale, half_ref, *refs):
+    operands = refs[:5]
+    first_weight_ref, first_momentum_ref, weight_hbm, momentum_hbm, new_weight_ref, new_momentum_ref, sems = refs[5:]
+    total = new_weight_ref.shape[0]
+    half = half_ref[0]
     copies = []
+
+    def store(source, target, base, row, count):
+        rows = pl.ds(pl.multiple_of(base + row, STORE), count)
+        copies.append(pltpu.make_async_copy(source.at[pl.ds(row, count)], target.at[rows], sems.at[len(copies)]))
+        copies[-1].start()
+
+    store(first_momentum_ref, momentum_hbm, (1 - half) * total, 0, total)
+    store(first_weight_ref, weight_hbm, (1 - half) * total, 0, total)
     for row in range(0, total, 128):
-        rows = slice(row, row + 128)
-        there = pl.ds(pl.multiple_of(base + row, 128), 128)
-        lane = row % section
-        place = row // section % 2 * KEEP
-        kept = kept_ref[row // (2 * section), place : place + KEEP, lane : lane + 128] * scale
-        kept_high = kept.astype(BF16)
-        kept_low = (kept - kept_high.astype(F32)).astype(BF16)
-        index = index_ref[:, there].astype(F32).astype(BF16)
-        high = jnp.zeros((HEAD_DIM, 128), BF16)
-        low = jnp.zeros((HEAD_DIM, 128), BF16)
-        for t in range(KEEP):
-            here = frequency == index[t : t + 1]
-            high = jnp.where(here, kept_high[t : t + 1], high)
-            low = jnp.where(here, kept_low[t : t + 1], low)
-        delta = dot(high, high_table, FIRST) + dot(low, high_table, FIRST) + dot(high, low_table, FIRST)
-        fresh = momentum_beta * momentum_ref[there] + delta
-        new_momentum_ref[rows] = fresh
-        new_weight_ref[rows] = (
-            weight_ref[there].astype(F32) - outer_rate * (delta + momentum_beta * fresh)
-        ).astype(BF16)
+        update_rows(scale, half * total, row, *operands, new_weight_ref, new_momentum_ref)
         if (row + 128) % STORE == 0:
-            done = pl.ds(row + 128 - STORE, STORE)
-            target = pl.ds(pl.multiple_of(base + row + 128 - STORE, STORE), STORE)
-            n = 2 * (row // STORE)
-            copies.append(pltpu.make_async_copy(new_momentum_ref.at[done], new_momentum_hbm.at[target], sems.at[n]))
-            copies.append(pltpu.make_async_copy(new_weight_ref.at[done], new_weight_hbm.at[target], sems.at[n + 1]))
-            copies[-2].start()
-            copies[-1].start()
+            store(new_momentum_ref, momentum_hbm, half * total, row + 128 - STORE, STORE)
+            store(new_weight_ref, weight_hbm, half * total, row + 128 - STORE, STORE)
     for copy in copies:
         copy.wait()
 
 
-def update(scale, half, kept, index, table, momentum, weight, before=()):
+def update_first(scale, half, kept, index, table, momentum, weight):
     rows = momentum.shape[0] // 2
     return pl.pallas_call(
-        functools.partial(update_kernel, scale),
+        functools.partial(update_first_kernel, scale),
+        out_shape=(
+            jax.ShapeDtypeStruct((rows, HEAD_DIM), BF16),
+            jax.ShapeDtypeStruct((rows, HEAD_DIM), F32),
+        ),
+        in_specs=[SMEM] + [VMEM] * 5,
+        out_specs=(VMEM, VMEM),
+        compiler_params=pltpu.CompilerParams(vmem_limit_bytes=16 * MIB),
+    )(half, *in_vmem(kept, index, table, momentum, weight))
+
+
+def update_second(scale, half, kept, index, table, momentum, weight, first_weight, first_momentum):
+    rows = momentum.shape[0] // 2
+    return pl.pallas_call(
+        functools.partial(update_second_kernel, scale),
         out_shape=(jax.ShapeDtypeStruct(weight.shape, BF16), jax.ShapeDtypeStruct(momentum.shape, F32)),
-        in_specs=[SMEM] + [VMEM] * 5 + [HBM] * len(before),
+        in_specs=[SMEM] + [VMEM] * 7,
         out_specs=(HBM, HBM),
         scratch_shapes=[
             pltpu.VMEM((rows, HEAD_DIM), BF16),
             pltpu.VMEM((rows, HEAD_DIM), F32),
-            pltpu.SemaphoreType.DMA((2 * rows // STORE,)),
+            pltpu.SemaphoreType.DMA((2 + 2 * rows // STORE,)),
         ],
-        input_output_aliases={6 + n: n for n in range(len(before))},
         compiler_params=pltpu.CompilerParams(vmem_limit_bytes=16 * MIB),
-    )(half, *in_vmem(kept, index, table, momentum, weight), *in_hbm(*before))
+    )(half, *in_vmem(kept, index, table, momentum, weight, first_weight, first_momentum))
 
 
 def swap(x):
@@ -270,7 +298,7 @@
 
 
 def local(hidden_rows, queries, key_states, out_grads, doc_ids, value_weight, momentum, keep_index):
-    tensor, plane, ring = ("x", "y_lo"), ("y_hi", "x", "y_lo"), ("z", "y_hi")
+    tensor, near, ring = ("x", "y_lo"), ("z_lo", "x", "y_lo"), ("y_hi", "z_hi", "z_lo")
     islands = lax.axis_size(ring) * 2
     core = lax.axis_index("core").astype(jnp.int32).reshape(1)
     hid_own = hidden_rows[0]
@@ -282,17 +310,17 @@
     other = swap(packed[:, :part])
     kept, table = encode(core, packed, other, hid_own, hid_other, dct_tables())
     kept = kept.reshape((-1,) + kept.shape[2:])
-    kept = lax.all_to_all(kept, plane, 0, 0, tiled=True)
+    kept = lax.all_to_all(kept, near, 0, 0, tiled=True)
     kept = lax.all_to_all(spread(kept, lax.axis_size(ring)), ring, 0, 0, tiled=True)
-    kept = jnp.sum(kept.reshape((lax.axis_size("z"), -1) + kept.shape[1:]).astype(F32), axis=0)
+    kept = jnp.sum(kept.reshape((-1, lax.axis_size("z_lo")) + kept.shape[1:]).astype(F32), axis=0)
     operands = (index, table, momentum, value_weight)
-    before = update(inner_rate / islands, core, kept, *operands)
-    return update(inner_rate / islands, 1 - core, swap(kept), *operands, before)
+    first = update_first(inner_rate / islands, core, kept, *operands)
+    return update_second(inner_rate / islands, 1 - core, swap(kept), *operands, *first)
 
 
 def solution(mesh):
-    fine = Mesh(mesh.devices.reshape(-1, 2, 2, 4, 2), ("z", "y_hi", "core", "x", "y_lo"))
-    island, tensor = ("z", "y_hi", "core"), ("x", "y_lo")
+    island, tensor = ("z_hi", "z_lo", "y_hi", "core"), ("x", "y_lo")
+    fine = Mesh(mesh.devices.reshape(-1, 2, 2, 2, 4, 2), island + tensor)
     in_specs = (
         P(island, tensor, None),
         P(island, None, tensor),

time: 65.7 us -> 62.5 us (0.951)
  blocking collectives: 45.1 us -> 42.5 us
    all_to_all x1, blocking collectives: 20.3 us -> 18.8 us  [local(): lax.all_to_all(spread(kept, lax.axis_size(ring)), ring, 0, 0, tiled=True)]
    all_to_all x1, blocking collectives: 12.1 us -> 11 us  [local(): kept = lax.all_to_all(kept, near, 0, 0, tiled=True)]
where the time goes in v6:
time: 62.5 us; the launch traced here: 62.3 us
  blocking collectives  42.5 us (68%)
  Pallas kernels  9.66 us (15%)
  starting transfers between devices  8.13 us (13%)
  waiting for transfers between devices  1.17 us (2%)
  between operations  0.71 us (1%)
    all_to_all x1, blocking collectives, local(): lax.all_to_all(spread(kept, lax.axis_size(ring)), ring, 0, 0, tiled=True)  18.8 us
    all_to_all x1, blocking collectives, local(): packed = lax.all_to_all(packed, tensor, 0, 0, tiled=True)  12.7 us
    all_to_all x1, blocking collectives, local(): kept = lax.all_to_all(kept, near, 0, 0, tiled=True)  11 us
    ppermute x3, starting transfers between devices, swap(): return lax.ppermute(x, 'core', [(0, 1), (1, 0)])  8.13 us
    pallas_call x1, Pallas kernels, value_grads(): pl.pallas_call(grads_kernel, out_shape=jax.ShapeDtypeStruct((parts, part...  4.9 us
    pallas_call x1, Pallas kernels, update_second(): pl.pallas_call(functools.partial(update_second_kernel, scale), out_shape=...  2.09 us
    pallas_call x1, Pallas kernels, encode(): pl.pallas_call(encode_kernel, out_shape=(jax.ShapeDtypeStruct((2, heads,...  1.58 us
  transfers between devices with their start and end apart: 3, of which 1 were waited for; matrix products, arithmetic and copies ran while one was open for 0% of the time, Pallas kernels for 10%

profile of v6, /device:TPU:1, one launch (start us, length us, event | category | flops | bytes accessed | tf_op | source)
XLA Modules:
  0.0 62.3 jit_solution(2686311035383393478)
XLA Ops:
  0.6 3.3 %collective-permute-start.1 = (bf16[128,4096]{1,0:T(8,128)(2,1)}, bf16[128,4096]{1,0:T(8,128)(2,1)S(1)}, u32[]{:S(2)}, u32[]{:S(2)}) collective-permute-start(bf16[128,4096]{1,0:T(8,128)(2,1)} %bitcast.14), channel_id=1, source_target_pairs={{0,8},{8,0},{1,9},{9,1},{2,10},{10,2},{3,11},{11,3},{4,12},{12,4},... | collective-permute-start | bytes 3145736 | tf_op jit(solution)/shard_map/ppermute | solution.py:297
  4.0 0.0 copy-start.3
  4.0 0.0 copy-start.4
  4.0 4.9 %shard_map.104 = bf16[8,256,128]{2,1,0:T(8,128)(2,1)S(1)} custom-call(s32[1]{0:T(128)} %bitcast.core_ref.half_ref, s32[1,1024]{1,0:T(1,128)} %doc_hbm.1, bf16[1024,512]{1,0:T(8,128)(2,1)} %bitcast.18, bf16[1024,128]{1,0:T(8,128)(2,1)} %bitcast.20, bf16[1024,512]{1,0:T(8,128)(2,1)} %bitcast.19, s32[8,4096]{1,0:T(8,128)} %bitcast.11), custom_call_target="tpu_custom_call" | custom-call | tf_op jit(solution)/shard_map/pallas_call | solution.py:130
  8.9 12.7 %all_to_all.15.own_ref = bf16[8,256,128]{2,1,0:T(8,128)(2,1)S(1)} all-to-all(bf16[8,256,128]{2,1,0:T(8,128)(2,1)S(1)} %shard_map.104), channel_id=1, replica_groups=mesh['z_hi'=4,'z_lo'=2,'y_hi'=2,'core'=2,'x'=4,'y_lo'=2] {'x','y_lo'}, dimensions={0} | all-to-all | bytes 1048576 | tf_op jit(solution)/shard_map/all_to_all | solution.py:309
  21.6 0.0 copy-start
  21.6 0.0 copy-start.1
  21.6 0.0 copy-start.2
  21.6 1.2 %collective-permute-start = (bf16[8,128,128]{2,1,0:T(8,128)(2,1)S(1)}, bf16[8,128,128]{2,1,0:T(8,128)(2,1)S(1)}, u32[]{:S(2)}, u32[]{:S(2)}) collective-permute-start(bf16[8,128,128]{2,1,0:T(8,128)(2,1)S(1)} %slice.4), channel_id=1, source_target_pairs={{0,8},{8,0},{1,9},{9,1},{2,10},{10,2},{3,11},{11,3},{4,12},{12,4},... | collective-permute-start | bytes 786440 | tf_op jit(solution)/shard_map/ppermute | solution.py:297
  22.8 1.2 %collective-permute-done.other_ref = bf16[8,128,128]{2,1,0:T(8,128)(2,1)S(1)} collective-permute-done((bf16[8,128,128]{2,1,0:T(8,128)(2,1)S(1)}, bf16[8,128,128]{2,1,0:T(8,128)(2,1)S(1)}, u32[]{:S(2)}, u32[]{:S(2)}) %collective-permute-start) | collective-permute-done | bytes 262176 | tf_op jit(solution)/shard_map/ppermute | solution.py:297
  24.0 0.0 collective-permute-done.1.hid_other_ref
  24.0 0.0 copy-done.3
  24.0 0.0 copy-done.4
  24.0 1.6 %shard_map.105 = (bf16[2,8,16,512]{3,2,1,0:T(8,128)(2,1)S(1)}, bf16[256,128]{1,0:T(8,128)(2,1)S(1)}) custom-call(s32[1]{0:T(128)} %bitcast.core_ref.half_ref, bf16[8,256,128]{2,1,0:T(8,128)(2,1)S(1)} %all_to_all.15.own_ref, bf16[8,128,128]{2,1,0:T(8,128)(2,1)S(1)} %collective-permute-done.other_ref, bf16[128,4096]{1,0:T(8,128)(2,1)S(1)} %bitcast.15, ...), custom_call_target="tpu_custom_call" | custom-call | tf_op jit(solution)/shard_map/pallas_call | solution.py:193
  25.6 11.0 %all_to_all.16 = bf16[16,16,512]{2,1,0:T(8,128)(2,1)S(1)} all-to-all(bf16[16,16,512]{2,1,0:T(8,128)(2,1)S(1)} %bitcast.16), channel_id=1, replica_groups=mesh['z_hi'=4,'z_lo'=2,'y_hi'=2,'core'=2,'x'=4,'y_lo'=2] {'z_lo','x','y_..., dimensions={0} | all-to-all | bytes 524288 | tf_op jit(solution)/shard_map/all_to_all | solution.py:313
  36.6 18.8 %all_to_all.17 = bf16[16,16,512]{2,1,0:T(8,128)(2,1)S(1)} all-to-all(bf16[16,16,512]{2,1,0:T(8,128)(2,1)S(1)} %broadcast_in_dim.2), channel_id=1, replica_groups=mesh['z_hi'=4,'z_lo'=2,'y_hi'=2,'core'=2,'x'=4,'y_lo'=2] {'y_hi','z_hi',..., dimensions={0} | all-to-all | bytes 524288 | tf_op jit(solution)/shard_map/all_to_all | solution.py:314
  55.5 3.6 %collective-permute-start.2 = (f32[2,16,512]{2,1,0:T(8,128)S(1)}, f32[2,16,512]{2,1,0:T(8,128)S(1)}, u32[]{:S(2)}, u32[]{:S(2)}) collective-permute-start(f32[2,16,512]{2,1,0:T(8,128)S(1)} %convert_reduce_fusion.refs_0_), channel_id=1, source_target_pairs={{0,8},{8,0},{1,9},{9,1},{2,10},{10,2},{3,11},{11,3},{4,12},{12,4},... | collective-permute-start | bytes 196616 | tf_op jit(solution)/shard_map/ppermute | solution.py:297
  59.1 0.0 copy-done
  59.1 0.0 copy-done.1
  59.1 0.0 copy-done.2
  59.1 1.1 %shard_map.106 = (bf16[2048,128]{1,0:T(8,128)(2,1)S(1)}, f32[2048,128]{1,0:T(8,128)S(1)}) custom-call(s32[1]{0:T(128)} %bitcast.core_ref.half_ref, f32[2,16,512]{2,1,0:T(8,128)S(1)} %convert_reduce_fusion.refs_0_, s32[8,4096]{1,0:T(8,128)S(1)} %bitcast.12, bf16[256,128]{1,0:T(8,128)(2,1)S(1)} %get-tuple-element.7.refs_2_, f32[4096,128]{1,0:T(8,128)S(1)} %copy-done, ...), custom_call_target="tpu_custom_call" | custom-call | tf_op jit(solution)/shard_map/pallas_call | solution.py:268
  60.2 0.0 collective-permute-done.2.refs_0_
  60.2 2.1 %shard_map.107 = (bf16[4096,128]{1,0:T(8,128)(2,1)}, f32[4096,128]{1,0:T(8,128)}) custom-call(s32[1]{0:T(128)S(6)} %sub.3.half_ref, f32[2,16,512]{2,1,0:T(8,128)S(1)} %collective-permute-done.2.refs_0_, s32[8,4096]{1,0:T(8,128)S(1)} %bitcast.13, bf16[256,128]{1,0:T(8,128)(2,1)S(1)} %get-tuple-element.7.refs_2_, f32[4096,128]{1,0:T(8,128)S(1)} %copy-done, ...), custom_call_target="tpu_custom_call" | custom-call | tf_op jit(solution)/shard_map/pallas_call | solution.py:282
  (4 shorter events, 0.1 us)
Async XLA Ops:
  0.6 23.3 %collective-permute-start.1 = (bf16[128,4096]{1,0:T(8,128)(2,1)}, bf16[128,4096]{1,0:T(8,128)(2,1)S(1)}, u32[]{:S(2)}, u32[]{:S(2)}) collective-permute-start(bf16[128,4096]{1,0:T(8,128)(2,1)} %bitcast.14), channel_id=1, source_target_pairs={{0,8},{8,0},{1,9},{9,1},{2,10},{10,2},{3,11},{11,3},{4,12},{12,4},... | collective-permute-start | bytes 3145736 | tf_op jit(solution)/shard_map/ppermute | solution.py:297
  4.0 20.0 %copy-start.3 = (bf16[1,128,4096]{2,1,0:T(8,128)(2,1)S(1)}, bf16[1,128,4096]{2,1,0:T(8,128)(2,1)}, u32[]{:S(2)}) copy-start(bf16[1,128,4096]{2,1,0:T(8,128)(2,1)} %param.9) | copy-start | bytes 3145732
  4.0 20.0 %copy-start.4 = (bf16[256,128]{1,0:T(8,128)(2,1)S(1)}, bf16[256,128]{1,0:T(8,128)(2,1)}, u32[]{:S(2)}) copy-start(bf16[256,128]{1,0:T(8,128)(2,1)} %constant.12.clone.table_ref) | copy-start | bytes 196612
  21.6 37.5 %copy-start = (f32[4096,128]{1,0:T(8,128)S(1)}, f32[4096,128]{1,0:T(8,128)}, u32[]{:S(2)}) copy-start(f32[4096,128]{1,0:T(8,128)} %refs_3_.3) | copy-start | bytes 6291460
  21.6 37.5 %copy-start.1 = (bf16[4096,128]{1,0:T(8,128)(2,1)S(1)}, bf16[4096,128]{1,0:T(8,128)(2,1)}, u32[]{:S(2)}) copy-start(bf16[4096,128]{1,0:T(8,128)(2,1)} %refs_4_.3) | copy-start | bytes 3145732
  21.6 37.5 %copy-start.2 = (s32[4096,1,8]{0,2,1:T(8,128)S(1)}, s32[4096,1,8]{0,2,1:T(8,128)}, u32[]{:S(2)}) copy-start(s32[4096,1,8]{0,2,1:T(8,128)} %param.16) | copy-start | bytes 393220
  21.6 2.4 %collective-permute-start = (bf16[8,128,128]{2,1,0:T(8,128)(2,1)S(1)}, bf16[8,128,128]{2,1,0:T(8,128)(2,1)S(1)}, u32[]{:S(2)}, u32[]{:S(2)}) collective-permute-start(bf16[8,128,128]{2,1,0:T(8,128)(2,1)S(1)} %slice.4), channel_id=1, source_target_pairs={{0,8},{8,0},{1,9},{9,1},{2,10},{10,2},{3,11},{11,3},{4,12},{12,4},... | collective-permute-start | bytes 786440 | tf_op jit(solution)/shard_map/ppermute | solution.py:297
  55.5 4.7 %collective-permute-start.2 = (f32[2,16,512]{2,1,0:T(8,128)S(1)}, f32[2,16,512]{2,1,0:T(8,128)S(1)}, u32[]{:S(2)}, u32[]{:S(2)}) collective-permute-start(f32[2,16,512]{2,1,0:T(8,128)S(1)} %convert_reduce_fusion.refs_0_), channel_id=1, source_target_pairs={{0,8},{8,0},{1,9},{9,1},{2,10},{10,2},{3,11},{11,3},{4,12},{12,4},... | collective-permute-start | bytes 196616 | tf_op jit(solution)/shard_map/ppermute | solution.py:297

commit v7 on v6

--- a/solution.py
+++ b/solution.py
@@ -185,7 +185,7 @@
                     piece = coeffs[v * 8 : v * 8 + 8, side * 128 : side * 128 + 128]
                     found = jnp.where(block == v, jnp.take_along_axis(piece, within, axis=0), found)
                 kept.append(found)
-            kept_ref[quarter, h, :, c * 128 : (c + 1) * 128] = jnp.concatenate(kept, axis=0).astype(BF16)
+            kept_ref[h, quarter, :, c * 128 : (c + 1) * 128] = jnp.concatenate(kept, axis=0).astype(BF16)
 
 
 def encode(core, own, other, hid_own, hid_other, table):
@@ -193,7 +193,7 @@
     return pl.pallas_call(
         encode_kernel,
         out_shape=(
-            jax.ShapeDtypeStruct((2, heads, 2 * KEEP, hid_own.shape[1] // 8), BF16),
+            jax.ShapeDtypeStruct((heads, 2, 2 * KEEP, hid_own.shape[1] // 8), BF16),
             jax.ShapeDtypeStruct(table.shape, BF16),
         ),
         in_specs=[SMEM] + [VMEM] * 5,
@@ -298,7 +298,7 @@
 
 
 def local(hidden_rows, queries, key_states, out_grads, doc_ids, value_weight, momentum, keep_index):
-    tensor, near, ring = ("x", "y_lo"), ("z_lo", "x", "y_lo"), ("y_hi", "z_hi", "z_lo")
+    tensor, near, ring = ("x", "y_lo"), ("x", "y_lo", "z_lo"), ("y_hi", "z_hi", "z_lo")
     islands = lax.axis_size(ring) * 2
     core = lax.axis_index("core").astype(jnp.int32).reshape(1)
     hid_own = hidden_rows[0]

time: 62.5 us -> 61.9 us (level)
  no operation moved by 1% of the time
where the time goes in v7:
time: 61.9 us; the launch traced here: 61.8 us
  blocking collectives  41.9 us (68%)
  Pallas kernels  9.67 us (16%)
  starting transfers between devices  8.16 us (13%)
  waiting for transfers between devices  1.17 us (2%)
  between operations  0.71 us (1%)
    all_to_all x1, blocking collectives, local(): lax.all_to_all(spread(kept, lax.axis_size(ring)), ring, 0, 0, tiled=True)  18.8 us
    all_to_all x1, blocking collectives, local(): packed = lax.all_to_all(packed, tensor, 0, 0, tiled=True)  12.7 us
    all_to_all x1, blocking collectives, local(): kept = lax.all_to_all(kept, near, 0, 0, tiled=True)  10.5 us
    ppermute x3, starting transfers between devices, swap(): return lax.ppermute(x, 'core', [(0, 1), (1, 0)])  8.16 us
    pallas_call x1, Pallas kernels, value_grads(): pl.pallas_call(grads_kernel, out_shape=jax.ShapeDtypeStruct((parts, part...  4.9 us
    pallas_call x1, Pallas kernels, update_second(): pl.pallas_call(functools.partial(update_second_kernel, scale), out_shape=...  2.09 us
    pallas_call x1, Pallas kernels, encode(): pl.pallas_call(encode_kernel, out_shape=(jax.ShapeDtypeStruct((heads, 2,...  1.58 us
  transfers between devices with their start and end apart: 3, of which 1 were waited for; matrix products, arithmetic and copies ran while one was open for 0% of the time, Pallas kernels for 10%

profile of v7, /device:TPU:1, one launch (start us, length us, event | category | flops | bytes accessed | tf_op | source)
XLA Modules:
  0.0 61.8 jit_solution(4844583683647573330)
XLA Ops:
  0.6 3.3 %collective-permute-start.1 = (bf16[128,4096]{1,0:T(8,128)(2,1)}, bf16[128,4096]{1,0:T(8,128)(2,1)S(1)}, u32[]{:S(2)}, u32[]{:S(2)}) collective-permute-start(bf16[128,4096]{1,0:T(8,128)(2,1)} %bitcast.14), channel_id=1, source_target_pairs={{0,8},{8,0},{1,9},{9,1},{2,10},{10,2},{3,11},{11,3},{4,12},{12,4},... | collective-permute-start | bytes 3145736 | tf_op jit(solution)/shard_map/ppermute | solution.py:297
  4.0 0.0 copy-start.3
  4.0 0.0 copy-start.4
  4.0 4.9 %shard_map.104 = bf16[8,256,128]{2,1,0:T(8,128)(2,1)S(1)} custom-call(s32[1]{0:T(128)} %bitcast.core_ref.half_ref, s32[1,1024]{1,0:T(1,128)} %doc_hbm.1, bf16[1024,512]{1,0:T(8,128)(2,1)} %bitcast.18, bf16[1024,128]{1,0:T(8,128)(2,1)} %bitcast.20, bf16[1024,512]{1,0:T(8,128)(2,1)} %bitcast.19, s32[8,4096]{1,0:T(8,128)} %bitcast.11), custom_call_target="tpu_custom_call" | custom-call | tf_op jit(solution)/shard_map/pallas_call | solution.py:130
  8.9 12.7 %all_to_all.15.own_ref = bf16[8,256,128]{2,1,0:T(8,128)(2,1)S(1)} all-to-all(bf16[8,256,128]{2,1,0:T(8,128)(2,1)S(1)} %shard_map.104), channel_id=1, replica_groups=mesh['z_hi'=4,'z_lo'=2,'y_hi'=2,'core'=2,'x'=4,'y_lo'=2] {'x','y_lo'}, dimensions={0} | all-to-all | bytes 1048576 | tf_op jit(solution)/shard_map/all_to_all | solution.py:309
  21.6 0.0 copy-start
  21.6 0.0 copy-start.1
  21.6 0.0 copy-start.2
  21.6 1.2 %collective-permute-start = (bf16[8,128,128]{2,1,0:T(8,128)(2,1)S(1)}, bf16[8,128,128]{2,1,0:T(8,128)(2,1)S(1)}, u32[]{:S(2)}, u32[]{:S(2)}) collective-permute-start(bf16[8,128,128]{2,1,0:T(8,128)(2,1)S(1)} %slice.4), channel_id=1, source_target_pairs={{0,8},{8,0},{1,9},{9,1},{2,10},{10,2},{3,11},{11,3},{4,12},{12,4},... | collective-permute-start | bytes 786440 | tf_op jit(solution)/shard_map/ppermute | solution.py:297
  22.8 1.2 %collective-permute-done.other_ref = bf16[8,128,128]{2,1,0:T(8,128)(2,1)S(1)} collective-permute-done((bf16[8,128,128]{2,1,0:T(8,128)(2,1)S(1)}, bf16[8,128,128]{2,1,0:T(8,128)(2,1)S(1)}, u32[]{:S(2)}, u32[]{:S(2)}) %collective-permute-start) | collective-permute-done | bytes 262176 | tf_op jit(solution)/shard_map/ppermute | solution.py:297
  24.0 0.0 collective-permute-done.1.hid_other_ref
  24.0 0.0 copy-done.3
  24.0 0.0 copy-done.4
  24.0 1.6 %shard_map.105 = (bf16[8,2,16,512]{3,2,1,0:T(8,128)(2,1)S(1)}, bf16[256,128]{1,0:T(8,128)(2,1)S(1)}) custom-call(s32[1]{0:T(128)} %bitcast.core_ref.half_ref, bf16[8,256,128]{2,1,0:T(8,128)(2,1)S(1)} %all_to_all.15.own_ref, bf16[8,128,128]{2,1,0:T(8,128)(2,1)S(1)} %collective-permute-done.other_ref, bf16[128,4096]{1,0:T(8,128)(2,1)S(1)} %bitcast.15, ...), custom_call_target="tpu_custom_call" | custom-call | tf_op jit(solution)/shard_map/pallas_call | solution.py:193
  25.6 10.5 %all_to_all.16 = bf16[16,16,512]{2,1,0:T(8,128)(2,1)S(1)} all-to-all(bf16[16,16,512]{2,1,0:T(8,128)(2,1)S(1)} %bitcast.16), channel_id=1, replica_groups=mesh['z_hi'=4,'z_lo'=2,'y_hi'=2,'core'=2,'x'=4,'y_lo'=2] {'x','y_lo','z_..., dimensions={0} | all-to-all | bytes 524288 | tf_op jit(solution)/shard_map/all_to_all | solution.py:313
  36.1 18.8 %all_to_all.17 = bf16[16,16,512]{2,1,0:T(8,128)(2,1)S(1)} all-to-all(bf16[16,16,512]{2,1,0:T(8,128)(2,1)S(1)} %broadcast_in_dim.2), channel_id=1, replica_groups=mesh['z_hi'=4,'z_lo'=2,'y_hi'=2,'core'=2,'x'=4,'y_lo'=2] {'y_hi','z_hi',..., dimensions={0} | all-to-all | bytes 524288 | tf_op jit(solution)/shard_map/all_to_all | solution.py:314
  54.9 3.6 %collective-permute-start.2 = (f32[2,16,512]{2,1,0:T(8,128)S(1)}, f32[2,16,512]{2,1,0:T(8,128)S(1)}, u32[]{:S(2)}, u32[]{:S(2)}) collective-permute-start(f32[2,16,512]{2,1,0:T(8,128)S(1)} %convert_reduce_fusion.refs_0_), channel_id=1, source_target_pairs={{0,8},{8,0},{1,9},{9,1},{2,10},{10,2},{3,11},{11,3},{4,12},{12,4},... | collective-permute-start | bytes 196616 | tf_op jit(solution)/shard_map/ppermute | solution.py:297
  58.5 0.0 copy-done
  58.5 0.0 copy-done.1
  58.5 0.0 copy-done.2
  58.5 1.1 %shard_map.106 = (bf16[2048,128]{1,0:T(8,128)(2,1)S(1)}, f32[2048,128]{1,0:T(8,128)S(1)}) custom-call(s32[1]{0:T(128)} %bitcast.core_ref.half_ref, f32[2,16,512]{2,1,0:T(8,128)S(1)} %convert_reduce_fusion.refs_0_, s32[8,4096]{1,0:T(8,128)S(1)} %bitcast.12, bf16[256,128]{1,0:T(8,128)(2,1)S(1)} %get-tuple-element.7.refs_2_, f32[4096,128]{1,0:T(8,128)S(1)} %copy-done, ...), custom_call_target="tpu_custom_call" | custom-call | tf_op jit(solution)/shard_map/pallas_call | solution.py:268
  59.6 0.0 collective-permute-done.2.refs_0_
  59.7 2.1 %shard_map.107 = (bf16[4096,128]{1,0:T(8,128)(2,1)}, f32[4096,128]{1,0:T(8,128)}) custom-call(s32[1]{0:T(128)S(6)} %sub.3.half_ref, f32[2,16,512]{2,1,0:T(8,128)S(1)} %collective-permute-done.2.refs_0_, s32[8,4096]{1,0:T(8,128)S(1)} %bitcast.13, bf16[256,128]{1,0:T(8,128)(2,1)S(1)} %get-tuple-element.7.refs_2_, f32[4096,128]{1,0:T(8,128)S(1)} %copy-done, ...), custom_call_target="tpu_custom_call" | custom-call | tf_op jit(solution)/shard_map/pallas_call | solution.py:282
  (4 shorter events, 0.1 us)
Async XLA Ops:
  0.6 23.3 %collective-permute-start.1 = (bf16[128,4096]{1,0:T(8,128)(2,1)}, bf16[128,4096]{1,0:T(8,128)(2,1)S(1)}, u32[]{:S(2)}, u32[]{:S(2)}) collective-permute-start(bf16[128,4096]{1,0:T(8,128)(2,1)} %bitcast.14), channel_id=1, source_target_pairs={{0,8},{8,0},{1,9},{9,1},{2,10},{10,2},{3,11},{11,3},{4,12},{12,4},... | collective-permute-start | bytes 3145736 | tf_op jit(solution)/shard_map/ppermute | solution.py:297
  4.0 20.0 %copy-start.3 = (bf16[1,128,4096]{2,1,0:T(8,128)(2,1)S(1)}, bf16[1,128,4096]{2,1,0:T(8,128)(2,1)}, u32[]{:S(2)}) copy-start(bf16[1,128,4096]{2,1,0:T(8,128)(2,1)} %param.9) | copy-start | bytes 3145732
  4.0 20.0 %copy-start.4 = (bf16[256,128]{1,0:T(8,128)(2,1)S(1)}, bf16[256,128]{1,0:T(8,128)(2,1)}, u32[]{:S(2)}) copy-start(bf16[256,128]{1,0:T(8,128)(2,1)} %constant.12.clone.table_ref) | copy-start | bytes 196612
  21.6 37.0 %copy-start = (f32[4096,128]{1,0:T(8,128)S(1)}, f32[4096,128]{1,0:T(8,128)}, u32[]{:S(2)}) copy-start(f32[4096,128]{1,0:T(8,128)} %refs_3_.3) | copy-start | bytes 6291460
  21.6 37.0 %copy-start.1 = (bf16[4096,128]{1,0:T(8,128)(2,1)S(1)}, bf16[4096,128]{1,0:T(8,128)(2,1)}, u32[]{:S(2)}) copy-start(bf16[4096,128]{1,0:T(8,128)(2,1)} %refs_4_.3) | copy-start | bytes 3145732
  21.6 37.0 %copy-start.2 = (s32[4096,1,8]{0,2,1:T(8,128)S(1)}, s32[4096,1,8]{0,2,1:T(8,128)}, u32[]{:S(2)}) copy-start(s32[4096,1,8]{0,2,1:T(8,128)} %param.16) | copy-start | bytes 393220
  21.6 2.4 %collective-permute-start = (bf16[8,128,128]{2,1,0:T(8,128)(2,1)S(1)}, bf16[8,128,128]{2,1,0:T(8,128)(2,1)S(1)}, u32[]{:S(2)}, u32[]{:S(2)}) collective-permute-start(bf16[8,128,128]{2,1,0:T(8,128)(2,1)S(1)} %slice.4), channel_id=1, source_target_pairs={{0,8},{8,0},{1,9},{9,1},{2,10},{10,2},{3,11},{11,3},{4,12},{12,4},... | collective-permute-start | bytes 786440 | tf_op jit(solution)/shard_map/ppermute | solution.py:297
  54.9 4.7 %collective-permute-start.2 = (f32[2,16,512]{2,1,0:T(8,128)S(1)}, f32[2,16,512]{2,1,0:T(8,128)S(1)}, u32[]{:S(2)}, u32[]{:S(2)}) collective-permute-start(f32[2,16,512]{2,1,0:T(8,128)S(1)} %convert_reduce_fusion.refs_0_), channel_id=1, source_target_pairs={{0,8},{8,0},{1,9},{9,1},{2,10},{10,2},{3,11},{11,3},{4,12},{12,4},... | collective-permute-start | bytes 196616 | tf_op jit(solution)/shard_map/ppermute | solution.py:297

commit v8 on v7

--- a/solution.py
+++ b/solution.py
@@ -72,20 +72,29 @@
     for ident in (1, 2, 3):
         before = jnp.sum((docs < ident).astype(jnp.int32), axis=1, keepdims=True)
         first = jnp.where(docs == ident, before, first)
-    copies[1].wait()
-    copies[2].wait()
+    blocks = []
+    place = 0
     for row in range(0, length, ROWS):
         low = max(0, row - SPAN)
         width = row + ROWS - low
         start = first[:, row : row + ROWS]
         key = lax.broadcasted_iota(jnp.int32, (width, ROWS), 0) + low
-        query = lax.broadcasted_iota(jnp.int32, (width, ROWS), 1) + row
-        allowed = (key >= start) & (key <= query)
-        cap_ref[:width] = jnp.where(allowed, jnp.finfo(F32).max, masked_score)
+        query = lax.broadcasted_iota(jnp.int32, (ROWS, ROWS), 1) + row
+        allowed = key >= start
+        corner = allowed[width - ROWS :] & (key[width - ROWS :] <= query)
+        top = jnp.finfo(F32).max
+        if width > ROWS:
+            cap_ref[place : place + width - ROWS] = jnp.where(allowed[: width - ROWS], top, masked_score)
+        cap_ref[place + width - ROWS : place + width] = jnp.where(corner, top, masked_score)
+        blocks.append((row, low, place, place + width))
+        place += width
+    copies[1].wait()
+    copies[2].wait()
+    for row, low, begin, end in blocks:
         for head in range(group):
             lanes = slice(head * HEAD_DIM, (head + 1) * HEAD_DIM)
             scores = dot(k_ref[low : row + ROWS], q_ref[row : row + ROWS, lanes], LAST)
-            scores = jnp.minimum(scores, cap_ref[:width])
+            scores = jnp.minimum(scores, cap_ref[begin:end])
             peak = jnp.max(scores, axis=0, keepdims=True)
             weights = jnp.exp2((scores - peak) * exp2_scale)
             inverse = 1.0 / jnp.sum(weights, axis=0, keepdims=True)
@@ -138,7 +147,7 @@
             pltpu.VMEM(key_states.shape, BF16),
             pltpu.VMEM(out_grads.shape, BF16),
             pltpu.VMEM((KEEP, half), jnp.int32),
-            pltpu.VMEM((SPAN + ROWS, ROWS), F32),
+            pltpu.VMEM((sum(min(row, SPAN) + ROWS for row in range(0, length, ROWS)), ROWS), F32),
             pltpu.VMEM((length, HEAD_DIM), F32),
             pltpu.SemaphoreType.DMA((5,)),
         ],

time: 61.9 us -> 61.8 us (level)
  transfers between devices with their start and end apart: 3 -> 3, of which waited for: 1 -> 1; matrix products, arithmetic and copies ran while one was open for 0% -> 0% of each run, Pallas kernels for 10% -> 9%
where the time goes in v8:
time: 61.8 us; the launch traced here: 61.6 us
  blocking collectives  41.9 us (68%)
  Pallas kernels  9.48 us (15%)
  starting transfers between devices  8.16 us (13%)
  waiting for transfers between devices  1.17 us (2%)
  between operations  0.71 us (1%)
    all_to_all x1, blocking collectives, local(): lax.all_to_all(spread(kept, lax.axis_size(ring)), ring, 0, 0, tiled=True)  18.8 us
    all_to_all x1, blocking collectives, local(): packed = lax.all_to_all(packed, tensor, 0, 0, tiled=True)  12.7 us
    all_to_all x1, blocking collectives, local(): kept = lax.all_to_all(kept, near, 0, 0, tiled=True)  10.5 us
    ppermute x3, starting transfers between devices, swap(): return lax.ppermute(x, 'core', [(0, 1), (1, 0)])  8.16 us
    pallas_call x1, Pallas kernels, value_grads(): pl.pallas_call(grads_kernel, out_shape=jax.ShapeDtypeStruct((parts, part...  4.72 us
    pallas_call x1, Pallas kernels, update_second(): pl.pallas_call(functools.partial(update_second_kernel, scale), out_shape=...  2.09 us
    pallas_call x1, Pallas kernels, encode(): pl.pallas_call(encode_kernel, out_shape=(jax.ShapeDtypeStruct((heads, 2,...  1.58 us
  transfers between devices with their start and end apart: 3, of which 1 were waited for; matrix products, arithmetic and copies ran while one was open for 0% of the time, Pallas kernels for 9%

profile of v8, /device:TPU:1, one launch (start us, length us, event | category | flops | bytes accessed | tf_op | source)
XLA Modules:
  0.0 61.6 jit_solution(5475912286026637027)
XLA Ops:
  0.6 3.3 %collective-permute-start.1 = (bf16[128,4096]{1,0:T(8,128)(2,1)}, bf16[128,4096]{1,0:T(8,128)(2,1)S(1)}, u32[]{:S(2)}, u32[]{:S(2)}) collective-permute-start(bf16[128,4096]{1,0:T(8,128)(2,1)} %bitcast.14), channel_id=1, source_target_pairs={{0,8},{8,0},{1,9},{9,1},{2,10},{10,2},{3,11},{11,3},{4,12},{12,4},... | collective-permute-start | bytes 3145736 | tf_op jit(solution)/shard_map/ppermute | solution.py:306
  4.0 0.0 copy-start.3
  4.0 0.0 copy-start.4
  4.0 4.7 %shard_map.104 = bf16[8,256,128]{2,1,0:T(8,128)(2,1)S(1)} custom-call(s32[1]{0:T(128)} %bitcast.core_ref.half_ref, s32[1,1024]{1,0:T(1,128)} %doc_hbm.1, bf16[1024,512]{1,0:T(8,128)(2,1)} %bitcast.18, bf16[1024,128]{1,0:T(8,128)(2,1)} %bitcast.20, bf16[1024,512]{1,0:T(8,128)(2,1)} %bitcast.19, s32[8,4096]{1,0:T(8,128)} %bitcast.11), custom_call_target="tpu_custom_call" | custom-call | tf_op jit(solution)/shard_map/pallas_call | solution.py:139
  8.7 12.7 %all_to_all.15.own_ref = bf16[8,256,128]{2,1,0:T(8,128)(2,1)S(1)} all-to-all(bf16[8,256,128]{2,1,0:T(8,128)(2,1)S(1)} %shard_map.104), channel_id=1, replica_groups=mesh['z_hi'=4,'z_lo'=2,'y_hi'=2,'core'=2,'x'=4,'y_lo'=2] {'x','y_lo'}, dimensions={0} | all-to-all | bytes 1048576 | tf_op jit(solution)/shard_map/all_to_all | solution.py:318
  21.4 0.0 copy-start
  21.4 0.0 copy-start.1
  21.4 0.0 copy-start.2
  21.4 1.2 %collective-permute-start = (bf16[8,128,128]{2,1,0:T(8,128)(2,1)S(1)}, bf16[8,128,128]{2,1,0:T(8,128)(2,1)S(1)}, u32[]{:S(2)}, u32[]{:S(2)}) collective-permute-start(bf16[8,128,128]{2,1,0:T(8,128)(2,1)S(1)} %slice.4), channel_id=1, source_target_pairs={{0,8},{8,0},{1,9},{9,1},{2,10},{10,2},{3,11},{11,3},{4,12},{12,4},... | collective-permute-start | bytes 786440 | tf_op jit(solution)/shard_map/ppermute | solution.py:306
  22.6 1.2 %collective-permute-done.other_ref = bf16[8,128,128]{2,1,0:T(8,128)(2,1)S(1)} collective-permute-done((bf16[8,128,128]{2,1,0:T(8,128)(2,1)S(1)}, bf16[8,128,128]{2,1,0:T(8,128)(2,1)S(1)}, u32[]{:S(2)}, u32[]{:S(2)}) %collective-permute-start) | collective-permute-done | bytes 262176 | tf_op jit(solution)/shard_map/ppermute | solution.py:306
  23.8 0.0 collective-permute-done.1.hid_other_ref
  23.8 0.0 copy-done.3
  23.8 0.0 copy-done.4
  23.8 1.6 %shard_map.105 = (bf16[8,2,16,512]{3,2,1,0:T(8,128)(2,1)S(1)}, bf16[256,128]{1,0:T(8,128)(2,1)S(1)}) custom-call(s32[1]{0:T(128)} %bitcast.core_ref.half_ref, bf16[8,256,128]{2,1,0:T(8,128)(2,1)S(1)} %all_to_all.15.own_ref, bf16[8,128,128]{2,1,0:T(8,128)(2,1)S(1)} %collective-permute-done.other_ref, bf16[128,4096]{1,0:T(8,128)(2,1)S(1)} %bitcast.15, ...), custom_call_target="tpu_custom_call" | custom-call | tf_op jit(solution)/shard_map/pallas_call | solution.py:202
  25.4 10.5 %all_to_all.16 = bf16[16,16,512]{2,1,0:T(8,128)(2,1)S(1)} all-to-all(bf16[16,16,512]{2,1,0:T(8,128)(2,1)S(1)} %bitcast.16), channel_id=1, replica_groups=mesh['z_hi'=4,'z_lo'=2,'y_hi'=2,'core'=2,'x'=4,'y_lo'=2] {'x','y_lo','z_..., dimensions={0} | all-to-all | bytes 524288 | tf_op jit(solution)/shard_map/all_to_all | solution.py:322
  35.9 18.8 %all_to_all.17 = bf16[16,16,512]{2,1,0:T(8,128)(2,1)S(1)} all-to-all(bf16[16,16,512]{2,1,0:T(8,128)(2,1)S(1)} %broadcast_in_dim.2), channel_id=1, replica_groups=mesh['z_hi'=4,'z_lo'=2,'y_hi'=2,'core'=2,'x'=4,'y_lo'=2] {'y_hi','z_hi',..., dimensions={0} | all-to-all | bytes 524288 | tf_op jit(solution)/shard_map/all_to_all | solution.py:323
  54.7 3.6 %collective-permute-start.2 = (f32[2,16,512]{2,1,0:T(8,128)S(1)}, f32[2,16,512]{2,1,0:T(8,128)S(1)}, u32[]{:S(2)}, u32[]{:S(2)}) collective-permute-start(f32[2,16,512]{2,1,0:T(8,128)S(1)} %convert_reduce_fusion.refs_0_), channel_id=1, source_target_pairs={{0,8},{8,0},{1,9},{9,1},{2,10},{10,2},{3,11},{11,3},{4,12},{12,4},... | collective-permute-start | bytes 196616 | tf_op jit(solution)/shard_map/ppermute | solution.py:306
  58.4 0.0 copy-done
  58.4 0.0 copy-done.1
  58.4 0.0 copy-done.2
  58.4 1.1 %shard_map.106 = (bf16[2048,128]{1,0:T(8,128)(2,1)S(1)}, f32[2048,128]{1,0:T(8,128)S(1)}) custom-call(s32[1]{0:T(128)} %bitcast.core_ref.half_ref, f32[2,16,512]{2,1,0:T(8,128)S(1)} %convert_reduce_fusion.refs_0_, s32[8,4096]{1,0:T(8,128)S(1)} %bitcast.12, bf16[256,128]{1,0:T(8,128)(2,1)S(1)} %get-tuple-element.7.refs_2_, f32[4096,128]{1,0:T(8,128)S(1)} %copy-done, ...), custom_call_target="tpu_custom_call" | custom-call | tf_op jit(solution)/shard_map/pallas_call | solution.py:277
  59.5 0.0 collective-permute-done.2.refs_0_
  59.5 2.1 %shard_map.107 = (bf16[4096,128]{1,0:T(8,128)(2,1)}, f32[4096,128]{1,0:T(8,128)}) custom-call(s32[1]{0:T(128)S(6)} %sub.3.half_ref, f32[2,16,512]{2,1,0:T(8,128)S(1)} %collective-permute-done.2.refs_0_, s32[8,4096]{1,0:T(8,128)S(1)} %bitcast.13, bf16[256,128]{1,0:T(8,128)(2,1)S(1)} %get-tuple-element.7.refs_2_, f32[4096,128]{1,0:T(8,128)S(1)} %copy-done, ...), custom_call_target="tpu_custom_call" | custom-call | tf_op jit(solution)/shard_map/pallas_call | solution.py:291
  (4 shorter events, 0.1 us)
Async XLA Ops:
  0.6 23.2 %collective-permute-start.1 = (bf16[128,4096]{1,0:T(8,128)(2,1)}, bf16[128,4096]{1,0:T(8,128)(2,1)S(1)}, u32[]{:S(2)}, u32[]{:S(2)}) collective-permute-start(bf16[128,4096]{1,0:T(8,128)(2,1)} %bitcast.14), channel_id=1, source_target_pairs={{0,8},{8,0},{1,9},{9,1},{2,10},{10,2},{3,11},{11,3},{4,12},{12,4},... | collective-permute-start | bytes 3145736 | tf_op jit(solution)/shard_map/ppermute | solution.py:306
  4.0 19.8 %copy-start.3 = (bf16[1,128,4096]{2,1,0:T(8,128)(2,1)S(1)}, bf16[1,128,4096]{2,1,0:T(8,128)(2,1)}, u32[]{:S(2)}) copy-start(bf16[1,128,4096]{2,1,0:T(8,128)(2,1)} %param.9) | copy-start | bytes 3145732
  4.0 19.8 %copy-start.4 = (bf16[256,128]{1,0:T(8,128)(2,1)S(1)}, bf16[256,128]{1,0:T(8,128)(2,1)}, u32[]{:S(2)}) copy-start(bf16[256,128]{1,0:T(8,128)(2,1)} %constant.12.clone.table_ref) | copy-start | bytes 196612
  21.4 37.0 %copy-start = (f32[4096,128]{1,0:T(8,128)S(1)}, f32[4096,128]{1,0:T(8,128)}, u32[]{:S(2)}) copy-start(f32[4096,128]{1,0:T(8,128)} %refs_3_.3) | copy-start | bytes 6291460
  21.4 37.0 %copy-start.1 = (bf16[4096,128]{1,0:T(8,128)(2,1)S(1)}, bf16[4096,128]{1,0:T(8,128)(2,1)}, u32[]{:S(2)}) copy-start(bf16[4096,128]{1,0:T(8,128)(2,1)} %refs_4_.3) | copy-start | bytes 3145732
  21.4 37.0 %copy-start.2 = (s32[4096,1,8]{0,2,1:T(8,128)S(1)}, s32[4096,1,8]{0,2,1:T(8,128)}, u32[]{:S(2)}) copy-start(s32[4096,1,8]{0,2,1:T(8,128)} %param.16) | copy-start | bytes 393220
  21.4 2.4 %collective-permute-start = (bf16[8,128,128]{2,1,0:T(8,128)(2,1)S(1)}, bf16[8,128,128]{2,1,0:T(8,128)(2,1)S(1)}, u32[]{:S(2)}, u32[]{:S(2)}) collective-permute-start(bf16[8,128,128]{2,1,0:T(8,128)(2,1)S(1)} %slice.4), channel_id=1, source_target_pairs={{0,8},{8,0},{1,9},{9,1},{2,10},{10,2},{3,11},{11,3},{4,12},{12,4},... | collective-permute-start | bytes 786440 | tf_op jit(solution)/shard_map/ppermute | solution.py:306
  54.7 4.7 %collective-permute-start.2 = (f32[2,16,512]{2,1,0:T(8,128)S(1)}, f32[2,16,512]{2,1,0:T(8,128)S(1)}, u32[]{:S(2)}, u32[]{:S(2)}) collective-permute-start(f32[2,16,512]{2,1,0:T(8,128)S(1)} %convert_reduce_fusion.refs_0_), channel_id=1, source_target_pairs={{0,8},{8,0},{1,9},{9,1},{2,10},{10,2},{3,11},{11,3},{4,12},{12,4},... | collective-permute-start | bytes 196616 | tf_op jit(solution)/shard_map/ppermute | solution.py:306

commit v9 on v8

--- a/solution.py
+++ b/solution.py
@@ -14,7 +14,7 @@
 KEEP = 8
 SPAN = 512
 ROWS = 128
-STORE = 512
+STORE = 256
 
 inner_rate = 0.01
 outer_rate = 0.7

time: 61.8 us -> 61.8 us (level)
  no operation moved by 1% of the time
where the time goes in v9:
time: 61.8 us; the launch traced here: 61.6 us
  blocking collectives  41.9 us (68%)
  Pallas kernels  9.53 us (15%)
  starting transfers between devices  8.16 us (13%)
  waiting for transfers between devices  1.17 us (2%)
  between operations  0.71 us (1%)
    all_to_all x1, blocking collectives, local(): lax.all_to_all(spread(kept, lax.axis_size(ring)), ring, 0, 0, tiled=True)  18.8 us
    all_to_all x1, blocking collectives, local(): packed = lax.all_to_all(packed, tensor, 0, 0, tiled=True)  12.7 us
    all_to_all x1, blocking collectives, local(): kept = lax.all_to_all(kept, near, 0, 0, tiled=True)  10.5 us
    ppermute x3, starting transfers between devices, swap(): return lax.ppermute(x, 'core', [(0, 1), (1, 0)])  8.16 us
    pallas_call x1, Pallas kernels, value_grads(): pl.pallas_call(grads_kernel, out_shape=jax.ShapeDtypeStruct((parts, part...  4.72 us
    pallas_call x1, Pallas kernels, update_second(): pl.pallas_call(functools.partial(update_second_kernel, scale), out_shape=...  2.14 us
    pallas_call x1, Pallas kernels, encode(): pl.pallas_call(encode_kernel, out_shape=(jax.ShapeDtypeStruct((heads, 2,...  1.58 us
  transfers between devices with their start and end apart: 3, of which 1 were waited for; matrix products, arithmetic and copies ran while one was open for 0% of the time, Pallas kernels for 9%

profile of v9, /device:TPU:1, one launch (start us, length us, event | category | flops | bytes accessed | tf_op | source)
XLA Modules:
  0.0 61.6 jit_solution(615809535493786513)
XLA Ops:
  0.6 3.3 %collective-permute-start.1 = (bf16[128,4096]{1,0:T(8,128)(2,1)}, bf16[128,4096]{1,0:T(8,128)(2,1)S(1)}, u32[]{:S(2)}, u32[]{:S(2)}) collective-permute-start(bf16[128,4096]{1,0:T(8,128)(2,1)} %bitcast.14), channel_id=1, source_target_pairs={{0,8},{8,0},{1,9},{9,1},{2,10},{10,2},{3,11},{11,3},{4,12},{12,4},... | collective-permute-start | bytes 3145736 | tf_op jit(solution)/shard_map/ppermute | solution.py:306
  4.0 0.0 copy-start.3
  4.0 0.0 copy-start.4
  4.0 4.7 %shard_map.104 = bf16[8,256,128]{2,1,0:T(8,128)(2,1)S(1)} custom-call(s32[1]{0:T(128)} %bitcast.core_ref.half_ref, s32[1,1024]{1,0:T(1,128)} %doc_hbm.1, bf16[1024,512]{1,0:T(8,128)(2,1)} %bitcast.18, bf16[1024,128]{1,0:T(8,128)(2,1)} %bitcast.20, bf16[1024,512]{1,0:T(8,128)(2,1)} %bitcast.19, s32[8,4096]{1,0:T(8,128)} %bitcast.11), custom_call_target="tpu_custom_call" | custom-call | tf_op jit(solution)/shard_map/pallas_call | solution.py:139
  8.7 12.7 %all_to_all.15.own_ref = bf16[8,256,128]{2,1,0:T(8,128)(2,1)S(1)} all-to-all(bf16[8,256,128]{2,1,0:T(8,128)(2,1)S(1)} %shard_map.104), channel_id=1, replica_groups=mesh['z_hi'=4,'z_lo'=2,'y_hi'=2,'core'=2,'x'=4,'y_lo'=2] {'x','y_lo'}, dimensions={0} | all-to-all | bytes 1048576 | tf_op jit(solution)/shard_map/all_to_all | solution.py:318
  21.4 0.0 copy-start
  21.4 0.0 copy-start.1
  21.4 0.0 copy-start.2
  21.4 1.2 %collective-permute-start = (bf16[8,128,128]{2,1,0:T(8,128)(2,1)S(1)}, bf16[8,128,128]{2,1,0:T(8,128)(2,1)S(1)}, u32[]{:S(2)}, u32[]{:S(2)}) collective-permute-start(bf16[8,128,128]{2,1,0:T(8,128)(2,1)S(1)} %slice.4), channel_id=1, source_target_pairs={{0,8},{8,0},{1,9},{9,1},{2,10},{10,2},{3,11},{11,3},{4,12},{12,4},... | collective-permute-start | bytes 786440 | tf_op jit(solution)/shard_map/ppermute | solution.py:306
  22.6 1.2 %collective-permute-done.other_ref = bf16[8,128,128]{2,1,0:T(8,128)(2,1)S(1)} collective-permute-done((bf16[8,128,128]{2,1,0:T(8,128)(2,1)S(1)}, bf16[8,128,128]{2,1,0:T(8,128)(2,1)S(1)}, u32[]{:S(2)}, u32[]{:S(2)}) %collective-permute-start) | collective-permute-done | bytes 262176 | tf_op jit(solution)/shard_map/ppermute | solution.py:306
  23.8 0.0 collective-permute-done.1.hid_other_ref
  23.8 0.0 copy-done.3
  23.8 0.0 copy-done.4
  23.8 1.6 %shard_map.105 = (bf16[8,2,16,512]{3,2,1,0:T(8,128)(2,1)S(1)}, bf16[256,128]{1,0:T(8,128)(2,1)S(1)}) custom-call(s32[1]{0:T(128)} %bitcast.core_ref.half_ref, bf16[8,256,128]{2,1,0:T(8,128)(2,1)S(1)} %all_to_all.15.own_ref, bf16[8,128,128]{2,1,0:T(8,128)(2,1)S(1)} %collective-permute-done.other_ref, bf16[128,4096]{1,0:T(8,128)(2,1)S(1)} %bitcast.15, ...), custom_call_target="tpu_custom_call" | custom-call | tf_op jit(solution)/shard_map/pallas_call | solution.py:202
  25.4 10.5 %all_to_all.16 = bf16[16,16,512]{2,1,0:T(8,128)(2,1)S(1)} all-to-all(bf16[16,16,512]{2,1,0:T(8,128)(2,1)S(1)} %bitcast.16), channel_id=1, replica_groups=mesh['z_hi'=4,'z_lo'=2,'y_hi'=2,'core'=2,'x'=4,'y_lo'=2] {'x','y_lo','z_..., dimensions={0} | all-to-all | bytes 524288 | tf_op jit(solution)/shard_map/all_to_all | solution.py:322
  35.9 18.8 %all_to_all.17 = bf16[16,16,512]{2,1,0:T(8,128)(2,1)S(1)} all-to-all(bf16[16,16,512]{2,1,0:T(8,128)(2,1)S(1)} %broadcast_in_dim.2), channel_id=1, replica_groups=mesh['z_hi'=4,'z_lo'=2,'y_hi'=2,'core'=2,'x'=4,'y_lo'=2] {'y_hi','z_hi',..., dimensions={0} | all-to-all | bytes 524288 | tf_op jit(solution)/shard_map/all_to_all | solution.py:323
  54.7 3.6 %collective-permute-start.2 = (f32[2,16,512]{2,1,0:T(8,128)S(1)}, f32[2,16,512]{2,1,0:T(8,128)S(1)}, u32[]{:S(2)}, u32[]{:S(2)}) collective-permute-start(f32[2,16,512]{2,1,0:T(8,128)S(1)} %convert_reduce_fusion.refs_0_), channel_id=1, source_target_pairs={{0,8},{8,0},{1,9},{9,1},{2,10},{10,2},{3,11},{11,3},{4,12},{12,4},... | collective-permute-start | bytes 196616 | tf_op jit(solution)/shard_map/ppermute | solution.py:306
  58.4 0.0 copy-done
  58.4 0.0 copy-done.1
  58.4 0.0 copy-done.2
  58.4 1.1 %shard_map.106 = (bf16[2048,128]{1,0:T(8,128)(2,1)S(1)}, f32[2048,128]{1,0:T(8,128)S(1)}) custom-call(s32[1]{0:T(128)} %bitcast.core_ref.half_ref, f32[2,16,512]{2,1,0:T(8,128)S(1)} %convert_reduce_fusion.refs_0_, s32[8,4096]{1,0:T(8,128)S(1)} %bitcast.12, bf16[256,128]{1,0:T(8,128)(2,1)S(1)} %get-tuple-element.7.refs_2_, f32[4096,128]{1,0:T(8,128)S(1)} %copy-done, ...), custom_call_target="tpu_custom_call" | custom-call | tf_op jit(solution)/shard_map/pallas_call | solution.py:277
  59.5 0.0 collective-permute-done.2.refs_0_
  59.5 2.1 %shard_map.107 = (bf16[4096,128]{1,0:T(8,128)(2,1)}, f32[4096,128]{1,0:T(8,128)}) custom-call(s32[1]{0:T(128)S(6)} %sub.3.half_ref, f32[2,16,512]{2,1,0:T(8,128)S(1)} %collective-permute-done.2.refs_0_, s32[8,4096]{1,0:T(8,128)S(1)} %bitcast.13, bf16[256,128]{1,0:T(8,128)(2,1)S(1)} %get-tuple-element.7.refs_2_, f32[4096,128]{1,0:T(8,128)S(1)} %copy-done, ...), custom_call_target="tpu_custom_call" | custom-call | tf_op jit(solution)/shard_map/pallas_call | solution.py:291
  (4 shorter events, 0.1 us)
Async XLA Ops:
  0.6 23.2 %collective-permute-start.1 = (bf16[128,4096]{1,0:T(8,128)(2,1)}, bf16[128,4096]{1,0:T(8,128)(2,1)S(1)}, u32[]{:S(2)}, u32[]{:S(2)}) collective-permute-start(bf16[128,4096]{1,0:T(8,128)(2,1)} %bitcast.14), channel_id=1, source_target_pairs={{0,8},{8,0},{1,9},{9,1},{2,10},{10,2},{3,11},{11,3},{4,12},{12,4},... | collective-permute-start | bytes 3145736 | tf_op jit(solution)/shard_map/ppermute | solution.py:306
  4.0 19.8 %copy-start.3 = (bf16[1,128,4096]{2,1,0:T(8,128)(2,1)S(1)}, bf16[1,128,4096]{2,1,0:T(8,128)(2,1)}, u32[]{:S(2)}) copy-start(bf16[1,128,4096]{2,1,0:T(8,128)(2,1)} %param.9) | copy-start | bytes 3145732
  4.0 19.8 %copy-start.4 = (bf16[256,128]{1,0:T(8,128)(2,1)S(1)}, bf16[256,128]{1,0:T(8,128)(2,1)}, u32[]{:S(2)}) copy-start(bf16[256,128]{1,0:T(8,128)(2,1)} %constant.12.clone.table_ref) | copy-start | bytes 196612
  21.4 37.0 %copy-start = (f32[4096,128]{1,0:T(8,128)S(1)}, f32[4096,128]{1,0:T(8,128)}, u32[]{:S(2)}) copy-start(f32[4096,128]{1,0:T(8,128)} %refs_3_.3) | copy-start | bytes 6291460
  21.4 37.0 %copy-start.1 = (bf16[4096,128]{1,0:T(8,128)(2,1)S(1)}, bf16[4096,128]{1,0:T(8,128)(2,1)}, u32[]{:S(2)}) copy-start(bf16[4096,128]{1,0:T(8,128)(2,1)} %refs_4_.3) | copy-start | bytes 3145732
  21.4 37.0 %copy-start.2 = (s32[4096,1,8]{0,2,1:T(8,128)S(1)}, s32[4096,1,8]{0,2,1:T(8,128)}, u32[]{:S(2)}) copy-start(s32[4096,1,8]{0,2,1:T(8,128)} %param.16) | copy-start | bytes 393220
  21.4 2.4 %collective-permute-start = (bf16[8,128,128]{2,1,0:T(8,128)(2,1)S(1)}, bf16[8,128,128]{2,1,0:T(8,128)(2,1)S(1)}, u32[]{:S(2)}, u32[]{:S(2)}) collective-permute-start(bf16[8,128,128]{2,1,0:T(8,128)(2,1)S(1)} %slice.4), channel_id=1, source_target_pairs={{0,8},{8,0},{1,9},{9,1},{2,10},{10,2},{3,11},{11,3},{4,12},{12,4},... | collective-permute-start | bytes 786440 | tf_op jit(solution)/shard_map/ppermute | solution.py:306
  54.7 4.7 %collective-permute-start.2 = (f32[2,16,512]{2,1,0:T(8,128)S(1)}, f32[2,16,512]{2,1,0:T(8,128)S(1)}, u32[]{:S(2)}, u32[]{:S(2)}) collective-permute-start(f32[2,16,512]{2,1,0:T(8,128)S(1)} %convert_reduce_fusion.refs_0_), channel_id=1, source_target_pairs={{0,8},{8,0},{1,9},{9,1},{2,10},{10,2},{3,11},{11,3},{4,12},{12,4},... | collective-permute-start | bytes 196616 | tf_op jit(solution)/shard_map/ppermute | solution.py:306
